TPU v7x, 32 devices: a whole 2x2x4 slice. The times are simulated.
32 devices in a mesh: pb: 8 (over z, core), pa: 4 (over y, x).
Axes of the slice: x: 2, y: 2, z: 4, core: 2. Of those that a mesh axis runs over, the one named last changes fastest.
Arguments:
- queries: float32 [4096, 1024], P(('pb', 'pa')), may hold values from -2 to 2
- passages: float32 [2048, 1024], P(('pa', 'pb')), may hold values from -2 to 2
- positive: int32 [4096], P('pb'), may hold values from 0 to 2047
Outputs:
- losses: float32 [4096], P('pb')
- query_grad: float32 [4096, 1024], P(('pb', 'pa'))
- passage_grad: float32 [2048, 1024], P(('pa', 'pb'))
All inputs are finite; a program needn't handle non-finite values.
Results may differ from a plain program's by a relative error of at most 0.0003.
Values sent between devices are 32-bit elements; how exact they have to be, the bound alone decides.
No kernel may reach another device: no remote copies, remote signals or barrier semaphores. Data moves between devices by JAX's collectives and lax.ppermute only.
A program may use at most 64 MiB of HBM per device.

v0:
```python
import jax
import jax.numpy as jnp
from jax import lax
from jax.sharding import PartitionSpec as P

inv_temp = 20.0


def normalize(rows):
    scale = lax.rsqrt(jnp.sum(rows * rows, axis=1, keepdims=True) + 1e-06)
    return (rows * scale, scale)


def body(queries, passages, positive):
    q_own_rows = queries.shape[0]
    p_own_rows = passages.shape[0]
    q_full = lax.all_gather(queries, "pa", axis=0, tiled=True)
    p_full = lax.all_gather(passages, "pb", axis=0, tiled=True)
    qn, rq = normalize(q_full)
    pn, rp = normalize(p_full)
    q_start = lax.axis_index("pa") * q_own_rows
    p_start = lax.axis_index("pb") * p_own_rows
    qn_own = lax.dynamic_slice_in_dim(qn, q_start, q_own_rows, 0)
    rq_own = lax.dynamic_slice_in_dim(rq, q_start, q_own_rows, 0)
    pn_own = lax.dynamic_slice_in_dim(pn, p_start, p_own_rows, 0)
    rp_own = lax.dynamic_slice_in_dim(rp, p_start, p_own_rows, 0)
    p_count = pn.shape[0]
    scores = inv_temp * lax.dot_general(
        qn,
        pn,
        (((1,), (1,)), ((), ())),
        precision=lax.Precision.HIGHEST,
        preferred_element_type=jnp.float32,
    )
    expo = jnp.exp(scores)
    first = lax.axis_index("pa") * p_count
    columns = first + jnp.arange(p_count, dtype=jnp.int32)
    onehot = (positive[:, None] == columns[None, :]).astype(jnp.float32)
    total, spos = lax.psum((jnp.sum(expo, axis=1), jnp.sum(onehot * scores, axis=1)), "pa")
    losses = jnp.log(total) - spos
    dscores = expo / total[:, None] - onehot
    gq = inv_temp * jnp.dot(
        dscores, pn, precision=lax.Precision.HIGHEST, preferred_element_type=jnp.float32
    )
    gp = inv_temp * lax.dot_general(
        dscores,
        qn,
        (((0,), (0,)), ((), ())),
        precision=lax.Precision.HIGHEST,
        preferred_element_type=jnp.float32,
    )
    q_part = lax.psum_scatter(gq, "pa", scatter_dimension=0, tiled=True)
    p_part = lax.psum_scatter(gp, "pb", scatter_dimension=0, tiled=True)
    query_grad = rq_own * (q_part - qn_own * jnp.sum(qn_own * q_part, axis=1, keepdims=True))
    passage_grad = rp_own * (p_part - pn_own * jnp.sum(pn_own * p_part, axis=1, keepdims=True))
    return (losses, query_grad, passage_grad)


def solution(mesh):
    placed = (P(("pb", "pa"), None), P(("pa", "pb"), None), P("pb"))
    return jax.shard_map(
        body,
        mesh=mesh,
        in_specs=placed,
        out_specs=(P("pb"), P(("pb", "pa"), None), P(("pa", "pb"), None)),
        check_vma=False,
    )
```

profile of v0, /device:TPU:0, one launch (start us, length us, event | category | flops | bytes accessed | tf_op | source)
XLA Modules:
  0.0 180.9 jit_solution(13853811334023382458)
XLA Ops:
  7.2 0.0 all-gather.3.cloned.1.call-start
  7.2 0.7 all-gather.3.cloned.1.call-update
  7.9 0.0 all-gather.5.cloned.1.call-start
  7.9 0.7 all-gather.5.cloned.1.call-update
  8.6 0.0 reduce-scatter.5.cloned.1.call-start
  8.7 39.2 %all-gather.3.cloned.1.call-done = f32[512,1024]{1,0:T(8,128)} async-done(((f32[128,1024]{1,0:T(8,128)}), f32[512,1024]{1,0:T(8,128)}) %all-gather.3.cloned.1.call-update) | async-done | bytes 2097168 | tf_op jit(solution)/shard_map/all_gather | solution.py:17
  47.9 2.0 %multiply_reduce_fusion.1 = f32[512]{0:T(512)S(1)} fusion(f32[512,1024]{1,0:T(8,128)} %all-gather.3.cloned.1.call-done), kind=kLoop, calls=%fused_computation.1 | loop fusion | flops 1048064 | bytes 2099200 | tf_op jit(solution)/shard_map/reduce_sum | solution.py:10
  49.9 0.3 copy-done.1
  50.1 0.2 broadcast_multiply_fusion.1
  50.3 28.3 %all-gather.5.cloned.1.call-done = f32[512,1024]{1,0:T(8,128)} async-done(((f32[64,1024]{1,0:T(8,128)}), f32[512,1024]{1,0:T(8,128)}) %all-gather.5.cloned.1.call-update) | async-done | bytes 2097168 | tf_op jit(solution)/shard_map/all_gather | solution.py:18
  78.6 2.0 %multiply_reduce_fusion = f32[512]{0:T(512)S(1)} fusion(f32[512,1024]{1,0:T(8,128)} %all-gather.5.cloned.1.call-done), kind=kLoop, calls=%fused_computation | loop fusion | flops 1048064 | bytes 2099200 | tf_op jit(solution)/shard_map/reduce_sum | solution.py:10
  80.6 0.3 copy-done.2
  80.8 0.2 broadcast_multiply_fusion
  81.1 0.5 copy-done.4
  81.5 3.7 %exponential_reduce_fusion = (f32[512]{0:T(512)S(1)}, f32[512]{0:T(512)S(1)}, f32[512,512]{0,1:T(8,128)S(1)}) fusion(s32[512]{0:T(512)S(1)} %iota_add_fusion, s32[512]{0:T(512)S(1)} %copy-done.4, f32[512,1024]{1,0:T(8,128)S(1)} %broadcast_multiply_fusion.1, f32[512,1024]{1,0:T(8,128)S(1)} %broadcast_multiply_fusion), kind=kOutput, calls=%fused_computation.11 | convolution fusion | flops 3222535168 | bytes 5251072 | tf_op jit(solution)/shard_map/dot_general | solution.py:28
  85.2 0.0 copy-done
  85.3 9.8 %all-reduce = (f32[512]{0:T(512)S(1)}, f32[512]{0:T(512)S(1)}) all-reduce(f32[512]{0:T(512)S(1)} %get-tuple-element.4, f32[512]{0:T(512)S(1)} %get-tuple-element.3), channel_id=1, replica_groups=mesh['pb'=8,'pa'=4] {'pa'}, use_global_device_ids=true, to_apply=%region_5.0 | all-reduce | flops 1024 | bytes 8192 | tf_op jit(solution)/shard_map/psum | solution.py:39
  95.1 5.0 %convolution_multiply_fusion = f32[512,1024]{1,0:T(8,128)} fusion(f32[512,1024]{1,0:T(8,128)S(1)} %broadcast_multiply_fusion.1, f32[512,512]{0,1:T(8,128)S(1)} %get-tuple-element.7, f32[512]{0:T(512)S(1)} %get-tuple-element.6, s32[512]{0:T(512)S(1)} %copy-done.4, s32[512]{0:T(512)S(1)} %iota_add_fusion), kind=kOutput, calls=%fused_computation.2 | convolution fusion | flops 3222798336 | bytes 5249024 | tf_op jit(solution)/shard_map/dot_general | solution.py:45
  100.1 0.0 reduce-scatter.5.cloned.1.call-update
  100.1 0.2 reduce-scatter.3.cloned.1.call-start
  100.3 6.5 %convolution_multiply_fusion.1 = f32[512,1024]{1,0:T(8,128)} fusion(f32[512,1024]{1,0:T(8,128)} %copy-done, f32[512,512]{0,1:T(8,128)S(1)} %get-tuple-element.7, f32[512]{0:T(512)S(1)} %get-tuple-element.6, s32[512]{0:T(512)S(1)} %copy-done.4, s32[512]{0:T(512)S(1)} %iota_add_fusion), kind=kOutput, calls=%fused_computation.3 | convolution fusion | flops 3222798336 | bytes 5249024 | tf_op jit(solution)/shard_map/dot_general | solution.py:42
  106.8 0.0 reduce-scatter.3.cloned.1.call-update
  106.9 0.1 dynamic-slice.6
  106.9 0.1 dynamic-slice.7
  107.0 0.6 log_subtract_fusion
  107.6 26.1 %reduce-scatter.5.cloned.1.call-done = f32[64,1024]{1,0:T(8,128)} async-done(((f32[512,1024]{1,0:T(8,128)}), f32[64,1024]{1,0:T(8,128)}) %reduce-scatter.5.cloned.1.call-update) | async-done | bytes 262160 | tf_op jit(solution)/shard_map/reduce_scatter | solution.py:53
  133.8 1.2 multiply_reduce_fusion.3
  134.9 35.4 %reduce-scatter.3.cloned.1.call-done = f32[128,1024]{1,0:T(8,128)} async-done(((f32[512,1024]{1,0:T(8,128)}), f32[128,1024]{1,0:T(8,128)}) %reduce-scatter.3.cloned.1.call-update) | async-done | bytes 524304 | tf_op jit(solution)/shard_map/reduce_scatter | solution.py:52
  170.3 1.2 multiply_reduce_fusion.2
  171.6 1.8 %subtract_multiply_fusion.1 = f32[64,1024]{1,0:T(8,128)} fusion(f32[64,1024]{1,0:T(8,128)} %reduce-scatter.5.cloned.1.call-done, f32[512,1024]{1,0:T(8,128)} %copy-done, s32[]{:T(128)S(6)} %select_n.9, f32[64]{0:T(128)S(1)} %multiply_reduce_fusion.3, f32[64]{0:T(128)S(1)} %dynamic-slice.7), kind=kLoop, calls=%fused_computation.14 | loop fusion | flops 196608 | bytes 786948 | tf_op jit(solution)/shard_map/mul | solution.py:55
  173.4 0.0 copy-done.3
  173.4 0.9 subtract_multiply_fusion
  (8 shorter events, 0.0 us)
Async XLA Ops:
  7.2 40.7 %all-gather.3.cloned.1.call-start = ((), (), s32[]{:S(2)}) async-start(), calls=%async_computation.2 | async-start | bytes 2621440 | tf_op jit(solution)/shard_map/all_gather | solution.py:17
  7.9 70.7 %all-gather.5.cloned.1.call-start = ((), (), s32[]{:S(2)}) async-start(), calls=%async_computation.3 | async-start | bytes 2359296 | tf_op jit(solution)/shard_map/all_gather | solution.py:18
  8.6 125.1 %reduce-scatter.5.cloned.1.call-start = ((), (), s32[]{:S(2)}) async-start(), calls=%async_computation.5 | async-start | bytes 2359296 | tf_op jit(solution)/shard_map/reduce_scatter | solution.py:53
  47.9 2.2 %copy-start.1 = (f32[512,1024]{1,0:T(8,128)S(1)}, f32[512,1024]{1,0:T(8,128)}, u32[]{:S(2)}) copy-start(f32[512,1024]{1,0:T(8,128)} %all-gather.3.cloned.1.call-done) | copy-start | bytes 6291460
  78.6 2.2 %copy-start.2 = (f32[512,1024]{1,0:T(8,128)S(1)}, f32[512,1024]{1,0:T(8,128)}, u32[]{:S(2)}) copy-start(f32[512,1024]{1,0:T(8,128)} %all-gather.5.cloned.1.call-done) | copy-start | bytes 6291460
  80.8 0.7 copy-start.4
  81.5 3.7 %copy-start = (f32[512,1024]{1,0:T(8,128)}, f32[512,1024]{1,0:T(8,128)S(1)}, u32[]{:S(2)}) copy-start(f32[512,1024]{1,0:T(8,128)S(1)} %broadcast_multiply_fusion) | copy-start | bytes 6291460
  100.1 70.2 %reduce-scatter.3.cloned.1.call-start = ((), (), s32[]{:S(2)}) async-start(), calls=%async_computation.4 | async-start | bytes 2621440 | tf_op jit(solution)/shard_map/reduce_scatter | solution.py:52
  170.3 3.1 %copy-start.3 = (f32[128,1024]{1,0:T(8,128)S(1)}, f32[128,1024]{1,0:T(8,128)}, u32[]{:S(2)}) copy-start(f32[128,1024]{1,0:T(8,128)} %reduce-scatter.3.cloned.1.call-done) | copy-start | bytes 1572868
Sparse Core Ops, SparseCore 0:
  9.8 38.0 all-gather.2
  49.5 29.0 all-gather.4
  100.2 33.4 reduce-scatter.4
  136.6 33.7 reduce-scatter.2
where the time goes:
time: 181 us
  waiting for transfers between devices  130 us (72%)
  matrix products  15.2 us (8%)
  between operations  13.8 us (8%)
  other arithmetic  10.1 us (6%)
  blocking collectives  9.85 us (5%)
    all_gather x1, waiting for transfers between devices, body(): q_full = lax.all_gather(queries, 'pa', axis=0, tiled=True)  39.2 us
    reduce_scatter x1, waiting for transfers between devices, body(): q_part = lax.psum_scatter(gq, 'pa', scatter_dimension=0, tiled=True)  35.4 us
    all_gather x1, waiting for transfers between devices, body(): p_full = lax.all_gather(passages, 'pb', axis=0, tiled=True)  28.3 us
    reduce_scatter x1, waiting for transfers between devices, body(): p_part = lax.psum_scatter(gp, 'pb', scatter_dimension=0, tiled=True)  26.1 us
    psum x1, blocking collectives, body(): lax.psum((jnp.sum(expo, axis=1), jnp.sum(onehot * scores, axis=1)), 'pa')  9.85 us
    dot_general x1, matrix products, body(): jnp.dot(dscores, pn, precision=lax.Precision.HIGHEST, preferred_element_t...  6.52 us
    dot_general x1, matrix products, body(): lax.dot_general(dscores, qn, (((0,), (0,)), ((), ())), precision=lax.Prec...  4.96 us
    reduce_sum x2, other arithmetic, normalize(): scale = lax.rsqrt(jnp.sum(rows * rows, axis=1, keepdims=True) + 1e-06)  3.9 us
  transfers between devices with their start and end apart: 4, of which 4 were waited for; matrix products, arithmetic and copies ran while one was open for 6% of the time, Pallas kernels for 0%

commit v1 on v0

v1 whole, which is shorter than its diff:
```python
import functools

import jax
import jax.numpy as jnp
from jax import lax
from jax.experimental import pallas as pl
from jax.experimental.pallas import tpu as pltpu
from jax.sharding import PartitionSpec as P

inv_temp = 20.0
f32 = jnp.float32
bf16 = jnp.bfloat16
AXES = ("pb", "pa")


def call(kernel, outs, flops, *args):
    return pl.pallas_call(
        kernel,
        out_shape=[jax.ShapeDtypeStruct(s, d) for s, d in outs],
        compiler_params=pltpu.CompilerParams(vmem_limit_bytes=40 * 1024 * 1024),
        cost_estimate=pl.CostEstimate(flops=flops, bytes_accessed=8 << 20, transcendentals=0),
    )(*args)


def split(x):
    hi = x.astype(bf16)
    return hi, (x - hi.astype(f32)).astype(bf16)


def mm(a, b, dims):
    return lax.dot_general(a, b, (dims, ((), ())), preferred_element_type=f32)


def mm3(a, b, dims):
    (ah, al), (bh, bl) = a, b
    return mm(al, bh, dims) + mm(ah, bl, dims) + mm(ah, bh, dims)


def normalize(rows):
    scale = lax.rsqrt(jnp.sum(rows * rows, axis=1, keepdims=True) + 1e-06)
    return rows * scale, scale


def onehot(pos_ref, shape):
    return lax.broadcasted_iota(jnp.int32, shape, 0) == pos_ref[...]


def combine(stats):
    n = stats[0].shape[1] // len(stats)
    blocks = [sum(r[:, (m ^ k) * n : (m ^ k) * n + n] for k, r in enumerate(stats)) for m in range(len(stats))]
    return jnp.concatenate(blocks, axis=1)


def scores_kernel(n_q, n_p, *refs):
    qs, ps = refs[:n_q], refs[n_q : n_q + n_p]
    pos, et, stats, qh, ql, ph, pl_ = refs[n_q + n_p :]
    for parts, hi, lo in ((qs, qh, ql), (ps, ph, pl_)):
        at = 0
        for r in parts:
            n = r.shape[0]
            hi[at : at + n], lo[at : at + n] = split(normalize(r[...])[0])
            at += n
    st = inv_temp * mm3((ph[...], pl_[...]), (qh[...], ql[...]), ((1,), (1,)))
    e = jnp.exp(st)
    et[...] = e
    stats[...] = jnp.zeros(stats.shape, f32)
    stats[0:1] = jnp.sum(e, axis=0, keepdims=True)
    stats[1:2] = jnp.sum(jnp.where(onehot(pos, st.shape), st, 0.0), axis=0, keepdims=True)


def unscaled_kernel(et, pos, ph, pl_, u, v):
    p = (ph[...], pl_[...])
    u[...] = mm3(split(et[...].T), p, ((1,), (0,)))
    o = onehot(pos, et.shape).astype(f32).T.astype(bf16)
    v[...] = mm(o, p[1], ((1,), (0,))) + mm(o, p[0], ((1,), (0,)))


def passage_kernel(n_stats, *refs):
    stats = refs[:n_stats]
    et, pos, qh, ql, gp = refs[n_stats:]
    total = combine(stats)[0:1]
    dt = et[...] * (1.0 / total) - onehot(pos, et.shape).astype(f32)
    gp[...] = mm3(split(dt), (qh[...], ql[...]), ((1,), (0,)))


def query_kernel(n_stats, cuts, *refs):
    stats = refs[:n_stats]
    u, v, losses = refs[n_stats : n_stats + 3]
    outs = refs[n_stats + 3 :]
    both = combine(stats)
    losses[...] = jnp.log(both[0:1]) - both[1:2]
    inv = (1.0 / both).T[:, 0:1]
    at = 0
    for out, n in zip(outs, cuts):
        out[...] = u[at : at + n] * inv[at : at + n] - v[at : at + n]
        at += n


def final_kernel(*refs):
    rows, parts, out = refs[0], refs[1:-1], refs[-1]
    xn, scale = normalize(rows[...])
    g = None
    for group in parts:
        g = group[...] if g is None else g + group[...]
    g = inv_temp * g
    out[...] = scale * (g - xn * jnp.sum(xn * g, axis=1, keepdims=True))


def flip(x, mask, only=None):
    n = lax.axis_size("pb") * lax.axis_size("pa")
    pairs = [(i, i ^ mask) for i in range(n) if only is None or only(i)]
    return lax.ppermute(x, AXES, pairs)


X, Y, C, Z1, Z2, Z3 = 1, 2, 4, 8, 16, 24


def middle(i):
    return (i // 8) in (1, 2)


def ends(i):
    return not middle(i)


def rows_of(x, *cuts):
    at, out = 0, []
    for n in cuts:
        out.append(lax.slice_in_dim(x, at, at + n, axis=0))
        at += n
    return out


def small_body(queries, passages, positive):
    qr, pr = queries.shape[0], passages.shape[0]
    h = qr // 2
    q_rows, p_rows = 4 * qr, 8 * pr
    pa, pb = lax.axis_index("pa"), lax.axis_index("pb")

    qa, qb = rows_of(queries, h, h)
    xa, yb = flip(qa, X), flip(qb, Y)
    xb, ya = flip(qb, X), flip(qa, Y)
    da, db = flip(xa, Y), flip(yb, X)
    z2 = flip(passages, Z2)
    z1 = flip(passages, Z1)
    pc = flip(passages, C)
    mid = flip(passages, Z3, middle)
    far = flip(z2, Z1, middle)
    z3 = mid + far
    z1c, z2c, z3c = flip(z1, C), flip(z2, C), flip(z3, C)
    q_parts = [qa, qb, xa, xb, ya, yb, da, db]
    p_parts = [passages, pc, z1, z1c, z2, z2c, z3, z3c]

    order = jnp.arange(4, dtype=jnp.int32) ^ pa
    pos = positive.reshape(4, qr)[order].reshape(1, q_rows)
    pos = jnp.where(pos // p_rows == pa, (pos % p_rows) ^ (pb * pr), -1)

    et, stats, qh, ql, ph, pl_ = scores(q_parts, p_parts, pos)
    both = [stats, flip(stats, X), flip(stats, Y), flip(stats, X + Y)]
    u, v = unscaled(et, pos, ph, pl_)
    gp = passage_grads(both, et, pos, qh, ql)
    losses, own, gxa, gxb, gya, gyb, gda, gdb = query_grads(both, u, v, (qr,) + (h,) * 6)

    fa, fb = flip(gda, X), flip(gdb, Y)
    rxa, ryb = flip(gxa, X), flip(gyb, Y)
    rxb, rya = flip(gxb + fb, X), flip(gya + fa, Y)

    g0, c0, g1, c1, g2, c2, g3, c3 = rows_of(gp, *([pr] * 8))
    g3 = g3 + flip(c3, C)
    ff = flip(g3, Z1, ends)
    g1 = g1 + flip(c1, C)
    g2 = g2 + flip(c2, C)
    rmid = flip(g3, Z3, middle)
    r1 = flip(g1, Z1)
    r2 = flip(g2 + ff, Z2)
    r0 = flip(c0, C)

    losses = losses.reshape(4, qr)[order].reshape(q_rows)
    query_grad = finish(queries, own, jnp.concatenate([rxa, rxb]), jnp.concatenate([rya, ryb]))
    passage_grad = finish(passages, g0, r0, r1, rmid, r2)
    return losses, query_grad, passage_grad


def scores(q_parts, p_parts, pos):
    q_rows, p_rows = sum(x.shape[0] for x in q_parts), sum(x.shape[0] for x in p_parts)
    d = q_parts[0].shape[1]
    return call(
        functools.partial(scores_kernel, len(q_parts), len(p_parts)),
        [((p_rows, q_rows), f32), ((8, q_rows), f32), ((q_rows, d), bf16), ((q_rows, d), bf16), ((p_rows, d), bf16), ((p_rows, d), bf16)],
        6 * q_rows * p_rows * d,
        *q_parts,
        *p_parts,
        pos,
    )


def unscaled(et, pos, ph, pl_):
    p_rows, q_rows = et.shape
    d = ph.shape[1]
    return call(unscaled_kernel, [((q_rows, d), f32)] * 2, 10 * q_rows * p_rows * d, et, pos, ph, pl_)


def passage_grads(both, et, pos, qh, ql):
    p_rows, q_rows = et.shape
    d = qh.shape[1]
    return call(functools.partial(passage_kernel, len(both)), [((p_rows, d), f32)], 6 * q_rows * p_rows * d, *both, et, pos, qh, ql)[0]


def query_grads(both, u, v, cuts):
    q_rows, d = u.shape
    return call(
        functools.partial(query_kernel, len(both), cuts),
        [((1, q_rows), f32)] + [((n, d), f32) for n in cuts],
        3 * q_rows * d,
        *both,
        u,
        v,
    )


def finish(rows, *parts):
    return call(final_kernel, [(rows.shape, f32)], 12 * rows.size, rows, *parts)[0]


def body(queries, passages, positive):
    qr, pr = queries.shape[0], passages.shape[0]
    pa = lax.axis_index("pa")
    q_full = lax.all_gather(queries, "pa", axis=0, tiled=True)
    p_full = lax.all_gather(passages, "pb", axis=0, tiled=True)
    p_rows = p_full.shape[0]
    pos = positive - pa * p_rows
    pos = jnp.where((pos >= 0) & (pos < p_rows), pos, -1).reshape(1, -1)
    et, stats, qh, ql, ph, pl_ = scores([q_full], [p_full], pos)
    both = [lax.psum(stats, "pa")]
    u, v = unscaled(et, pos, ph, pl_)
    gp = passage_grads(both, et, pos, qh, ql)
    losses, gq = query_grads(both, u, v, (q_full.shape[0],))
    q_part = lax.psum_scatter(gq, "pa", scatter_dimension=0, tiled=True)
    p_part = lax.psum_scatter(gp, "pb", scatter_dimension=0, tiled=True)
    return losses.reshape(-1), finish(queries, q_part), finish(passages, p_part)


def solution(mesh):
    placed = (P(("pb", "pa"), None), P(("pa", "pb"), None), P("pb"))
    small = mesh.shape["pa"] == 4 and mesh.shape["pb"] == 8
    return jax.shard_map(
        small_body if small else body,
        mesh=mesh,
        in_specs=placed,
        out_specs=(P("pb"), P(("pb", "pa"), None), P(("pa", "pb"), None)),
        check_vma=False,
    )
```

time: 181 us -> 99.8 us (0.55)
  waiting for transfers between devices: 130 us -> 49.6 us
  starting transfers between devices: 0.34 us -> 30.7 us
  matrix products: 15.2 us -> 0 us
  between operations: 13.8 us -> 0.9 us
  Pallas kernels: 0 us -> 10.7 us
  blocking collectives: 9.85 us -> 0 us
  other arithmetic: 10.1 us -> 3.18 us
  local copies, waits for them, and re-layouts: 1.15 us -> 4.46 us
    all_gather x2 -> x0, waiting for transfers between devices: 67.5 us -> none  [the longest x1 39.2 us: body(): q_full = lax.all_gather(queries, 'pa', axis=0, tiled=True)]
    reduce_scatter x2 -> x0, waiting for transfers between devices: 61.6 us -> none  [the longest x1 35.4 us: body(): q_part = lax.psum_scatter(gq, 'pa', scatter_dimension=0, tiled=True)]
    ppermute x0 -> x31, waiting for transfers between devices: none -> 49.6 us  [flip(): return lax.ppermute(x, AXES, pairs)]
    ppermute x0 -> x31, starting transfers between devices: none -> 30.7 us  [flip(): return lax.ppermute(x, AXES, pairs)]
    dot_general x3 -> x0, matrix products: 15.2 us -> none  [the longest x1 6.52 us: body(): jnp.dot(dscores, pn, precision=lax.Precision.HIGHEST, preferred_element_t...]
    pallas_call x0 -> x6, Pallas kernels: none -> 10.7 us  [call(): pl.pallas_call(kernel, out_shape=[jax.ShapeDtypeStruct(s, d) for s, d in...]
    psum x1 -> x0, blocking collectives: 9.85 us -> none  [body(): lax.psum((jnp.sum(expo, axis=1), jnp.sum(onehot * scores, axis=1)), 'pa')]
    reduce_sum x4 -> x0, other arithmetic: 6.3 us -> none  [the longest x2 3.9 us: normalize(): scale = lax.rsqrt(jnp.sum(rows * rows, axis=1, keepdims=True) + 1e-06)]
  transfers between devices with their start and end apart: 4 -> 31, of which waited for: 4 -> 17; matrix products, arithmetic and copies ran while one was open for 6% -> 6% of each run, Pallas kernels for 0% -> 4%
where the time goes in v1:
time: 99.8 us; the launch traced here: 99.5 us
  waiting for transfers between devices  49.6 us (50%)
  starting transfers between devices  30.7 us (31%)
  Pallas kernels  10.7 us (11%)
  local copies, waits for them, and re-layouts  4.46 us (4%)
  other arithmetic  3.18 us (3%)
    ppermute x31, waiting for transfers between devices, flip(): return lax.ppermute(x, AXES, pairs)  49.6 us
    ppermute x31, starting transfers between devices, flip(): return lax.ppermute(x, AXES, pairs)  30.7 us
    pallas_call x6, Pallas kernels, call(): pl.pallas_call(kernel, out_shape=[jax.ShapeDtypeStruct(s, d) for s, d in...  10.7 us
  transfers between devices with their start and end apart: 31, of which 17 were waited for; matrix products, arithmetic and copies ran while one was open for 6% of the time, Pallas kernels for 4%

profile of v1, /device:TPU:0, one launch (start us, length us, event | category | flops | bytes accessed | tf_op | source)
XLA Modules:
  0.0 99.5 jit_solution(16381320876903597687)
XLA Ops:
  0.6 4.1 %collective-permute-start.9 = (f32[64,1024]{1,0:T(8,128)}, f32[64,1024]{1,0:T(8,128)S(1)}, u32[]{:S(2)}, u32[]{:S(2)}) collective-permute-start(f32[64,1024]{1,0:T(8,128)} %refs_0_.3), channel_id=1, source_target_pairs={{0,16},{1,17},{2,18},{3,19},{4,20},{5,21},{6,22},{7,23},{8,24},{9,... | collective-permute-start | bytes 786440 | tf_op jit(solution)/shard_map/ppermute | solution.py:112
  5.4 2.9 %collective-permute-start.7 = (f32[64,1024]{1,0:T(8,128)}, f32[64,1024]{1,0:T(8,128)S(1)}, u32[]{:S(2)}, u32[]{:S(2)}) collective-permute-start(f32[64,1024]{1,0:T(8,128)} %refs_0_.3), channel_id=1, source_target_pairs={{0,8},{1,9},{2,10},{3,11},{4,12},{5,13},{6,14},{7,15},{8,0},{9,1},... | collective-permute-start | bytes 786440 | tf_op jit(solution)/shard_map/ppermute | solution.py:112
  8.3 9.5 %collective-permute-done.9.refs_12_ = f32[64,1024]{1,0:T(8,128)S(1)} collective-permute-done((f32[64,1024]{1,0:T(8,128)}, f32[64,1024]{1,0:T(8,128)S(1)}, u32[]{:S(2)}, u32[]{:S(2)}) %collective-permute-start.9) | collective-permute-done | bytes 262176 | tf_op jit(solution)/shard_map/ppermute | solution.py:112
  17.8 1.3 %collective-permute-start.12 = (f32[64,1024]{1,0:T(8,128)S(1)}, f32[64,1024]{1,0:T(8,128)S(1)}, u32[]{:S(2)}, u32[]{:S(2)}) collective-permute-start(f32[64,1024]{1,0:T(8,128)S(1)} %collective-permute-done.9.refs_12_), channel_id=1, source_target_pairs={{8,0},{9,1},{10,2},{11,3},{12,4},{13,5},{14,6},{15,7},{16,24},{17,... | collective-permute-start | bytes 786440 | tf_op jit(solution)/shard_map/ppermute | solution.py:112
  20.2 1.9 %collective-permute-start.3 = (f32[64,1024]{1,0:T(8,128)S(1)}, f32[64,1024]{1,0:T(8,128)S(1)}, u32[]{:S(2)}, u32[]{:S(2)}) collective-permute-start(f32[64,1024]{1,0:T(8,128)S(1)} %get-tuple-element.41.refs_1_), channel_id=1, source_target_pairs={{0,2},{1,3},{2,0},{3,1},{4,6},{5,7},{6,4},{7,5},{8,10},{9,11},{10,... | collective-permute-start | bytes 786440 | tf_op jit(solution)/shard_map/ppermute | solution.py:112
  22.1 1.5 %collective-permute-start.1 = (f32[64,1024]{1,0:T(8,128)S(1)}, f32[64,1024]{1,0:T(8,128)S(1)}, u32[]{:S(2)}, u32[]{:S(2)}) collective-permute-start(f32[64,1024]{1,0:T(8,128)S(1)} %get-tuple-element.41.refs_1_), channel_id=1, source_target_pairs={{0,1},{1,0},{2,3},{3,2},{4,5},{5,4},{6,7},{7,6},{8,9},{9,8},{10,11... | collective-permute-start | bytes 786440 | tf_op jit(solution)/shard_map/ppermute | solution.py:112
  24.2 2.1 %collective-permute-done.12 = f32[64,1024]{1,0:T(8,128)S(1)} collective-permute-done((f32[64,1024]{1,0:T(8,128)S(1)}, f32[64,1024]{1,0:T(8,128)S(1)}, u32[]{:S(2)}, u32[]{:S(2)}) %collective-permute-start.12) | collective-permute-done | bytes 262176 | tf_op jit(solution)/shard_map/ppermute | solution.py:112
  26.3 1.6 %collective-permute-start.2 = (f32[64,1024]{1,0:T(8,128)S(1)}, f32[64,1024]{1,0:T(8,128)S(1)}, u32[]{:S(2)}, u32[]{:S(2)}) collective-permute-start(f32[64,1024]{1,0:T(8,128)S(1)} %get-tuple-element.42.refs_0_), channel_id=1, source_target_pairs={{0,2},{1,3},{2,0},{3,1},{4,6},{5,7},{6,4},{7,5},{8,10},{9,11},{10,... | collective-permute-start | bytes 786440 | tf_op jit(solution)/shard_map/ppermute | solution.py:112
  28.0 1.3 %collective-permute-done.3.refs_5_ = f32[64,1024]{1,0:T(8,128)S(1)} collective-permute-done((f32[64,1024]{1,0:T(8,128)S(1)}, f32[64,1024]{1,0:T(8,128)S(1)}, u32[]{:S(2)}, u32[]{:S(2)}) %collective-permute-start.3) | collective-permute-done | bytes 262176 | tf_op jit(solution)/shard_map/ppermute | solution.py:112
  29.4 1.9 %collective-permute-done.1.refs_3_ = f32[64,1024]{1,0:T(8,128)S(1)} collective-permute-done((f32[64,1024]{1,0:T(8,128)S(1)}, f32[64,1024]{1,0:T(8,128)S(1)}, u32[]{:S(2)}, u32[]{:S(2)}) %collective-permute-start.1) | collective-permute-done | bytes 262176 | tf_op jit(solution)/shard_map/ppermute | solution.py:112
  31.3 1.5 %collective-permute-start.5 = (f32[64,1024]{1,0:T(8,128)S(1)}, f32[64,1024]{1,0:T(8,128)S(1)}, u32[]{:S(2)}, u32[]{:S(2)}) collective-permute-start(f32[64,1024]{1,0:T(8,128)S(1)} %collective-permute-done.3.refs_5_), channel_id=1, source_target_pairs={{0,1},{1,0},{2,3},{3,2},{4,5},{5,4},{6,7},{7,6},{8,9},{9,8},{10,11... | collective-permute-start | bytes 786440 | tf_op jit(solution)/shard_map/ppermute | solution.py:112
  32.8 4.1 %collective-permute-done.refs_2_ = f32[64,1024]{1,0:T(8,128)S(1)} collective-permute-done((f32[64,1024]{1,0:T(8,128)S(1)}, f32[64,1024]{1,0:T(8,128)S(1)}, u32[]{:S(2)}, u32[]{:S(2)}) %collective-permute-start) | collective-permute-done | bytes 262176 | tf_op jit(solution)/shard_map/ppermute | solution.py:112
  37.7 4.1 %collective-permute-done.5.refs_7_ = f32[64,1024]{1,0:T(8,128)S(1)} collective-permute-done((f32[64,1024]{1,0:T(8,128)S(1)}, f32[64,1024]{1,0:T(8,128)S(1)}, u32[]{:S(2)}, u32[]{:S(2)}) %collective-permute-start.5) | collective-permute-done | bytes 262176 | tf_op jit(solution)/shard_map/ppermute | solution.py:112
  41.8 2.1 %collective-permute-done.4.refs_6_ = f32[64,1024]{1,0:T(8,128)} collective-permute-done((f32[64,1024]{1,0:T(8,128)S(1)}, f32[64,1024]{1,0:T(8,128)}, u32[]{:S(2)}, u32[]{:S(2)}) %collective-permute-start.4) | collective-permute-done | bytes 262176 | tf_op jit(solution)/shard_map/ppermute | solution.py:112
  44.8 3.6 %shard_map.58 = (f32[512,512]{1,0:T(8,128)S(1)}, f32[8,512]{1,0:T(8,128)S(1)}, bf16[512,1024]{1,0:T(8,128)(2,1)S(1)}, bf16[512,1024]{1,0:T(8,128)(2,1)S(1)}, bf1...) custom-call(f32[64,1024]{1,0:T(8,128)S(1)} %get-tuple-element.42.refs_0_, ...), custom_call_target="tpu_custom_call" | custom-call | flops 1610612736 | bytes 8388608 | tf_op jit(solution)/shard_map/pallas_call | solution.py:17
  48.5 1.5 %collective-permute-start.16 = (f32[8,512]{1,0:T(8,128)S(1)}, f32[8,512]{1,0:T(8,128)S(1)}, u32[]{:S(2)}, u32[]{:S(2)}) collective-permute-start(f32[8,512]{1,0:T(8,128)S(1)} %get-tuple-element.19.refs_0_), channel_id=1, source_target_pairs={{0,3},{1,2},{2,1},{3,0},{4,7},{5,6},{6,5},{7,4},{8,11},{9,10},{10,... | collective-permute-start | bytes 49160 | tf_op jit(solution)/shard_map/ppermute | solution.py:112
  50.0 1.5 %collective-permute-start.15 = (f32[8,512]{1,0:T(8,128)S(1)}, f32[8,512]{1,0:T(8,128)S(1)}, u32[]{:S(2)}, u32[]{:S(2)}) collective-permute-start(f32[8,512]{1,0:T(8,128)S(1)} %get-tuple-element.19.refs_0_), channel_id=1, source_target_pairs={{0,2},{1,3},{2,0},{3,1},{4,6},{5,7},{6,4},{7,5},{8,10},{9,11},{10,... | collective-permute-start | bytes 49160 | tf_op jit(solution)/shard_map/ppermute | solution.py:112
  52.0 1.1 %collective-permute-done.16.refs_3_ = f32[8,512]{1,0:T(8,128)S(1)} collective-permute-done((f32[8,512]{1,0:T(8,128)S(1)}, f32[8,512]{1,0:T(8,128)S(1)}, u32[]{:S(2)}, u32[]{:S(2)}) %collective-permute-start.16) | collective-permute-done | bytes 16416 | tf_op jit(solution)/shard_map/ppermute | solution.py:112
  53.7 1.5 %collective-permute-done.14.refs_1_ = f32[8,512]{1,0:T(8,128)S(1)} collective-permute-done((f32[8,512]{1,0:T(8,128)S(1)}, f32[8,512]{1,0:T(8,128)S(1)}, u32[]{:S(2)}, u32[]{:S(2)}) %collective-permute-start.14) | collective-permute-done | bytes 16416 | tf_op jit(solution)/shard_map/ppermute | solution.py:112
  55.2 1.8 %shard_map.62 = f32[512,1024]{1,0:T(8,128)S(1)} custom-call(f32[8,512]{1,0:T(8,128)S(1)} %get-tuple-element.19.refs_0_, f32[8,512]{1,0:T(8,128)S(1)} %collective-permute-done.14.refs_1_, f32[8,512]{1,0:T(8,128)S(1)} %collective-permute-done.15.refs_2_, f32[8,512]{1,0:T(8,128)S(1)} %collective-permute-done.16.refs_3_, ...), custom_call_target="tpu_custom_call" | custom-call | flops 1610612736 | bytes 8388608 | tf_op jit(solution)/shard_map/pallas_call | solution.py:17
  58.7 4.6 %collective-permute-start.29 = (f32[64,1024]{1,0:T(8,128)S(1)}, f32[64,1024]{1,0:T(8,128)S(1)}, u32[]{:S(2)}, u32[]{:S(2)}) collective-permute-start(f32[64,1024]{1,0:T(8,128)S(1)} %slice_add_fusion.1), channel_id=1, source_target_pairs={{0,8},{1,9},{2,10},{3,11},{4,12},{5,13},{6,14},{7,15},{24,16},{25,... | collective-permute-start | bytes 786440 | tf_op jit(solution)/shard_map/ppermute | solution.py:112
  63.3 2.9 %shard_map.59 = (f32[512,1024]{1,0:T(8,128)S(1)}, f32[512,1024]{1,0:T(8,128)S(1)}) custom-call(f32[512,512]{1,0:T(8,128)S(1)} %get-tuple-element.20.et.refs_4_, s32[1,512]{1,0:T(1,128)S(1)} %compare_select_fusion.refs_16_.pos.refs_5_, bf16[512,1024]{1,0:T(8,128)(2,1)S(1)} %get-tuple-element.21.ph, bf16[512,1024]{1,0:T(8,128)(2,1)S(1)} %get-tuple-element.22.pl_), custom_call_target="tpu_custom_call" | custom-call | flops 2684354560 | bytes 8388608 | tf_op jit(solution)/shard_map/pallas_call | solution.py:17
  67.9 1.3 %collective-permute-done.29 = f32[64,1024]{1,0:T(8,128)S(1)} collective-permute-done((f32[64,1024]{1,0:T(8,128)S(1)}, f32[64,1024]{1,0:T(8,128)S(1)}, u32[]{:S(2)}, u32[]{:S(2)}) %collective-permute-start.29) | collective-permute-done | bytes 262176 | tf_op jit(solution)/shard_map/ppermute | solution.py:112
  69.9 1.1 %collective-permute-start.22 = (f32[64,1024]{1,0:T(8,128)S(1)}, f32[64,1024]{1,0:T(8,128)S(1)}, u32[]{:S(2)}, u32[]{:S(2)}) collective-permute-start(f32[64,1024]{1,0:T(8,128)S(1)} %get-tuple-element.32), channel_id=1, source_target_pairs={{0,2},{1,3},{2,0},{3,1},{4,6},{5,7},{6,4},{7,5},{8,10},{9,11},{10,... | collective-permute-start | bytes 786440 | tf_op jit(solution)/shard_map/ppermute | solution.py:112
  71.0 4.9 %collective-permute-done.18 = f32[64,1024]{1,0:T(8,128)S(1)} collective-permute-done((f32[64,1024]{1,0:T(8,128)S(1)}, f32[64,1024]{1,0:T(8,128)S(1)}, u32[]{:S(2)}, u32[]{:S(2)}) %collective-permute-start.18) | collective-permute-done | bytes 262176 | tf_op jit(solution)/shard_map/ppermute | solution.py:112
  77.9 1.5 %collective-permute-start.21 = (f32[64,1024]{1,0:T(8,128)}, f32[64,1024]{1,0:T(8,128)}, u32[]{:S(2)}, u32[]{:S(2)}) collective-permute-start(f32[64,1024]{1,0:T(8,128)} %add.59), channel_id=1, source_target_pairs={{0,2},{1,3},{2,0},{3,1},{4,6},{5,7},{6,4},{7,5},{8,10},{9,11},{10,... | collective-permute-start | bytes 786440 | tf_op jit(solution)/shard_map/ppermute | solution.py:112
  79.4 2.7 %collective-permute-done.17 = f32[64,1024]{1,0:T(8,128)S(1)} collective-permute-done((f32[64,1024]{1,0:T(8,128)S(1)}, f32[64,1024]{1,0:T(8,128)S(1)}, u32[]{:S(2)}, u32[]{:S(2)}) %collective-permute-start.17) | collective-permute-done | bytes 262176 | tf_op jit(solution)/shard_map/ppermute | solution.py:112
  82.2 4.1 %collective-permute-done.19 = f32[64,1024]{1,0:T(8,128)S(1)} collective-permute-done((f32[64,1024]{1,0:T(8,128)S(1)}, f32[64,1024]{1,0:T(8,128)S(1)}, u32[]{:S(2)}, u32[]{:S(2)}) %collective-permute-start.19) | collective-permute-done | bytes 262176 | tf_op jit(solution)/shard_map/ppermute | solution.py:112
  86.9 1.1 %gather_fusion.1 = f32[4,128]{1,0:T(4,128)} fusion(f32[4,128]{1,0:T(4,128)S(1)} %bitcast.7, s32[1024]{0:T(1024)S(1)} %pad_clamp_fusion), kind=kCustom, calls=%fused_computation.1 | custom fusion | bytes 4112 | tf_op jit(solution)/shard_map/gather | solution.py:178
  89.2 1.1 %pad_maximum_fusion.1.refs_3_ = f32[128,1024]{1,0:T(8,128)S(1)} fusion(f32[64,1024]{1,0:T(8,128)} %copy-done.4, f32[64,1024]{1,0:T(8,128)} %collective-permute-done.21), kind=kLoop, calls=%fused_computation.3 | loop fusion | flops 131072 | bytes 1048576 | tf_op jit(solution)/shard_map/concatenate | solution.py:179
  91.4 3.6 %collective-permute-done.30.refs_5_ = f32[64,1024]{1,0:T(8,128)S(1)} collective-permute-done((f32[64,1024]{1,0:T(8,128)S(1)}, f32[64,1024]{1,0:T(8,128)S(1)}, u32[]{:S(2)}, u32[]{:S(2)}) %collective-permute-start.30) | collective-permute-done | bytes 262176 | tf_op jit(solution)/shard_map/ppermute | solution.py:112
  95.0 3.6 %collective-permute-done.25.refs_3_ = f32[64,1024]{1,0:T(8,128)S(1)} collective-permute-done((f32[64,1024]{1,0:T(8,128)S(1)}, f32[64,1024]{1,0:T(8,128)S(1)}, u32[]{:S(2)}, u32[]{:S(2)}) %collective-permute-start.25) | collective-permute-done | bytes 262176 | tf_op jit(solution)/shard_map/ppermute | solution.py:112
  (65 shorter events, 15.1 us)
Async XLA Ops:
  0.6 36.4 %copy-start = (s32[512]{0:T(512)S(1)}, s32[512]{0:T(512)}, u32[]{:S(2)}) copy-start(s32[512]{0:T(512)} %param.5) | copy-start | bytes 6148
  0.6 17.1 %collective-permute-start.9 = (f32[64,1024]{1,0:T(8,128)}, f32[64,1024]{1,0:T(8,128)S(1)}, u32[]{:S(2)}, u32[]{:S(2)}) collective-permute-start(f32[64,1024]{1,0:T(8,128)} %refs_0_.3), channel_id=1, source_target_pairs={{0,16},{1,17},{2,18},{3,19},{4,20},{5,21},{6,22},{7,23},{8,24},{9,... | collective-permute-start | bytes 786440 | tf_op jit(solution)/shard_map/ppermute | solution.py:112
  4.7 17.4 %collective-permute-start.11 = (f32[64,1024]{1,0:T(8,128)}, f32[64,1024]{1,0:T(8,128)S(1)}, u32[]{:S(2)}, u32[]{:S(2)}) collective-permute-start(f32[64,1024]{1,0:T(8,128)} %refs_0_.3), channel_id=1, source_target_pairs={{8,16},{9,17},{10,18},{11,19},{12,20},{13,21},{14,22},{15,23},{16,... | collective-permute-start | bytes 786440 | tf_op jit(solution)/shard_map/ppermute | solution.py:112
  5.4 18.2 %collective-permute-start.7 = (f32[64,1024]{1,0:T(8,128)}, f32[64,1024]{1,0:T(8,128)S(1)}, u32[]{:S(2)}, u32[]{:S(2)}) collective-permute-start(f32[64,1024]{1,0:T(8,128)} %refs_0_.3), channel_id=1, source_target_pairs={{0,8},{1,9},{2,10},{3,11},{4,12},{5,13},{6,14},{7,15},{8,0},{9,1},... | collective-permute-start | bytes 786440 | tf_op jit(solution)/shard_map/ppermute | solution.py:112
  17.8 8.5 %collective-permute-start.12 = (f32[64,1024]{1,0:T(8,128)S(1)}, f32[64,1024]{1,0:T(8,128)S(1)}, u32[]{:S(2)}, u32[]{:S(2)}) collective-permute-start(f32[64,1024]{1,0:T(8,128)S(1)} %collective-permute-done.9.refs_12_), channel_id=1, source_target_pairs={{8,0},{9,1},{10,2},{11,3},{12,4},{13,5},{14,6},{15,7},{16,24},{17,... | collective-permute-start | bytes 786440 | tf_op jit(solution)/shard_map/ppermute | solution.py:112
  19.0 8.9 %collective-permute-start.6 = (f32[64,1024]{1,0:T(8,128)}, f32[64,1024]{1,0:T(8,128)S(1)}, u32[]{:S(2)}, u32[]{:S(2)}) collective-permute-start(f32[64,1024]{1,0:T(8,128)} %refs_0_.3), channel_id=1, source_target_pairs={{0,4},{1,5},{2,6},{3,7},{4,0},{5,1},{6,2},{7,3},{8,12},{9,13},{10,... | collective-permute-start | bytes 786440 | tf_op jit(solution)/shard_map/ppermute | solution.py:112
  20.2 9.1 %collective-permute-start.3 = (f32[64,1024]{1,0:T(8,128)S(1)}, f32[64,1024]{1,0:T(8,128)S(1)}, u32[]{:S(2)}, u32[]{:S(2)}) collective-permute-start(f32[64,1024]{1,0:T(8,128)S(1)} %get-tuple-element.41.refs_1_), channel_id=1, source_target_pairs={{0,2},{1,3},{2,0},{3,1},{4,6},{5,7},{6,4},{7,5},{8,10},{9,11},{10,... | collective-permute-start | bytes 786440 | tf_op jit(solution)/shard_map/ppermute | solution.py:112
  22.1 9.1 %collective-permute-start.1 = (f32[64,1024]{1,0:T(8,128)S(1)}, f32[64,1024]{1,0:T(8,128)S(1)}, u32[]{:S(2)}, u32[]{:S(2)}) collective-permute-start(f32[64,1024]{1,0:T(8,128)S(1)} %get-tuple-element.41.refs_1_), channel_id=1, source_target_pairs={{0,1},{1,0},{2,3},{3,2},{4,5},{5,4},{6,7},{7,6},{8,9},{9,8},{10,11... | collective-permute-start | bytes 786440 | tf_op jit(solution)/shard_map/ppermute | solution.py:112
  23.6 13.3 %collective-permute-start = (f32[64,1024]{1,0:T(8,128)S(1)}, f32[64,1024]{1,0:T(8,128)S(1)}, u32[]{:S(2)}, u32[]{:S(2)}) collective-permute-start(f32[64,1024]{1,0:T(8,128)S(1)} %get-tuple-element.42.refs_0_), channel_id=1, source_target_pairs={{0,1},{1,0},{2,3},{3,2},{4,5},{5,4},{6,7},{7,6},{8,9},{9,8},{10,11... | collective-permute-start | bytes 786440 | tf_op jit(solution)/shard_map/ppermute | solution.py:112
  26.3 10.7 %collective-permute-start.2 = (f32[64,1024]{1,0:T(8,128)S(1)}, f32[64,1024]{1,0:T(8,128)S(1)}, u32[]{:S(2)}, u32[]{:S(2)}) collective-permute-start(f32[64,1024]{1,0:T(8,128)S(1)} %get-tuple-element.42.refs_0_), channel_id=1, source_target_pairs={{0,2},{1,3},{2,0},{3,1},{4,6},{5,7},{6,4},{7,5},{8,10},{9,11},{10,... | collective-permute-start | bytes 786440 | tf_op jit(solution)/shard_map/ppermute | solution.py:112
  27.9 9.7 %collective-permute-start.10 = (f32[64,1024]{1,0:T(8,128)S(1)}, f32[64,1024]{1,0:T(8,128)S(1)}, u32[]{:S(2)}, u32[]{:S(2)}) collective-permute-start(f32[64,1024]{1,0:T(8,128)S(1)} %collective-permute-done.9.refs_12_), channel_id=1, source_target_pairs={{0,4},{1,5},{2,6},{3,7},{4,0},{5,1},{6,2},{7,3},{8,12},{9,13},{10,... | collective-permute-start | bytes 786440 | tf_op jit(solution)/shard_map/ppermute | solution.py:112
  29.4 8.3 %collective-permute-start.8 = (f32[64,1024]{1,0:T(8,128)S(1)}, f32[64,1024]{1,0:T(8,128)S(1)}, u32[]{:S(2)}, u32[]{:S(2)}) collective-permute-start(f32[64,1024]{1,0:T(8,128)S(1)} %collective-permute-done.7.refs_10_), channel_id=1, source_target_pairs={{0,4},{1,5},{2,6},{3,7},{4,0},{5,1},{6,2},{7,3},{8,12},{9,13},{10,... | collective-permute-start | bytes 786440 | tf_op jit(solution)/shard_map/ppermute | solution.py:112
  31.3 10.5 %collective-permute-start.5 = (f32[64,1024]{1,0:T(8,128)S(1)}, f32[64,1024]{1,0:T(8,128)S(1)}, u32[]{:S(2)}, u32[]{:S(2)}) collective-permute-start(f32[64,1024]{1,0:T(8,128)S(1)} %collective-permute-done.3.refs_5_), channel_id=1, source_target_pairs={{0,1},{1,0},{2,3},{3,2},{4,5},{5,4},{6,7},{7,6},{8,9},{9,8},{10,11... | collective-permute-start | bytes 786440 | tf_op jit(solution)/shard_map/ppermute | solution.py:112
  36.9 7.0 %collective-permute-start.4 = (f32[64,1024]{1,0:T(8,128)S(1)}, f32[64,1024]{1,0:T(8,128)}, u32[]{:S(2)}, u32[]{:S(2)}) collective-permute-start(f32[64,1024]{1,0:T(8,128)S(1)} %collective-permute-done.refs_2_), channel_id=1, source_target_pairs={{0,2},{1,3},{2,0},{3,1},{4,6},{5,7},{6,4},{7,5},{8,10},{9,11},{10,... | collective-permute-start | bytes 786440 | tf_op jit(solution)/shard_map/ppermute | solution.py:112
  37.0 6.9 %collective-permute-start.13 = (f32[64,1024]{1,0:T(8,128)S(1)}, f32[64,1024]{1,0:T(8,128)}, u32[]{:S(2)}, u32[]{:S(2)}) collective-permute-start(f32[64,1024]{1,0:T(8,128)S(1)} %add.55.refs_14_), channel_id=1, source_target_pairs={{0,4},{1,5},{2,6},{3,7},{4,0},{5,1},{6,2},{7,3},{8,12},{9,13},{10,... | collective-permute-start | bytes 786440 | tf_op jit(solution)/shard_map/ppermute | solution.py:112
  48.5 4.7 %collective-permute-start.16 = (f32[8,512]{1,0:T(8,128)S(1)}, f32[8,512]{1,0:T(8,128)S(1)}, u32[]{:S(2)}, u32[]{:S(2)}) collective-permute-start(f32[8,512]{1,0:T(8,128)S(1)} %get-tuple-element.19.refs_0_), channel_id=1, source_target_pairs={{0,3},{1,2},{2,1},{3,0},{4,7},{5,6},{6,5},{7,4},{8,11},{9,10},{10,... | collective-permute-start | bytes 49160 | tf_op jit(solution)/shard_map/ppermute | solution.py:112
  50.0 3.7 %collective-permute-start.15 = (f32[8,512]{1,0:T(8,128)S(1)}, f32[8,512]{1,0:T(8,128)S(1)}, u32[]{:S(2)}, u32[]{:S(2)}) collective-permute-start(f32[8,512]{1,0:T(8,128)S(1)} %get-tuple-element.19.refs_0_), channel_id=1, source_target_pairs={{0,2},{1,3},{2,0},{3,1},{4,6},{5,7},{6,4},{7,5},{8,10},{9,11},{10,... | collective-permute-start | bytes 49160 | tf_op jit(solution)/shard_map/ppermute | solution.py:112
  51.5 3.7 %collective-permute-start.14 = (f32[8,512]{1,0:T(8,128)S(1)}, f32[8,512]{1,0:T(8,128)S(1)}, u32[]{:S(2)}, u32[]{:S(2)}) collective-permute-start(f32[8,512]{1,0:T(8,128)S(1)} %get-tuple-element.19.refs_0_), channel_id=1, source_target_pairs={{0,1},{1,0},{2,3},{3,2},{4,5},{5,4},{6,7},{7,6},{8,9},{9,8},{10,11... | collective-permute-start | bytes 49160 | tf_op jit(solution)/shard_map/ppermute | solution.py:112
  57.1 1.6 %collective-permute-start.26 = (f32[64,1024]{1,0:T(8,128)S(1)}, f32[64,1024]{1,0:T(8,128)S(1)}, u32[]{:S(2)}, u32[]{:S(2)}) collective-permute-start(f32[64,1024]{1,0:T(8,128)S(1)} %get-tuple-element.40), channel_id=1, source_target_pairs={{0,4},{1,5},{2,6},{3,7},{4,0},{5,1},{6,2},{7,3},{8,12},{9,13},{10,... | collective-permute-start | bytes 786440 | tf_op jit(solution)/shard_map/ppermute | solution.py:112
  57.2 10.7 %collective-permute-start.28 = (f32[64,1024]{1,0:T(8,128)S(1)}, f32[64,1024]{1,0:T(8,128)S(1)}, u32[]{:S(2)}, u32[]{:S(2)}) collective-permute-start(f32[64,1024]{1,0:T(8,128)S(1)} %get-tuple-element.39), channel_id=1, source_target_pairs={{0,4},{1,5},{2,6},{3,7},{4,0},{5,1},{6,2},{7,3},{8,12},{9,13},{10,... | collective-permute-start | bytes 786440 | tf_op jit(solution)/shard_map/ppermute | solution.py:112
  58.7 10.4 %collective-permute-start.29 = (f32[64,1024]{1,0:T(8,128)S(1)}, f32[64,1024]{1,0:T(8,128)S(1)}, u32[]{:S(2)}, u32[]{:S(2)}) collective-permute-start(f32[64,1024]{1,0:T(8,128)S(1)} %slice_add_fusion.1), channel_id=1, source_target_pairs={{0,8},{1,9},{2,10},{3,11},{4,12},{5,13},{6,14},{7,15},{24,16},{25,... | collective-permute-start | bytes 786440 | tf_op jit(solution)/shard_map/ppermute | solution.py:112
  66.6 9.3 %collective-permute-start.18 = (f32[64,1024]{1,0:T(8,128)S(1)}, f32[64,1024]{1,0:T(8,128)S(1)}, u32[]{:S(2)}, u32[]{:S(2)}) collective-permute-start(f32[64,1024]{1,0:T(8,128)S(1)} %get-tuple-element.29), channel_id=1, source_target_pairs={{0,2},{1,3},{2,0},{3,1},{4,6},{5,7},{6,4},{7,5},{8,10},{9,11},{10,... | collective-permute-start | bytes 786440 | tf_op jit(solution)/shard_map/ppermute | solution.py:112
  67.2 9.2 %collective-permute-start.20 = (f32[64,1024]{1,0:T(8,128)S(1)}, f32[64,1024]{1,0:T(8,128)S(1)}, u32[]{:S(2)}, u32[]{:S(2)}) collective-permute-start(f32[64,1024]{1,0:T(8,128)S(1)} %get-tuple-element.31), channel_id=1, source_target_pairs={{0,1},{1,0},{2,3},{3,2},{4,5},{5,4},{6,7},{7,6},{8,9},{9,8},{10,11... | collective-permute-start | bytes 786440 | tf_op jit(solution)/shard_map/ppermute | solution.py:112
  69.3 8.6 %collective-permute-start.24 = (f32[64,1024]{1,0:T(8,128)S(1)}, f32[64,1024]{1,0:T(8,128)S(1)}, u32[]{:S(2)}, u32[]{:S(2)}) collective-permute-start(f32[64,1024]{1,0:T(8,128)S(1)} %get-tuple-element.36), channel_id=1, source_target_pairs={{0,4},{1,5},{2,6},{3,7},{4,0},{5,1},{6,2},{7,3},{8,12},{9,13},{10,... | collective-permute-start | bytes 786440 | tf_op jit(solution)/shard_map/ppermute | solution.py:112
  69.3 12.7 %collective-permute-start.17 = (f32[64,1024]{1,0:T(8,128)S(1)}, f32[64,1024]{1,0:T(8,128)S(1)}, u32[]{:S(2)}, u32[]{:S(2)}) collective-permute-start(f32[64,1024]{1,0:T(8,128)S(1)} %get-tuple-element.27), channel_id=1, source_target_pairs={{0,1},{1,0},{2,3},{3,2},{4,5},{5,4},{6,7},{7,6},{8,9},{9,8},{10,11... | collective-permute-start | bytes 786440 | tf_op jit(solution)/shard_map/ppermute | solution.py:112
  69.9 12.1 %collective-permute-start.22 = (f32[64,1024]{1,0:T(8,128)S(1)}, f32[64,1024]{1,0:T(8,128)S(1)}, u32[]{:S(2)}, u32[]{:S(2)}) collective-permute-start(f32[64,1024]{1,0:T(8,128)S(1)} %get-tuple-element.32), channel_id=1, source_target_pairs={{0,2},{1,3},{2,0},{3,1},{4,6},{5,7},{6,4},{7,5},{8,10},{9,11},{10,... | collective-permute-start | bytes 786440 | tf_op jit(solution)/shard_map/ppermute | solution.py:112
  75.9 10.3 %collective-permute-start.19 = (f32[64,1024]{1,0:T(8,128)S(1)}, f32[64,1024]{1,0:T(8,128)S(1)}, u32[]{:S(2)}, u32[]{:S(2)}) collective-permute-start(f32[64,1024]{1,0:T(8,128)S(1)} %add.58), channel_id=1, source_target_pairs={{0,1},{1,0},{2,3},{3,2},{4,5},{5,4},{6,7},{7,6},{8,9},{9,8},{10,11... | collective-permute-start | bytes 786440 | tf_op jit(solution)/shard_map/ppermute | solution.py:112
  76.5 14.9 %collective-permute-start.27 = (f32[64,1024]{1,0:T(8,128)S(1)}, f32[64,1024]{1,0:T(8,128)S(1)}, u32[]{:S(2)}, u32[]{:S(2)}) collective-permute-start(f32[64,1024]{1,0:T(8,128)S(1)} %slice_add_fusion.1), channel_id=1, source_target_pairs={{8,16},{9,17},{10,18},{11,19},{12,20},{13,21},{14,22},{15,23},{16,... | collective-permute-start | bytes 786440 | tf_op jit(solution)/shard_map/ppermute | solution.py:112
  77.9 11.3 %collective-permute-start.21 = (f32[64,1024]{1,0:T(8,128)}, f32[64,1024]{1,0:T(8,128)}, u32[]{:S(2)}, u32[]{:S(2)}) collective-permute-start(f32[64,1024]{1,0:T(8,128)} %add.59), channel_id=1, source_target_pairs={{0,2},{1,3},{2,0},{3,1},{4,6},{5,7},{6,4},{7,5},{8,10},{9,11},{10,... | collective-permute-start | bytes 786440 | tf_op jit(solution)/shard_map/ppermute | solution.py:112
  82.1 12.9 %collective-permute-start.30 = (f32[64,1024]{1,0:T(8,128)S(1)}, f32[64,1024]{1,0:T(8,128)S(1)}, u32[]{:S(2)}, u32[]{:S(2)}) collective-permute-start(f32[64,1024]{1,0:T(8,128)S(1)} %get-tuple-element.35), channel_id=1, source_target_pairs={{0,16},{1,17},{2,18},{3,19},{4,20},{5,21},{6,22},{7,23},{8,24},{9,... | collective-permute-start | bytes 786440 | tf_op jit(solution)/shard_map/ppermute | solution.py:112
  82.1 12.9 %collective-permute-start.23 = (f32[64,1024]{1,0:T(8,128)S(1)}, f32[64,1024]{1,0:T(8,128)S(1)}, u32[]{:S(2)}, u32[]{:S(2)}) collective-permute-start(f32[64,1024]{1,0:T(8,128)S(1)} %get-tuple-element.37), channel_id=1, source_target_pairs={{0,4},{1,5},{2,6},{3,7},{4,0},{5,1},{6,2},{7,3},{8,12},{9,13},{10,... | collective-permute-start | bytes 786440 | tf_op jit(solution)/shard_map/ppermute | solution.py:112
  86.2 12.4 %collective-permute-start.25 = (f32[64,1024]{1,0:T(8,128)S(1)}, f32[64,1024]{1,0:T(8,128)S(1)}, u32[]{:S(2)}, u32[]{:S(2)}) collective-permute-start(f32[64,1024]{1,0:T(8,128)S(1)} %slice_add_fusion.2), channel_id=1, source_target_pairs={{0,8},{1,9},{2,10},{3,11},{4,12},{5,13},{6,14},{7,15},{8,0},{9,1},... | collective-permute-start | bytes 786440 | tf_op jit(solution)/shard_map/ppermute | solution.py:112
  (6 other events, 33.9 us)

commit v2 on v1

v2 whole, which is shorter than its diff:
```python
import functools

import jax
import jax.numpy as jnp
from jax import lax
from jax.experimental import pallas as pl
from jax.experimental.pallas import tpu as pltpu
from jax.sharding import PartitionSpec as P

inv_temp = 20.0
f32 = jnp.float32
bf16 = jnp.bfloat16
AXES = ("pb", "pa")


def call(kernel, outs, flops, *args):
    return pl.pallas_call(
        kernel,
        out_shape=[jax.ShapeDtypeStruct(s, d) for s, d in outs],
        compiler_params=pltpu.CompilerParams(vmem_limit_bytes=40 * 1024 * 1024),
        cost_estimate=pl.CostEstimate(flops=flops, bytes_accessed=8 << 20, transcendentals=0),
    )(*args)


def split(x):
    hi = x.astype(bf16)
    return hi, (x - hi.astype(f32)).astype(bf16)


def mm(a, b, dims):
    return lax.dot_general(a, b, (dims, ((), ())), preferred_element_type=f32)


def mm3(a, b, dims):
    (ah, al), (bh, bl) = a, b
    return mm(al, bh, dims) + mm(ah, bl, dims) + mm(ah, bh, dims)


def normalize(rows):
    scale = lax.rsqrt(jnp.sum(rows * rows, axis=1, keepdims=True) + 1e-06)
    return rows * scale, scale


def onehot(pos, shape, first):
    return lax.broadcasted_iota(jnp.int32, shape, 0) + first == pos


def combine(stats):
    n = stats[0].shape[1] // len(stats)
    blocks = [sum(r[:, (m ^ k) * n : (m ^ k) * n + n] for k, r in enumerate(stats)) for m in range(len(stats))]
    return jnp.concatenate(blocks, axis=1)


def load(parts, hi, lo):
    at = 0
    for r in parts:
        n = r.shape[0]
        hi[at : at + n], lo[at : at + n] = split(normalize(r[...])[0])
        at += n


def product(p, q):
    return inv_temp * mm3((p[0][...], p[1][...]), (q[0][...], q[1][...]), ((1,), (1,)))


def first_scores_kernel(n_q, n_p, *refs):
    qs, ps = refs[:n_q], refs[n_q : n_q + n_p]
    pos, et, stats, qh, ql, ph, pl_ = refs[n_q + n_p :]
    load(qs, qh, ql)
    load(ps, ph, pl_)
    st = product((ph, pl_), (qh, ql))
    write_stats(stats, et, st, pos[:, : st.shape[1]], 0)


def write_stats(stats, et, st, pos, first):
    e = jnp.exp(st)
    et[...] = e
    stats[...] = jnp.zeros(stats.shape, f32)
    stats[0:1] = jnp.sum(e, axis=0, keepdims=True)
    stats[1:2] = jnp.sum(jnp.where(onehot(pos, st.shape, first), st, 0.0), axis=0, keepdims=True)


def rest_scores_kernel(n_q, n_p, *refs):
    qs, ps = refs[:n_q], refs[n_q : n_q + n_p]
    pos, et1, stats1, qh1, ql1, ph1, pl1, et, stats, qh, ql, ph, pl_ = refs[n_q + n_p :]
    n, m = qh1.shape[0], ph1.shape[0]
    rows, cols = qh.shape[0], m + ph.shape[0]
    qh[:n] = qh1[...]
    ql[:n] = ql1[...]
    load(qs, qh.at[n:], ql.at[n:])
    load(ps, ph, pl_)
    top = product((ph1, pl1), (qh.at[n:], ql.at[n:]))
    low = product((ph, pl_), (qh, ql))
    e_top, e_low = jnp.exp(top), jnp.exp(low)
    et[:m, :n] = et1[...]
    et[:m, n:] = e_top
    et[m:, :] = e_low
    o_top, o_low = onehot(pos[:, n:], top.shape, 0), onehot(pos[...], low.shape, m)
    sum_low = jnp.sum(e_low, axis=0, keepdims=True)
    pos_low = jnp.sum(jnp.where(o_low, low, 0.0), axis=0, keepdims=True)
    stats[...] = jnp.zeros(stats.shape, f32)
    stats[0:1, :n] = stats1[0:1] + sum_low[:, :n]
    stats[1:2, :n] = stats1[1:2] + pos_low[:, :n]
    stats[0:1, n:] = jnp.sum(e_top, axis=0, keepdims=True) + sum_low[:, n:]
    stats[1:2, n:] = jnp.sum(jnp.where(o_top, top, 0.0), axis=0, keepdims=True) + pos_low[:, n:]


def unscaled_kernel(n_p, et, pos, *refs):
    ps, (u, v) = refs[: 2 * n_p], refs[2 * n_p :]
    at = 0
    for ph, pl_ in zip(ps[:n_p], ps[n_p:]):
        n = ph.shape[0]
        p = (ph[...], pl_[...])
        o = onehot(pos[...], (n, et.shape[1]), at).astype(f32).T.astype(bf16)
        part_u = mm3(split(et[at : at + n].T), p, ((1,), (0,)))
        part_v = mm(o, p[1], ((1,), (0,))) + mm(o, p[0], ((1,), (0,)))
        u[...] = part_u if at == 0 else u[...] + part_u
        v[...] = part_v if at == 0 else v[...] + part_v
        at += n


def scale_kernel(n_stats, q_cuts, p_rows, *refs):
    stats = refs[:n_stats]
    u, v, et, pos, qh, ql, losses, dh, dl, *outs = refs[n_stats:]
    both = combine(stats)
    losses[...] = jnp.log(both[0:1]) - both[1:2]
    total = both[0:1]
    d = et[...] * (1.0 / total) - onehot(pos[...], et.shape, 0).astype(f32)
    dh[...], dl[...] = split(d)
    at = et.shape[0]
    q = (qh[...], ql[...])
    for out, n in reversed(list(zip(outs[len(q_cuts) :], p_rows))):
        at -= n
        out[...] = mm3((dh[at : at + n], dl[at : at + n]), q, ((1,), (0,)))
    inv = (1.0 / both).T[:, 0:1]
    at = u.shape[0]
    for out, n in reversed(list(zip(outs, q_cuts))):
        at -= n
        out[...] = u[at : at + n] * inv[at : at + n] - v[at : at + n]


def passage_kernel(cuts, dh, dl, qh, ql, *outs):
    q = (qh[...], ql[...])
    at = 0
    for out, n in zip(outs, cuts):
        out[...] = mm3((dh[at : at + n], dl[at : at + n]), q, ((1,), (0,)))
        at += n


def query_kernel(n_stats, *refs):
    stats = refs[:n_stats]
    u, v, fa, fb, gx, gy, own = refs[n_stats:]
    inv = (1.0 / combine(stats)).T[:, 0:1]
    h = fa.shape[0]

    def part(k):
        return u[k * h : k * h + h] * inv[k * h : k * h + h] - v[k * h : k * h + h]

    gx[:h] = part(2)
    gx[h:] = part(3) + fb[...]
    gy[:h] = part(4) + fa[...]
    gy[h:] = part(5)
    own[:h] = part(0)
    own[h:] = part(1)


def final_kernel(*refs):
    rows, parts, out = refs[0], refs[1:-1], refs[-1]
    xn, scale = normalize(rows[...])
    g = parts[0][...]
    for part in parts[1:]:
        g = g + part[...]
    g = inv_temp * g
    out[...] = scale * (g - xn * jnp.sum(xn * g, axis=1, keepdims=True))


def flip(x, mask, only=None):
    n = lax.axis_size("pb") * lax.axis_size("pa")
    pairs = [(i, i ^ mask) for i in range(n) if only is None or only(i)]
    return lax.ppermute(x, AXES, pairs)


X, Y, C, Z1, Z2, Z3 = 1, 2, 4, 8, 16, 24


def middle(i):
    return (i // 8) in (1, 2)


def ends(i):
    return not middle(i)


def rows_of(x, *cuts):
    at, out = 0, []
    for n in cuts:
        out.append(lax.slice_in_dim(x, at, at + n, axis=0))
        at += n
    return out


def after(x, *others):
    return lax.optimization_barrier((x,) + others)[0]


def small_body(queries, passages, positive):
    qr, pr = queries.shape[0], passages.shape[0]
    h = qr // 2
    p_rows = 8 * pr
    pa, pb = lax.axis_index("pa"), lax.axis_index("pb")

    order = jnp.arange(4, dtype=jnp.int32) ^ pa
    pos = positive.reshape(4, qr)[order].reshape(1, 4 * qr)
    block = ((pos % p_rows) // pr) ^ pb
    place = jnp.array([0, 3, 1, 4, 2, 5, 6, 7], jnp.int32)
    pos = jnp.where(pos // p_rows == pa, place[block] * pr + pos % pr, -1)

    x, y = flip(queries, X), flip(queries, Y)
    z2, z1 = flip(passages, Z2), flip(passages, Z1)
    c0 = flip(passages, C)
    da, db = flip(x[:h], Y), flip(y[h:], X)
    far = flip(z2, Z1, middle)
    mid = flip(after(passages, z2), Z3, middle)
    c1, c2 = flip(z1, C), flip(z2, C)
    first = first_scores([queries, x], [passages, z1, z2, c0], pos)
    z3 = mid + far
    c3 = flip(z3, C)

    et, stats, qh, ql, ph2, pl2 = rest_scores([y, da, db], [c1, c2, z3, c3], pos, first)
    et1, stats1, qh1, ql1, ph1, pl1 = first
    both = [stats, flip(stats, X), flip(stats, Y), flip(stats, X + Y)]
    u, v = unscaled(et, pos, [ph1, ph2], [pl1, pl2])
    losses, dh, dl, gda, gdb, g3, gc3 = scale(both, u, v, et, pos, qh, ql, (h, h), (pr, pr))

    t3 = flip(gc3, C)
    fa, fb = flip(gda, X), flip(gdb, Y)
    g3 = g3 + t3
    ff = flip(g3, Z1, ends)
    rmid = flip(g3, Z3, middle)
    gz, gc = passage_grads(dh, dl, qh, ql, (3 * pr, 3 * pr))
    tc = flip(gc, C)
    gx, gy, own = query_grads(both, u, v, fa, fb)
    rx, ry = flip(gx, X), flip(gy, Y)
    r1 = flip(after(gz[pr : 2 * pr] + tc[pr : 2 * pr], ff), Z1)
    r2 = flip(gz[2 * pr :] + tc[2 * pr :] + ff, Z2)

    losses = losses.reshape(4, qr)[order].reshape(4 * qr)
    query_grad = finish(queries, own, rx, ry)
    passage_grad = finish(passages, gz[:pr], tc[:pr], r1, rmid, r2)
    return losses, query_grad, passage_grad


def rows(parts):
    return sum(x.shape[0] for x in parts)


def first_scores(q_parts, p_parts, pos):
    q, p, d = rows(q_parts), rows(p_parts), q_parts[0].shape[1]
    return call(
        functools.partial(first_scores_kernel, len(q_parts), len(p_parts)),
        [((p, q), f32), ((8, q), f32), ((q, d), bf16), ((q, d), bf16), ((p, d), bf16), ((p, d), bf16)],
        6 * q * p * d,
        *q_parts,
        *p_parts,
        pos,
    )


def rest_scores(q_parts, p_parts, pos, first):
    p1, q1 = first[0].shape
    q, p, d = q1 + rows(q_parts), rows(p_parts), q_parts[0].shape[1]
    return call(
        functools.partial(rest_scores_kernel, len(q_parts), len(p_parts)),
        [((p1 + p, q), f32), ((8, q), f32), ((q, d), bf16), ((q, d), bf16), ((p, d), bf16), ((p, d), bf16)],
        6 * q * p * d,
        *q_parts,
        *p_parts,
        pos,
        *first,
    )


def unscaled(et, pos, hi, lo):
    p, q = et.shape
    d = hi[0].shape[1]
    return call(
        functools.partial(unscaled_kernel, len(hi)), [((q, d), f32)] * 2, 10 * q * p * d, et, pos, *hi, *lo
    )


def scale(both, u, v, et, pos, qh, ql, q_cuts, p_cuts):
    p, q = et.shape
    d = qh.shape[1]
    return call(
        functools.partial(scale_kernel, len(both), q_cuts, p_cuts),
        [((1, q), f32), ((p, q), bf16), ((p, q), bf16)] + [((n, d), f32) for n in q_cuts + p_cuts],
        6 * q * sum(p_cuts) * d,
        *both,
        u,
        v,
        et,
        pos,
        qh,
        ql,
    )


def passage_grads(dh, dl, qh, ql, cuts):
    q, d = qh.shape
    return call(
        functools.partial(passage_kernel, cuts), [((n, d), f32) for n in cuts], 6 * q * sum(cuts) * d, dh, dl, qh, ql
    )


def query_grads(both, u, v, fa, fb):
    h, d = fa.shape
    return call(
        functools.partial(query_kernel, len(both)), [((2 * h, d), f32)] * 3, 18 * h * d, *both, u, v, fa, fb
    )


def finish(rows, *parts):
    return call(final_kernel, [(rows.shape, f32)], 12 * rows.size, rows, *parts)[0]


def body(queries, passages, positive):
    pa = lax.axis_index("pa")
    q_full = lax.all_gather(queries, "pa", axis=0, tiled=True)
    p_full = lax.all_gather(passages, "pb", axis=0, tiled=True)
    p_rows, q_rows = p_full.shape[0], q_full.shape[0]
    pos = positive - pa * p_rows
    pos = jnp.where((pos >= 0) & (pos < p_rows), pos, -1).reshape(1, -1)
    et, stats, qh, ql, ph, pl_ = first_scores([q_full], [p_full], pos)
    both = [lax.psum(stats, "pa")]
    u, v = unscaled(et, pos, [ph], [pl_])
    losses, dh, dl, gq, gp = scale(both, u, v, et, pos, qh, ql, (q_rows,), (p_rows,))
    q_part = lax.psum_scatter(gq, "pa", scatter_dimension=0, tiled=True)
    p_part = lax.psum_scatter(gp, "pb", scatter_dimension=0, tiled=True)
    return losses.reshape(-1), finish(queries, q_part), finish(passages, p_part)


def solution(mesh):
    placed = (P(("pb", "pa"), None), P(("pa", "pb"), None), P("pb"))
    small = mesh.shape["pa"] == 4 and mesh.shape["pb"] == 8
    return jax.shard_map(
        small_body if small else body,
        mesh=mesh,
        in_specs=placed,
        out_specs=(P("pb"), P(("pb", "pa"), None), P(("pa", "pb"), None)),
        check_vma=False,
    )
```

time: 99.8 us -> 79.4 us (0.80)
  waiting for transfers between devices: 49.6 us -> 33.7 us
  starting transfers between devices: 30.7 us -> 27.1 us
  Pallas kernels: 10.7 us -> 12.9 us
  local copies, waits for them, and re-layouts: 4.46 us -> 2.69 us
  other arithmetic: 3.18 us -> 1.81 us
    ppermute x31 -> x25, waiting for transfers between devices: 49.6 us -> 33.7 us  [flip(): return lax.ppermute(x, AXES, pairs)]
    ppermute x31 -> x25, starting transfers between devices: 30.7 us -> 27.1 us  [flip(): return lax.ppermute(x, AXES, pairs)]
    pallas_call x6 -> x8, Pallas kernels: 10.7 us -> 12.9 us  [call(): pl.pallas_call(kernel, out_shape=[jax.ShapeDtypeStruct(s, d) for s, d in...]
    concatenate x2 -> x0, other arithmetic: 2.18 us -> none  [the longest x1 1.11 us: small_body(): jnp.concatenate([rya, ryb])]
    slice x2, local copies, waits for them, and re-layouts: 1.11 us -> 0.04 us  [small_body(): da, db = (flip(x[:h], Y), flip(y[h:], X))]
  transfers between devices with their start and end apart: 31 -> 25, of which waited for: 17 -> 9; matrix products, arithmetic and copies ran while one was open for 6% -> 4% of each run, Pallas kernels for 4% -> 8%
where the time goes in v2:
time: 79.4 us; the launch traced here: 79.2 us
  waiting for transfers between devices  33.7 us (42%)
  starting transfers between devices  27.1 us (34%)
  Pallas kernels  12.9 us (16%)
  local copies, waits for them, and re-layouts  2.69 us (3%)
  other arithmetic  1.81 us (2%)
  between operations  0.89 us (1%)
    ppermute x25, waiting for transfers between devices, flip(): return lax.ppermute(x, AXES, pairs)  33.7 us
    ppermute x25, starting transfers between devices, flip(): return lax.ppermute(x, AXES, pairs)  27.1 us
    pallas_call x8, Pallas kernels, call(): pl.pallas_call(kernel, out_shape=[jax.ShapeDtypeStruct(s, d) for s, d in...  12.9 us
  transfers between devices with their start and end apart: 25, of which 9 were waited for; matrix products, arithmetic and copies ran while one was open for 4% of the time, Pallas kernels for 8%

profile of v2, /device:TPU:0, one launch (start us, length us, event | category | flops | bytes accessed | tf_op | source)
XLA Modules:
  0.0 79.2 jit_solution(3753147370073334780)
XLA Ops:
  0.7 3.0 %collective-permute-start.1 = (f32[128,1024]{1,0:T(8,128)}, f32[128,1024]{1,0:T(8,128)S(1)}, u32[]{:S(2)}, u32[]{:S(2)}) collective-permute-start(f32[128,1024]{1,0:T(8,128)} %refs_0_.4), channel_id=1, source_target_pairs={{0,1},{1,0},{2,3},{3,2},{4,5},{5,4},{6,7},{7,6},{8,9},{9,8},{10,11... | collective-permute-start | bytes 1572872 | tf_op jit(solution)/shard_map/ppermute | solution.py:180
  3.7 1.5 %collective-permute-start = (f32[128,1024]{1,0:T(8,128)}, f32[128,1024]{1,0:T(8,128)S(1)}, u32[]{:S(2)}, u32[]{:S(2)}) collective-permute-start(f32[128,1024]{1,0:T(8,128)} %refs_0_.4), channel_id=1, source_target_pairs={{0,2},{1,3},{2,0},{3,1},{4,6},{5,7},{6,4},{7,5},{8,10},{9,11},{10,... | collective-permute-start | bytes 1572872 | tf_op jit(solution)/shard_map/ppermute | solution.py:180
  5.2 1.6 %collective-permute-start.4 = (f32[64,1024]{1,0:T(8,128)}, f32[64,1024]{1,0:T(8,128)S(1)}, u32[]{:S(2)}, u32[]{:S(2)}) collective-permute-start(f32[64,1024]{1,0:T(8,128)} %refs_0_.5), channel_id=1, source_target_pairs={{0,8},{1,9},{2,10},{3,11},{4,12},{5,13},{6,14},{7,15},{8,0},{9,1},... | collective-permute-start | bytes 786440 | tf_op jit(solution)/shard_map/ppermute | solution.py:180
  6.8 2.6 %collective-permute-start.6 = (f32[64,1024]{1,0:T(8,128)}, f32[64,1024]{1,0:T(8,128)S(1)}, u32[]{:S(2)}, u32[]{:S(2)}) collective-permute-start(f32[64,1024]{1,0:T(8,128)} %refs_0_.5), channel_id=1, source_target_pairs={{0,16},{1,17},{2,18},{3,19},{4,20},{5,21},{6,22},{7,23},{8,24},{9,... | collective-permute-start | bytes 786440 | tf_op jit(solution)/shard_map/ppermute | solution.py:180
  10.0 10.8 %collective-permute-done.6.refs_4_ = f32[64,1024]{1,0:T(8,128)S(1)} collective-permute-done((f32[64,1024]{1,0:T(8,128)}, f32[64,1024]{1,0:T(8,128)S(1)}, u32[]{:S(2)}, u32[]{:S(2)}) %collective-permute-start.6) | collective-permute-done | bytes 262176 | tf_op jit(solution)/shard_map/ppermute | solution.py:180
  21.4 1.3 %collective-permute-start.9 = (f32[64,1024]{1,0:T(8,128)S(1)}, f32[64,1024]{1,0:T(8,128)S(1)}, u32[]{:S(2)}, u32[]{:S(2)}) collective-permute-start(f32[64,1024]{1,0:T(8,128)S(1)} %collective-permute-done.6.refs_4_), channel_id=1, source_target_pairs={{8,0},{9,1},{10,2},{11,3},{12,4},{13,5},{14,6},{15,7},{16,24},{17,... | collective-permute-start | bytes 786440 | tf_op jit(solution)/shard_map/ppermute | solution.py:180
  24.0 5.7 %collective-permute-done.9 = f32[64,1024]{1,0:T(8,128)S(1)} collective-permute-done((f32[64,1024]{1,0:T(8,128)S(1)}, f32[64,1024]{1,0:T(8,128)S(1)}, u32[]{:S(2)}, u32[]{:S(2)}) %collective-permute-start.9) | collective-permute-done | bytes 262176 | tf_op jit(solution)/shard_map/ppermute | solution.py:180
  30.4 0.9 %copy-done.2 = f32[64,1024]{1,0:T(8,128)S(1)} copy-done((f32[64,1024]{1,0:T(8,128)S(1)}, f32[64,1024]{1,0:T(8,128)}, u32[]{:S(2)}) %copy-start.2) | copy-done | bytes 262168
  31.4 0.9 %shard_map.67 = (f32[256,256]{1,0:T(8,128)S(1)}, f32[8,256]{1,0:T(8,128)S(1)}, bf16[256,1024]{1,0:T(8,128)(2,1)S(1)}, bf16[256,1024]{1,0:T(8,128)(2,1)S(1)}, bf1...) custom-call(f32[128,1024]{1,0:T(8,128)S(1)} %copy-done.1, f32[128,1024]{1,0:T(8,128)S(1)} %collective-permute-done.1.refs_1_, ...), custom_call_target="tpu_custom_call" | custom-call | flops 402653184 | bytes 8388608 | tf_op jit(solution)/shard_map/pallas_call | solution.py:17
  32.3 3.8 %collective-permute-done.3.refs_2_ = f32[64,1024]{1,0:T(8,128)S(1)} collective-permute-done((f32[64,1024]{1,0:T(8,128)S(1)}, f32[64,1024]{1,0:T(8,128)S(1)}, u32[]{:S(2)}, u32[]{:S(2)}) %collective-permute-start.3) | collective-permute-done | bytes 262176 | tf_op jit(solution)/shard_map/ppermute | solution.py:180
  36.1 1.8 %shard_map.68 = (f32[512,512]{1,0:T(8,128)S(1)}, f32[8,512]{1,0:T(8,128)S(1)}, bf16[512,1024]{1,0:T(8,128)(2,1)S(1)}, bf16[512,1024]{1,0:T(8,128)(2,1)S(1)}, bf1...) custom-call(f32[128,1024]{1,0:T(8,128)S(1)} %collective-permute-done.refs_0_, ...), custom_call_target="tpu_custom_call" | custom-call | flops 805306368 | bytes 8388608 | tf_op jit(solution)/shard_map/pallas_call | solution.py:17
  39.0 2.5 %collective-permute-start.14 = (f32[8,512]{1,0:T(8,128)S(1)}, f32[8,512]{1,0:T(8,128)S(1)}, u32[]{:S(2)}, u32[]{:S(2)}) collective-permute-start(f32[8,512]{1,0:T(8,128)S(1)} %get-tuple-element.38.refs_0_), channel_id=1, source_target_pairs={{0,3},{1,2},{2,1},{3,0},{4,7},{5,6},{6,5},{7,4},{8,11},{9,10},{10,... | collective-permute-start | bytes 49160 | tf_op jit(solution)/shard_map/ppermute | solution.py:180
  41.5 2.9 %shard_map.69 = (f32[512,1024]{1,0:T(8,128)S(1)}, f32[512,1024]{1,0:T(8,128)S(1)}) custom-call(f32[512,512]{1,0:T(8,128)S(1)} %get-tuple-element.39.et.refs_6_, s32[1,512]{1,0:T(1,128)S(1)} %compare_select_fusion.9.refs_6_.refs_7_.pos, bf16[256,1024]{1,0:T(8,128)(2,1)S(1)} %get-tuple-element.36.refs_12_.refs_0_, ...), custom_call_target="tpu_custom_call" | custom-call | flops 2684354560 | bytes 8388608 | tf_op jit(solution)/shard_map/pallas_call | solution.py:17
  44.5 1.6 %shard_map.70 = (f32[1,512]{1,0:T(1,128)S(1)}, bf16[512,512]{1,0:T(8,128)(2,1)S(1)}, bf16[512,512]{1,0:T(8,128)(2,1)S(1)}, f32[64,1024]{1,0:T(8,128)S(1)}, f32[6...) custom-call(f32[8,512]{1,0:T(8,128)S(1)} %get-tuple-element.38.refs_0_, ...), custom_call_target="tpu_custom_call" | custom-call | flops 402653184 | bytes 8388608 | tf_op jit(solution)/shard_map/pallas_call | solution.py:17
  46.1 1.4 %shard_map.73 = (f32[192,1024]{1,0:T(8,128)S(1)}, f32[192,1024]{1,0:T(8,128)S(1)}) custom-call(bf16[512,512]{1,0:T(8,128)(2,1)S(1)} %get-tuple-element.52.dh, bf16[512,512]{1,0:T(8,128)(2,1)S(1)} %get-tuple-element.53.dl, bf16[512,1024]{1,0:T(8,128)(2,1)S(1)} %get-tuple-element.44.refs_8_.qh, bf16[512,1024]{1,0:T(8,128)(2,1)S(1)} %get-tuple-element.45.refs_9_.ql), custom_call_target="tpu_custom_call" | custom-call | flops 1207959552 | bytes 8388608 | tf_op jit(solution)/shard_map/pallas_call | solution.py:17
  48.1 0.7 collective-permute-start.15
  48.8 1.5 %collective-permute-start.16 = (f32[64,1024]{1,0:T(8,128)S(1)}, f32[64,1024]{1,0:T(8,128)S(1)}, u32[]{:S(2)}, u32[]{:S(2)}) collective-permute-start(f32[64,1024]{1,0:T(8,128)S(1)} %get-tuple-element.48), channel_id=1, source_target_pairs={{0,2},{1,3},{2,0},{3,1},{4,6},{5,7},{6,4},{7,5},{8,10},{9,11},{10,... | collective-permute-start | bytes 786440 | tf_op jit(solution)/shard_map/ppermute | solution.py:180
  50.3 0.7 add.106
  51.0 2.6 %collective-permute-start.21 = (f32[64,1024]{1,0:T(8,128)}, f32[64,1024]{1,0:T(8,128)S(1)}, u32[]{:S(2)}, u32[]{:S(2)}) collective-permute-start(f32[64,1024]{1,0:T(8,128)} %add.106), channel_id=1, source_target_pairs={{0,8},{1,9},{2,10},{3,11},{4,12},{5,13},{6,14},{7,15},{24,16},{25,... | collective-permute-start | bytes 786440 | tf_op jit(solution)/shard_map/ppermute | solution.py:180
  54.4 2.0 %collective-permute-done.15.refs_6_ = f32[64,1024]{1,0:T(8,128)S(1)} collective-permute-done((f32[64,1024]{1,0:T(8,128)S(1)}, f32[64,1024]{1,0:T(8,128)S(1)}, u32[]{:S(2)}, u32[]{:S(2)}) %collective-permute-start.15) | collective-permute-done | bytes 262176 | tf_op jit(solution)/shard_map/ppermute | solution.py:180
  56.8 1.3 %shard_map.71 = (f32[128,1024]{1,0:T(8,128)}, f32[128,1024]{1,0:T(8,128)}, f32[128,1024]{1,0:T(8,128)S(1)}) custom-call(f32[8,512]{1,0:T(8,128)S(1)} %get-tuple-element.38.refs_0_, f32[8,512]{1,0:T(8,128)S(1)} %collective-permute-done.12.refs_1_, f32[8,512]{1,0:T(8,128)S(1)} %collective-permute-done.13.refs_2_, ...), custom_call_target="tpu_custom_call" | custom-call | flops 1179648 | bytes 8388608 | tf_op jit(solution)/shard_map/pallas_call | solution.py:17
  58.1 1.3 %collective-permute-start.17 = (f32[128,1024]{1,0:T(8,128)}, f32[128,1024]{1,0:T(8,128)S(1)}, u32[]{:S(2)}, u32[]{:S(2)}) collective-permute-start(f32[128,1024]{1,0:T(8,128)} %get-tuple-element.50), channel_id=1, source_target_pairs={{0,1},{1,0},{2,3},{3,2},{4,5},{5,4},{6,7},{7,6},{8,9},{9,8},{10,11... | collective-permute-start | bytes 1572872 | tf_op jit(solution)/shard_map/ppermute | solution.py:180
  59.4 0.7 collective-permute-start.18
  60.2 0.9 %fusion = (f32[64,1024]{1,0:T(8,128)}, f32[64,1024]{1,0:T(8,128)}, f32[64,1024]{1,0:T(8,128)S(1)}, f32[64,1024]{1,0:T(8,128)S(1)}) fusion(f32[64,1024]{1,0:T(8,128)S(1)} %collective-permute-done.21, f32[192,1024]{1,0:T(8,128)S(1)} %collective-permute-done.19, f32[192,1024]{1,0:T(8,128)S(1)} %get-tuple-element.54), kind=kLoop, calls=%fused_computation.3 | loop fusion | flops 196608 | bytes 2883584 | tf_op jit(solution)/shard_map/add | solution.py:245
  61.1 2.0 %collective-permute-start.22 = (f32[64,1024]{1,0:T(8,128)}, f32[64,1024]{1,0:T(8,128)S(1)}, u32[]{:S(2)}, u32[]{:S(2)}) collective-permute-start(f32[64,1024]{1,0:T(8,128)} %get-tuple-element.58), channel_id=1, source_target_pairs={{0,8},{1,9},{2,10},{3,11},{4,12},{5,13},{6,14},{7,15},{8,0},{9,1},... | collective-permute-start | bytes 786440 | tf_op jit(solution)/shard_map/ppermute | solution.py:180
  63.2 1.0 %collective-permute-start.24 = (f32[64,1024]{1,0:T(8,128)}, f32[64,1024]{1,0:T(8,128)}, u32[]{:S(2)}, u32[]{:S(2)}) collective-permute-start(f32[64,1024]{1,0:T(8,128)} %get-tuple-element.61), channel_id=1, source_target_pairs={{0,16},{1,17},{2,18},{3,19},{4,20},{5,21},{6,22},{7,23},{8,24},{9,... | collective-permute-start | bytes 786440 | tf_op jit(solution)/shard_map/ppermute | solution.py:180
  64.1 1.1 %gather_fusion.1 = f32[4,128]{1,0:T(4,128)} fusion(f32[4,128]{1,0:T(4,128)S(1)} %bitcast.10, s32[1024]{0:T(1024)S(1)} %pad_clamp_fusion), kind=kCustom, calls=%fused_computation.1 | custom fusion | bytes 4112 | tf_op jit(solution)/shard_map/gather | solution.py:247
  65.3 5.8 %collective-permute-done.17.refs_2_ = f32[128,1024]{1,0:T(8,128)S(1)} collective-permute-done((f32[128,1024]{1,0:T(8,128)}, f32[128,1024]{1,0:T(8,128)S(1)}, u32[]{:S(2)}, u32[]{:S(2)}) %collective-permute-start.17) | collective-permute-done | bytes 524320 | tf_op jit(solution)/shard_map/ppermute | solution.py:180
  71.1 1.1 %collective-permute-done.18.refs_3_ = f32[128,1024]{1,0:T(8,128)S(1)} collective-permute-done((f32[128,1024]{1,0:T(8,128)}, f32[128,1024]{1,0:T(8,128)S(1)}, u32[]{:S(2)}, u32[]{:S(2)}) %collective-permute-start.18) | collective-permute-done | bytes 524320 | tf_op jit(solution)/shard_map/ppermute | solution.py:180
  72.1 1.0 %shard_map.72 = f32[128,1024]{1,0:T(8,128)} custom-call(f32[128,1024]{1,0:T(8,128)S(1)} %copy-done.1, f32[128,1024]{1,0:T(8,128)S(1)} %get-tuple-element.49.refs_1_, f32[128,1024]{1,0:T(8,128)S(1)} %collective-permute-done.17.refs_2_, f32[128,1024]{1,0:T(8,128)S(1)} %collective-permute-done.18.refs_3_), custom_call_target="tpu_custom_call" | custom-call | flops 1572864 | bytes 8388608 | tf_op jit(solution)/shard_map/pallas_call | solution.py:17
  73.5 3.8 %collective-permute-done.24.refs_5_ = f32[64,1024]{1,0:T(8,128)} collective-permute-done((f32[64,1024]{1,0:T(8,128)}, f32[64,1024]{1,0:T(8,128)}, u32[]{:S(2)}, u32[]{:S(2)}) %collective-permute-start.24) | collective-permute-done | bytes 262176 | tf_op jit(solution)/shard_map/ppermute | solution.py:180
  77.3 1.9 %shard_map.74 = f32[64,1024]{1,0:T(8,128)} custom-call(f32[64,1024]{1,0:T(8,128)S(1)} %copy-done.3, f32[64,1024]{1,0:T(8,128)S(1)} %get-tuple-element.63.refs_1_, f32[64,1024]{1,0:T(8,128)S(1)} %get-tuple-element.64.refs_2_, f32[64,1024]{1,0:T(8,128)S(1)} %collective-permute-done.22.refs_3_, f32[64,1024]{1,0:T(8,128)S(1)} %collective-permute-done.23.refs_4_, ...), custom_call_target="tpu_custom_call" | custom-call | flops 786432 | bytes 8388608 | tf_op jit(solution)/shard_map/pallas_call | solution.py:17
  (47 shorter events, 6.3 us)
Async XLA Ops:
  0.6 8.7 %copy-start = (s32[512]{0:T(512)S(1)}, s32[512]{0:T(512)}, u32[]{:S(2)}) copy-start(s32[512]{0:T(512)} %param.6) | copy-start | bytes 6148
  0.6 29.8 %copy-start.1 = (f32[128,1024]{1,0:T(8,128)S(1)}, f32[128,1024]{1,0:T(8,128)}, u32[]{:S(2)}) copy-start(f32[128,1024]{1,0:T(8,128)} %refs_0_.4) | copy-start | bytes 1572868
  0.7 20.8 %collective-permute-start.1 = (f32[128,1024]{1,0:T(8,128)}, f32[128,1024]{1,0:T(8,128)S(1)}, u32[]{:S(2)}, u32[]{:S(2)}) collective-permute-start(f32[128,1024]{1,0:T(8,128)} %refs_0_.4), channel_id=1, source_target_pairs={{0,1},{1,0},{2,3},{3,2},{4,5},{5,4},{6,7},{7,6},{8,9},{9,8},{10,11... | collective-permute-start | bytes 1572872 | tf_op jit(solution)/shard_map/ppermute | solution.py:180
  3.7 19.2 %collective-permute-start = (f32[128,1024]{1,0:T(8,128)}, f32[128,1024]{1,0:T(8,128)S(1)}, u32[]{:S(2)}, u32[]{:S(2)}) collective-permute-start(f32[128,1024]{1,0:T(8,128)} %refs_0_.4), channel_id=1, source_target_pairs={{0,2},{1,3},{2,0},{3,1},{4,6},{5,7},{6,4},{7,5},{8,10},{9,11},{10,... | collective-permute-start | bytes 1572872 | tf_op jit(solution)/shard_map/ppermute | solution.py:180
  5.2 17.6 %collective-permute-start.4 = (f32[64,1024]{1,0:T(8,128)}, f32[64,1024]{1,0:T(8,128)S(1)}, u32[]{:S(2)}, u32[]{:S(2)}) collective-permute-start(f32[64,1024]{1,0:T(8,128)} %refs_0_.5), channel_id=1, source_target_pairs={{0,8},{1,9},{2,10},{3,11},{4,12},{5,13},{6,14},{7,15},{8,0},{9,1},... | collective-permute-start | bytes 786440 | tf_op jit(solution)/shard_map/ppermute | solution.py:180
  6.8 14.0 %collective-permute-start.6 = (f32[64,1024]{1,0:T(8,128)}, f32[64,1024]{1,0:T(8,128)S(1)}, u32[]{:S(2)}, u32[]{:S(2)}) collective-permute-start(f32[64,1024]{1,0:T(8,128)} %refs_0_.5), channel_id=1, source_target_pairs={{0,16},{1,17},{2,18},{3,19},{4,20},{5,21},{6,22},{7,23},{8,24},{9,... | collective-permute-start | bytes 786440 | tf_op jit(solution)/shard_map/ppermute | solution.py:180
  9.3 20.9 %collective-permute-start.11 = (f32[64,1024]{1,0:T(8,128)}, f32[64,1024]{1,0:T(8,128)S(1)}, u32[]{:S(2)}, u32[]{:S(2)}) collective-permute-start(f32[64,1024]{1,0:T(8,128)} %refs_0_.5), channel_id=1, source_target_pairs={{0,4},{1,5},{2,6},{3,7},{4,0},{5,1},{6,2},{7,3},{8,12},{9,13},{10,... | collective-permute-start | bytes 786440 | tf_op jit(solution)/shard_map/ppermute | solution.py:180
  20.8 2.7 %collective-permute-start.8 = (f32[64,1024]{1,0:T(8,128)}, f32[64,1024]{1,0:T(8,128)S(1)}, u32[]{:S(2)}, u32[]{:S(2)}) collective-permute-start(f32[64,1024]{1,0:T(8,128)} %refs_0_.5), channel_id=1, source_target_pairs={{8,16},{9,17},{10,18},{11,19},{12,20},{13,21},{14,22},{15,23},{16,... | collective-permute-start | bytes 786440 | tf_op jit(solution)/shard_map/ppermute | solution.py:180
  21.4 8.3 %collective-permute-start.9 = (f32[64,1024]{1,0:T(8,128)S(1)}, f32[64,1024]{1,0:T(8,128)S(1)}, u32[]{:S(2)}, u32[]{:S(2)}) collective-permute-start(f32[64,1024]{1,0:T(8,128)S(1)} %collective-permute-done.6.refs_4_), channel_id=1, source_target_pairs={{8,0},{9,1},{10,2},{11,3},{12,4},{13,5},{14,6},{15,7},{16,24},{17,... | collective-permute-start | bytes 786440 | tf_op jit(solution)/shard_map/ppermute | solution.py:180
  22.8 9.5 %collective-permute-start.7 = (f32[64,1024]{1,0:T(8,128)S(1)}, f32[64,1024]{1,0:T(8,128)S(1)}, u32[]{:S(2)}, u32[]{:S(2)}) collective-permute-start(f32[64,1024]{1,0:T(8,128)S(1)} %collective-permute-done.6.refs_4_), channel_id=1, source_target_pairs={{0,4},{1,5},{2,6},{3,7},{4,0},{5,1},{6,2},{7,3},{8,12},{9,13},{10,... | collective-permute-start | bytes 786440 | tf_op jit(solution)/shard_map/ppermute | solution.py:180
  22.9 9.4 %collective-permute-start.5 = (f32[64,1024]{1,0:T(8,128)S(1)}, f32[64,1024]{1,0:T(8,128)S(1)}, u32[]{:S(2)}, u32[]{:S(2)}) collective-permute-start(f32[64,1024]{1,0:T(8,128)S(1)} %collective-permute-done.4.refs_3_), channel_id=1, source_target_pairs={{0,4},{1,5},{2,6},{3,7},{4,0},{5,1},{6,2},{7,3},{8,12},{9,13},{10,... | collective-permute-start | bytes 786440 | tf_op jit(solution)/shard_map/ppermute | solution.py:180
  23.4 8.9 %collective-permute-start.2 = (f32[64,1024]{1,0:T(8,128)S(1)}, f32[64,1024]{1,0:T(8,128)S(1)}, u32[]{:S(2)}, u32[]{:S(2)}) collective-permute-start(f32[64,1024]{1,0:T(8,128)S(1)} %slice.45), channel_id=1, source_target_pairs={{0,2},{1,3},{2,0},{3,1},{4,6},{5,7},{6,4},{7,5},{8,10},{9,11},{10,... | collective-permute-start | bytes 786440 | tf_op jit(solution)/shard_map/ppermute | solution.py:180
  29.7 6.4 %collective-permute-start.3 = (f32[64,1024]{1,0:T(8,128)S(1)}, f32[64,1024]{1,0:T(8,128)S(1)}, u32[]{:S(2)}, u32[]{:S(2)}) collective-permute-start(f32[64,1024]{1,0:T(8,128)S(1)} %slice.46), channel_id=1, source_target_pairs={{0,1},{1,0},{2,3},{3,2},{4,5},{5,4},{6,7},{7,6},{8,9},{9,8},{10,11... | collective-permute-start | bytes 786440 | tf_op jit(solution)/shard_map/ppermute | solution.py:180
  30.3 5.8 %collective-permute-start.10 = (f32[64,1024]{1,0:T(8,128)S(1)}, f32[64,1024]{1,0:T(8,128)S(1)}, u32[]{:S(2)}, u32[]{:S(2)}) collective-permute-start(f32[64,1024]{1,0:T(8,128)S(1)} %add.98.refs_5_), channel_id=1, source_target_pairs={{0,4},{1,5},{2,6},{3,7},{4,0},{5,1},{6,2},{7,3},{8,12},{9,13},{10,... | collective-permute-start | bytes 786440 | tf_op jit(solution)/shard_map/ppermute | solution.py:180
  30.4 1.0 %copy-start.2 = (f32[64,1024]{1,0:T(8,128)S(1)}, f32[64,1024]{1,0:T(8,128)}, u32[]{:S(2)}) copy-start(f32[64,1024]{1,0:T(8,128)} %refs_0_.5) | copy-start | bytes 786436
  37.9 6.5 %collective-permute-start.12 = (f32[8,512]{1,0:T(8,128)S(1)}, f32[8,512]{1,0:T(8,128)S(1)}, u32[]{:S(2)}, u32[]{:S(2)}) collective-permute-start(f32[8,512]{1,0:T(8,128)S(1)} %get-tuple-element.38.refs_0_), channel_id=1, source_target_pairs={{0,1},{1,0},{2,3},{3,2},{4,5},{5,4},{6,7},{7,6},{8,9},{9,8},{10,11... | collective-permute-start | bytes 49160 | tf_op jit(solution)/shard_map/ppermute | solution.py:180
  38.5 5.9 %collective-permute-start.13 = (f32[8,512]{1,0:T(8,128)S(1)}, f32[8,512]{1,0:T(8,128)S(1)}, u32[]{:S(2)}, u32[]{:S(2)}) collective-permute-start(f32[8,512]{1,0:T(8,128)S(1)} %get-tuple-element.38.refs_0_), channel_id=1, source_target_pairs={{0,2},{1,3},{2,0},{3,1},{4,6},{5,7},{6,4},{7,5},{8,10},{9,11},{10,... | collective-permute-start | bytes 49160 | tf_op jit(solution)/shard_map/ppermute | solution.py:180
  39.0 5.4 %collective-permute-start.14 = (f32[8,512]{1,0:T(8,128)S(1)}, f32[8,512]{1,0:T(8,128)S(1)}, u32[]{:S(2)}, u32[]{:S(2)}) collective-permute-start(f32[8,512]{1,0:T(8,128)S(1)} %get-tuple-element.38.refs_0_), channel_id=1, source_target_pairs={{0,3},{1,2},{2,1},{3,0},{4,7},{5,6},{6,5},{7,4},{8,11},{9,10},{10,... | collective-permute-start | bytes 49160 | tf_op jit(solution)/shard_map/ppermute | solution.py:180
  47.5 12.7 %collective-permute-start.19 = (f32[192,1024]{1,0:T(8,128)S(1)}, f32[192,1024]{1,0:T(8,128)S(1)}, u32[]{:S(2)}, u32[]{:S(2)}) collective-permute-start(f32[192,1024]{1,0:T(8,128)S(1)} %get-tuple-element.55), channel_id=1, source_target_pairs={{0,4},{1,5},{2,6},{3,7},{4,0},{5,1},{6,2},{7,3},{8,12},{9,13},{10,... | collective-permute-start | bytes 2359304 | tf_op jit(solution)/shard_map/ppermute | solution.py:180
  47.6 2.7 %collective-permute-start.20 = (f32[64,1024]{1,0:T(8,128)S(1)}, f32[64,1024]{1,0:T(8,128)S(1)}, u32[]{:S(2)}, u32[]{:S(2)}) collective-permute-start(f32[64,1024]{1,0:T(8,128)S(1)} %get-tuple-element.57), channel_id=1, source_target_pairs={{0,4},{1,5},{2,6},{3,7},{4,0},{5,1},{6,2},{7,3},{8,12},{9,13},{10,... | collective-permute-start | bytes 786440 | tf_op jit(solution)/shard_map/ppermute | solution.py:180
  48.1 8.3 %collective-permute-start.15 = (f32[64,1024]{1,0:T(8,128)S(1)}, f32[64,1024]{1,0:T(8,128)S(1)}, u32[]{:S(2)}, u32[]{:S(2)}) collective-permute-start(f32[64,1024]{1,0:T(8,128)S(1)} %get-tuple-element.47), channel_id=1, source_target_pairs={{0,1},{1,0},{2,3},{3,2},{4,5},{5,4},{6,7},{7,6},{8,9},{9,8},{10,11... | collective-permute-start | bytes 786440 | tf_op jit(solution)/shard_map/ppermute | solution.py:180
  48.8 8.0 %collective-permute-start.16 = (f32[64,1024]{1,0:T(8,128)S(1)}, f32[64,1024]{1,0:T(8,128)S(1)}, u32[]{:S(2)}, u32[]{:S(2)}) collective-permute-start(f32[64,1024]{1,0:T(8,128)S(1)} %get-tuple-element.48), channel_id=1, source_target_pairs={{0,2},{1,3},{2,0},{3,1},{4,6},{5,7},{6,4},{7,5},{8,10},{9,11},{10,... | collective-permute-start | bytes 786440 | tf_op jit(solution)/shard_map/ppermute | solution.py:180
  51.0 9.1 %collective-permute-start.21 = (f32[64,1024]{1,0:T(8,128)}, f32[64,1024]{1,0:T(8,128)S(1)}, u32[]{:S(2)}, u32[]{:S(2)}) collective-permute-start(f32[64,1024]{1,0:T(8,128)} %add.106), channel_id=1, source_target_pairs={{0,8},{1,9},{2,10},{3,11},{4,12},{5,13},{6,14},{7,15},{24,16},{25,... | collective-permute-start | bytes 786440 | tf_op jit(solution)/shard_map/ppermute | solution.py:180
  53.7 19.5 %collective-permute-start.23 = (f32[64,1024]{1,0:T(8,128)}, f32[64,1024]{1,0:T(8,128)S(1)}, u32[]{:S(2)}, u32[]{:S(2)}) collective-permute-start(f32[64,1024]{1,0:T(8,128)} %add.106), channel_id=1, source_target_pairs={{8,16},{9,17},{10,18},{11,19},{12,20},{13,21},{14,22},{15,23},{16,... | collective-permute-start | bytes 786440 | tf_op jit(solution)/shard_map/ppermute | solution.py:180
  58.1 13.0 %collective-permute-start.17 = (f32[128,1024]{1,0:T(8,128)}, f32[128,1024]{1,0:T(8,128)S(1)}, u32[]{:S(2)}, u32[]{:S(2)}) collective-permute-start(f32[128,1024]{1,0:T(8,128)} %get-tuple-element.50), channel_id=1, source_target_pairs={{0,1},{1,0},{2,3},{3,2},{4,5},{5,4},{6,7},{7,6},{8,9},{9,8},{10,11... | collective-permute-start | bytes 1572872 | tf_op jit(solution)/shard_map/ppermute | solution.py:180
  59.4 12.7 %collective-permute-start.18 = (f32[128,1024]{1,0:T(8,128)}, f32[128,1024]{1,0:T(8,128)S(1)}, u32[]{:S(2)}, u32[]{:S(2)}) collective-permute-start(f32[128,1024]{1,0:T(8,128)} %get-tuple-element.51), channel_id=1, source_target_pairs={{0,2},{1,3},{2,0},{3,1},{4,6},{5,7},{6,4},{7,5},{8,10},{9,11},{10,... | collective-permute-start | bytes 1572872 | tf_op jit(solution)/shard_map/ppermute | solution.py:180
  60.2 17.1 %copy-start.3 = (f32[64,1024]{1,0:T(8,128)S(1)}, f32[64,1024]{1,0:T(8,128)}, u32[]{:S(2)}) copy-start(f32[64,1024]{1,0:T(8,128)} %refs_0_.5) | copy-start | bytes 786436
  61.1 12.4 %collective-permute-start.22 = (f32[64,1024]{1,0:T(8,128)}, f32[64,1024]{1,0:T(8,128)S(1)}, u32[]{:S(2)}, u32[]{:S(2)}) collective-permute-start(f32[64,1024]{1,0:T(8,128)} %get-tuple-element.58), channel_id=1, source_target_pairs={{0,8},{1,9},{2,10},{3,11},{4,12},{5,13},{6,14},{7,15},{8,0},{9,1},... | collective-permute-start | bytes 786440 | tf_op jit(solution)/shard_map/ppermute | solution.py:180
  63.2 14.1 %collective-permute-start.24 = (f32[64,1024]{1,0:T(8,128)}, f32[64,1024]{1,0:T(8,128)}, u32[]{:S(2)}, u32[]{:S(2)}) collective-permute-start(f32[64,1024]{1,0:T(8,128)} %get-tuple-element.61), channel_id=1, source_target_pairs={{0,16},{1,17},{2,18},{3,19},{4,20},{5,21},{6,22},{7,23},{8,24},{9,... | collective-permute-start | bytes 786440 | tf_op jit(solution)/shard_map/ppermute | solution.py:180

commit v3 on v2

v3 whole, which is shorter than its diff:
```python
import functools

import jax
import jax.numpy as jnp
from jax import lax
from jax.experimental import pallas as pl
from jax.experimental.pallas import tpu as pltpu
from jax.sharding import PartitionSpec as P

inv_temp = 20.0
f32 = jnp.float32
bf16 = jnp.bfloat16
AXES = ("pb", "pa")


def call(kernel, outs, flops, *args, kept=True):
    return pl.pallas_call(
        kernel,
        out_shape=[pltpu.VMEM(s, d) if kept else jax.ShapeDtypeStruct(s, d) for s, d in outs],
        compiler_params=pltpu.CompilerParams(vmem_limit_bytes=24 * 1024 * 1024),
        cost_estimate=pl.CostEstimate(flops=flops, bytes_accessed=8 << 20, transcendentals=0),
    )(*args)


def split(x):
    hi = x.astype(bf16)
    return hi, (x - hi.astype(f32)).astype(bf16)


def mm(a, b, dims):
    return lax.dot_general(a, b, (dims, ((), ())), preferred_element_type=f32)


def mm3(a, b, dims):
    (ah, al), (bh, bl) = a, b
    n = ah.shape[0]
    if n > 256:
        return mm(al, bh, dims) + mm(ah, bl, dims) + mm(ah, bh, dims)
    both = mm(jnp.concatenate([al, ah], axis=0), bh, dims)
    return both[:n] + mm(ah, bl, dims) + both[n:]


def lift(scale):
    return jnp.broadcast_to(scale, (scale.shape[0], 128))


def normalize(rows):
    scale = lax.rsqrt(jnp.sum(rows * rows, axis=1, keepdims=True) + 1e-06)
    return rows * scale, scale


def onehot(pos, shape, first):
    return lax.broadcasted_iota(jnp.int32, shape, 0) + first == pos


def combine(stats):
    n = stats[0].shape[1] // len(stats)
    blocks = [sum(r[:, (m ^ k) * n : (m ^ k) * n + n] for k, r in enumerate(stats)) for m in range(len(stats))]
    return jnp.concatenate(blocks, axis=1)


def load(parts, hi, lo):
    at = 0
    for r in parts:
        if isinstance(r, tuple):
            n = r[0].shape[0]
            hi[at : at + n], lo[at : at + n] = r[0][...], r[1][...]
        else:
            n = r.shape[0]
            hi[at : at + n], lo[at : at + n] = split(normalize(r[...])[0])
        at += n


def own_kernel(queries, passages, qn, qs, qh, ql, pn, ps, ph, pl_):
    for rows, xn, scale, hi, lo in ((queries, qn, qs, qh, ql), (passages, pn, ps, ph, pl_)):
        x, r = normalize(rows[...])
        xn[...] = x
        scale[...] = lift(r)
        hi[...], lo[...] = split(x)


def product(p, q):
    return inv_temp * mm3((p[0][...], p[1][...]), (q[0][...], q[1][...]), ((1,), (1,)))


def positives(pos, ph, pl_, first):
    o = onehot(pos[...], (ph.shape[0], pos.shape[1]), first).astype(f32).T.astype(bf16)
    return mm(o, pl_[...], ((1,), (0,))) + mm(o, ph[...], ((1,), (0,)))


def first_scores_kernel(*refs):
    qh0, ql0, ph0, pl0, x, y, *ps, pos, et, stats, qh, ql, ph, pl_, v = refs
    load([(qh0, ql0), x, y], qh, ql)
    load([(ph0, pl0), *ps], ph, pl_)
    st = product((ph, pl_), (qh, ql))
    write_stats(stats, et, st, pos[:, : st.shape[1]], 0)
    v[...] = positives(pos, ph, pl_, 0)


def all_scores_kernel(q, p, pos, et, stats, qh, ql, ph, pl_):
    load([q], qh, ql)
    load([p], ph, pl_)
    write_stats(stats, et, product((ph, pl_), (qh, ql)), pos[...], 0)


def write_stats(stats, et, st, pos, first):
    e = jnp.exp(st)
    et[...] = e
    stats[...] = jnp.zeros(stats.shape, f32)
    stats[0:1] = jnp.sum(e, axis=0, keepdims=True)
    stats[1:2] = jnp.sum(jnp.where(onehot(pos, st.shape, first), st, 0.0), axis=0, keepdims=True)


def rest_scores_kernel(n_q, n_p, *refs):
    qs, ps = refs[:n_q], refs[n_q : n_q + n_p]
    pos, et1, stats1, qh1, ql1, ph1, pl1, v1, et, stats, qh, ql, ph, pl_ = refs[n_q + n_p :]
    n, m = qh1.shape[0], ph1.shape[0]
    del v1
    qh[:n] = qh1[...]
    ql[:n] = ql1[...]
    load(qs, qh.at[n:], ql.at[n:])
    load(ps, ph, pl_)
    top = product((ph1, pl1), (qh.at[n:], ql.at[n:]))
    low = product((ph, pl_), (qh, ql))
    e_top, e_low = jnp.exp(top), jnp.exp(low)
    et[:m, :n] = et1[...]
    et[:m, n:] = e_top
    et[m:, :] = e_low
    o_top, o_low = onehot(pos[:, n:], top.shape, 0), onehot(pos[...], low.shape, m)
    sum_low = jnp.sum(e_low, axis=0, keepdims=True)
    pos_low = jnp.sum(jnp.where(o_low, low, 0.0), axis=0, keepdims=True)
    stats[...] = jnp.zeros(stats.shape, f32)
    stats[0:1, :n] = stats1[0:1] + sum_low[:, :n]
    stats[1:2, :n] = stats1[1:2] + pos_low[:, :n]
    stats[0:1, n:] = jnp.sum(e_top, axis=0, keepdims=True) + sum_low[:, n:]
    stats[1:2, n:] = jnp.sum(jnp.where(o_top, top, 0.0), axis=0, keepdims=True) + pos_low[:, n:]


def unscaled_kernel(n_p, et, pos, *refs):
    ps, v1, (u, v) = refs[: 2 * n_p], refs[2 * n_p : -2], refs[-2:]
    at = 0
    for ph, pl_ in zip(ps[:n_p], ps[n_p:]):
        n = ph.shape[0]
        part_u = mm3(split(et[at : at + n].T), (ph[...], pl_[...]), ((1,), (0,)))
        u[...] = part_u if at == 0 else u[...] + part_u
        at += n
    v[...] = positives(pos, ph, pl_, at - n) + (v1[0][...] if v1 else 0.0)


def query_kernel(n_stats, cuts, *refs):
    stats = refs[:n_stats]
    u, v, losses, *outs = refs[n_stats:]
    both = combine(stats)
    losses[...] = jnp.log(both[0:1]) - both[1:2]
    inv = (1.0 / both).T[:, 0:1]
    for out, ranges in zip(outs, cuts):
        at = 0
        for a, b in ranges:
            out[at : at + b - a] = u[a:b] * inv[a:b] - v[a:b]
            at += b - a


def passage_kernel(n_stats, cuts, *refs):
    stats = refs[:n_stats]
    et, pos, qh, ql, *outs = refs[n_stats:]
    weight = 1.0 / combine(stats)[0:1]
    d = et[...] * weight - onehot(pos[...], et.shape, 0).astype(f32)
    g = mm3(split(d), (qh[...], ql[...]), ((1,), (0,)))
    at = 0
    for out, n in zip(outs, cuts):
        out[...] = g[at : at + n]
        at += n


def core_sum_kernel(g, tc, g3, t1, t2, t3):
    n = g3.shape[0]
    t1[...] = g[n : 2 * n] + tc[n : 2 * n]
    t2[...] = g[2 * n :] + tc[2 * n : 3 * n]
    t3[...] = g3[...] + tc[3 * n :]


def add_kernel(a, b, out):
    out[...] = a[...] + b[...]


def cross_kernel(gx, gy, x1, y1, x, y):
    n = gx.shape[0]
    h = (n + x1.shape[0]) // 3
    x[: n - h] = gx[: n - h]
    x[n - h :] = gx[n - h :] + y1[:h]
    y[:h] = gy[:h] + x1[:h]
    y[h:] = gy[h:]


def project(g, xn, scale):
    g = inv_temp * g
    return scale * (g - xn * jnp.sum(xn * g, axis=1, keepdims=True))


def last_kernel(qn, qs, pn, ps, own, x1, y1, x2, y2, g, tc, r1, rmid, r2, out_q, out_p):
    h, m = qn.shape[0] // 2, pn.shape[0]
    k = x1.shape[0] - h
    for at, n, p, pa, q, qa in ((0, k, x1, h, y2, 0), (k, h - k, x2, 0, y2, k), (h, k, y1, h, x2, h - k), (h + k, h - k, y2, h, x2, h)):
        if n:
            s = own[at : at + n] + p[pa : pa + n] + q[qa : qa + n]
            out_q[at : at + n] = project(s, qn[at : at + n], qs[at : at + n, 0:1])
    out_p[...] = project(g[:m] + tc[:m] + r1[...] + rmid[...] + r2[...], pn[...], ps[:, 0:1])


def final_kernel(rows, g, out):
    xn, scale = normalize(rows[...])
    out[...] = project(g[...], xn, scale)


def flip(x, mask, only=None):
    n = lax.axis_size("pb") * lax.axis_size("pa")
    pairs = [(i, i ^ mask) for i in range(n) if only is None or only(i)]
    return lax.ppermute(x, AXES, pairs)


X, Y, C, Z1, Z2, Z3 = 1, 2, 4, 8, 16, 24
EARLY = 2


def middle(i):
    return (i // 8) in (1, 2)


def ends(i):
    return not middle(i)


def rows_of(x, *cuts):
    at, out = 0, []
    for n in cuts:
        out.append(lax.slice_in_dim(x, at, at + n, axis=0))
        at += n
    return out


def after(x, *others):
    return lax.optimization_barrier((x,) + others)[0]


def by_xor(x, k):
    x = jnp.where(k & 1, jnp.stack([x[1], x[0], x[3], x[2]]), x)
    return jnp.where(k & 2, jnp.stack([x[2], x[3], x[0], x[1]]), x)


def small_body(queries, passages, positive):
    qr, pr = queries.shape[0], passages.shape[0]
    h = qr // 2
    p_rows = 8 * pr
    pa, pb = lax.axis_index("pa"), lax.axis_index("pb")

    pos = by_xor(positive.reshape(4, qr), pa).reshape(1, 4 * qr)
    block = ((pos % p_rows) // pr) ^ pb
    place = jnp.where(block == 6, 7, block // 2 + 3 * (block % 2))
    pos = jnp.where(pos // p_rows == pa, place * pr + pos % pr, -1)

    z2, z1 = flip(passages, Z2), flip(passages, Z1)
    x, y = flip(queries, X), flip(queries, Y)
    c0 = flip(passages, C)
    qn, qs, qh0, ql0, pn, ps, ph0, pl0 = own_rows(queries, passages)
    z2 = after(z2, qh0, pos)
    far = flip(z2, Z1, middle)
    mid = flip(after(passages, z2), Z3, middle)
    da, db = flip(after(x[:h], c0), Y), flip(after(y[h:], c0), X)
    c1 = flip(after(z1, qh0, pos), C)
    c2 = flip(after(z2, c1), C)
    first = first_scores((qh0, ql0, ph0, pl0, x, y, z1, z2, c0), pos)
    z3 = mid + far
    c3 = flip(z3, C)

    et, stats, qh, ql, ph2, pl2 = rest_scores([da, db], [c1, c2, c3, z3], pos, first)
    ph1, pl1, v1 = first[4:]
    both = [stats, flip(stats, X), flip(stats, Y), flip(stats, X + Y)]
    u, v = unscaled(et, pos, (ph1, ph2), (pl1, pl2), (v1,))

    def part(k, n):
        return (k * n, k * n + n)

    g, gc, g3 = passage_grads(both, after(et, u), pos, qh, ql, (3 * pr, 4 * pr, pr))
    tc = flip(gc, C)
    k = EARLY * h // 4
    kx, ky = 2 * h + k, 5 * h + k
    cuts = ((part(6, h), (2 * h, kx)), (part(7, h), (5 * h, ky)), ((kx, 4 * h),), (part(4, h), (ky, 6 * h)), ((0, qr),))
    losses, gx1, gy1, gx, gy, own = query_grads(both, after(u, gc), v, cuts)
    x1, y1 = flip(gx1, X), flip(gy1, Y)
    t1, t2, t3 = core_sums(g, tc, g3)
    ff = flip(t3, Z1, ends)
    rmid = flip(t3, Z3, middle)
    t2 = add(t2, ff)
    r1, r2 = flip(after(t1, t2, rmid), Z1), flip(t2, Z2)
    gx, gy = cross(after(gx, t2), gy, x1, y1)
    x2, y2 = flip(gx, X), flip(gy, Y)

    losses = by_xor(losses.reshape(4, qr), pa).reshape(4 * qr)
    query_grad, passage_grad = call(
        last_kernel,
        [(queries.shape, f32), (passages.shape, f32)],
        12 * queries.size,
        *(qn, qs, pn, ps, own, x1, y1, x2, y2, g, tc, r1, rmid, r2),
        kept=False,
    )
    return losses, query_grad, passage_grad


def rows(parts):
    return sum(x.shape[0] for x in parts)


def own_rows(queries, passages):
    outs = []
    for n, d in (queries.shape, passages.shape):
        outs += [((n, d), f32), ((n, 128), f32), ((n, d), bf16), ((n, d), bf16)]
    return call(own_kernel, outs, 4 * queries.size, queries, passages)


def scores_outs(q, p, d):
    return [((p, q), f32), ((8, q), f32), ((q, d), bf16), ((q, d), bf16), ((p, d), bf16), ((p, d), bf16)]


def first_scores(parts, pos):
    qh0, _, ph0, _, x, y, *ps = parts
    q, p, d = rows([qh0, x, y]), rows([ph0] + ps), x.shape[1]
    return call(
        first_scores_kernel, scores_outs(q, p, d) + [((pos.shape[1], d), f32)], 10 * q * p * d, *parts, pos
    )


def all_scores(q, p, pos):
    work = 6 * q.size * p.shape[0]
    return call(all_scores_kernel, scores_outs(q.shape[0], p.shape[0], q.shape[1]), work, q, p, pos)


def rest_scores(q_parts, p_parts, pos, first):
    p1, q1 = first[0].shape
    q, p, d = q1 + rows(q_parts), rows(p_parts), q_parts[0].shape[1]
    return call(
        functools.partial(rest_scores_kernel, len(q_parts), len(p_parts)),
        [((p1 + p, q), f32)] + scores_outs(q, p, d)[1:],
        6 * q * p * d,
        *q_parts,
        *p_parts,
        pos,
        *first,
    )


def unscaled(et, pos, hi, lo, v=()):
    p, q = et.shape
    d = hi[0].shape[1]
    kernel = functools.partial(unscaled_kernel, len(hi))
    return call(kernel, [((q, d), f32)] * 2, 8 * q * p * d, et, pos, *hi, *lo, *v)


def query_grads(both, u, v, cuts):
    q, d = u.shape
    return call(
        functools.partial(query_kernel, len(both), cuts),
        [((1, q), f32)] + [((sum(b - a for a, b in ranges), d), f32) for ranges in cuts],
        3 * q * d,
        *both,
        u,
        v,
    )


def passage_grads(both, et, pos, qh, ql, cuts):
    q, d = qh.shape
    return call(
        functools.partial(passage_kernel, len(both), cuts),
        [((n, d), f32) for n in cuts],
        6 * q * d * sum(cuts),
        *both,
        et,
        pos,
        qh,
        ql,
    )


def add(a, b):
    return call(add_kernel, [(a.shape, f32)], a.size, a, b)[0]


def core_sums(g, tc, g3):
    return call(core_sum_kernel, [(g3.shape, f32)] * 3, 3 * g3.size, g, tc, g3)


def cross(gx, gy, x1, y1):
    return call(cross_kernel, [(gx.shape, f32)] * 2, 2 * gx.size, gx, gy, x1, y1)


def finish(rows, g):
    return call(final_kernel, [(rows.shape, f32)], 12 * rows.size, rows, g, kept=False)[0]


def body(queries, passages, positive):
    pa = lax.axis_index("pa")
    q_full = lax.all_gather(queries, "pa", axis=0, tiled=True)
    p_full = lax.all_gather(passages, "pb", axis=0, tiled=True)
    p_rows, q_rows = p_full.shape[0], q_full.shape[0]
    pos = positive - pa * p_rows
    pos = jnp.where((pos >= 0) & (pos < p_rows), pos, -1).reshape(1, -1)
    et, stats, qh, ql, ph, pl_ = all_scores(q_full, p_full, pos)
    both = [lax.psum(stats, "pa")]
    u, v = unscaled(et, pos, [ph], [pl_])
    losses, gq = query_grads(both, u, v, (((0, q_rows),),))
    (gp,) = passage_grads(both, et, pos, qh, ql, (p_rows,))
    q_part = lax.psum_scatter(gq, "pa", scatter_dimension=0, tiled=True)
    p_part = lax.psum_scatter(gp, "pb", scatter_dimension=0, tiled=True)
    return losses.reshape(-1), finish(queries, q_part), finish(passages, p_part)


def solution(mesh):
    placed = (P(("pb", "pa"), None), P(("pa", "pb"), None), P("pb"))
    small = mesh.shape["pa"] == 4 and mesh.shape["pb"] == 8
    return jax.shard_map(
        small_body if small else body,
        mesh=mesh,
        in_specs=placed,
        out_specs=(P("pb"), P(("pb", "pa"), None), P(("pa", "pb"), None)),
        check_vma=False,
    )
```

time: 79.4 us -> 73.2 us (0.922)
  waiting for transfers between devices: 33.7 us -> 26.6 us
  starting transfers between devices: 27.1 us -> 30.7 us
  Pallas kernels: 12.9 us -> 9.73 us
    ppermute x25 -> x24, waiting for transfers between devices: 33.7 us -> 26.6 us  [flip(): return lax.ppermute(x, AXES, pairs)]
    ppermute x25 -> x24, starting transfers between devices: 27.1 us -> 30.7 us  [flip(): return lax.ppermute(x, AXES, pairs)]
    pallas_call x8 -> x10, Pallas kernels: 12.9 us -> 9.73 us  [call(): pl.pallas_call(kernel, out_shape=[pltpu.VMEM(s, d) if kept else jax.Shape...]
    select_n x2 -> x4, other arithmetic: 0.03 us -> 2.03 us  [the longest x1 0.73 us: small_body(): pos = jnp.where(pos // p_rows == pa, place * pr + pos % pr, -1)]
    gather x2 -> x0, local copies, waits for them, and re-layouts: 1.69 us -> none  [the longest x1 1.13 us: small_body(): losses = losses.reshape(4, qr)[order].reshape(4 * qr)]
    add x2 -> x0, other arithmetic: 1.68 us -> none  [the longest x1 0.95 us: small_body(): r2 = flip(gz[2 * pr:] + tc[2 * pr:] + ff, Z2)]
    unnamed x8 -> x4, local copies, waits for them, and re-layouts: 0.96 us -> 1.99 us
    slice x2 -> x6, local copies, waits for them, and re-layouts: 0.04 us -> 0.88 us  [the longest x2 0.84 us: by_xor(): x = jnp.where(k & 1, jnp.stack([x[1], x[0], x[3], x[2]]), x)]
  transfers between devices with their start and end apart: 25 -> 24, of which waited for: 9 -> 8; matrix products, arithmetic and copies ran while one was open for 4% -> 4% of each run, Pallas kernels for 8% -> 7%
where the time goes in v3:
time: 73.2 us; the launch traced here: 72.8 us
  starting transfers between devices  30.7 us (42%)
  waiting for transfers between devices  26.6 us (36%)
  Pallas kernels  9.73 us (13%)
  local copies, waits for them, and re-layouts  2.87 us (4%)
  other arithmetic  2.07 us (3%)
  between operations  0.83 us (1%)
    ppermute x24, starting transfers between devices, flip(): return lax.ppermute(x, AXES, pairs)  30.7 us
    ppermute x24, waiting for transfers between devices, flip(): return lax.ppermute(x, AXES, pairs)  26.6 us
    pallas_call x10, Pallas kernels, call(): pl.pallas_call(kernel, out_shape=[pltpu.VMEM(s, d) if kept else jax.Shape...  9.73 us
    unnamed x4, local copies, waits for them, and re-layouts  1.99 us
  transfers between devices with their start and end apart: 24, of which 8 were waited for; matrix products, arithmetic and copies ran while one was open for 4% of the time, Pallas kernels for 7%

profile of v3, /device:TPU:0, one launch (start us, length us, event | category | flops | bytes accessed | tf_op | source)
XLA Modules:
  0.0 72.8 jit_solution(12250725261374960303)
XLA Ops:
  0.6 3.1 %collective-permute-start.5 = (f32[64,1024]{1,0:T(8,128)}, f32[64,1024]{1,0:T(8,128)S(1)}, u32[]{:S(2)}, u32[]{:S(2)}) collective-permute-start(f32[64,1024]{1,0:T(8,128)} %passages.1), channel_id=1, source_target_pairs={{0,8},{1,9},{2,10},{3,11},{4,12},{5,13},{6,14},{7,15},{8,0},{9,1},... | collective-permute-start | bytes 786440 | tf_op jit(solution)/shard_map/ppermute | solution.py:218
  3.7 2.6 %collective-permute-start.7 = (f32[64,1024]{1,0:T(8,128)}, f32[64,1024]{1,0:T(8,128)S(1)}, u32[]{:S(2)}, u32[]{:S(2)}) collective-permute-start(f32[64,1024]{1,0:T(8,128)} %passages.1), channel_id=1, source_target_pairs={{0,16},{1,17},{2,18},{3,19},{4,20},{5,21},{6,22},{7,23},{8,24},{9,... | collective-permute-start | bytes 786440 | tf_op jit(solution)/shard_map/ppermute | solution.py:218
  6.3 1.5 %collective-permute-start = (f32[128,1024]{1,0:T(8,128)}, f32[128,1024]{1,0:T(8,128)S(1)}, u32[]{:S(2)}, u32[]{:S(2)}) collective-permute-start(f32[128,1024]{1,0:T(8,128)} %queries.1), channel_id=1, source_target_pairs={{0,1},{1,0},{2,3},{3,2},{4,5},{5,4},{6,7},{7,6},{8,9},{9,8},{10,11... | collective-permute-start | bytes 1572872 | tf_op jit(solution)/shard_map/ppermute | solution.py:218
  7.8 1.5 %collective-permute-start.3 = (f32[128,1024]{1,0:T(8,128)}, f32[128,1024]{1,0:T(8,128)S(1)}, u32[]{:S(2)}, u32[]{:S(2)}) collective-permute-start(f32[128,1024]{1,0:T(8,128)} %queries.1), channel_id=1, source_target_pairs={{0,2},{1,3},{2,0},{3,1},{4,6},{5,7},{6,4},{7,5},{8,10},{9,11},{10,... | collective-permute-start | bytes 1572872 | tf_op jit(solution)/shard_map/ppermute | solution.py:218
  9.3 0.8 %slice_bitcast_fusion.3 = (s32[1,128]{1,0:T(1,128)S(1)}, s32[1,128]{1,0:T(1,128)S(1)}, s32[1,128]{1,0:T(1,128)S(1)}, s32[1,128]{1,0:T(1,128)S(1)}) fusion(s32[512]{0:T(512)} %param.5), kind=kLoop, calls=%fused_computation.46 | loop fusion | bytes 4096 | tf_op jit(solution)/shard_map/slice | solution.py:246
  10.2 0.7 bitcast_select_fusion.2
  10.9 0.7 %fusion.7 = s32[512]{0:T(512)S(1)} fusion(s32[512]{0:T(512)} %param.5, s32[2,128]{1,0:T(2,128)S(1)} %get-tuple-element.108, s32[2,128]{1,0:T(2,128)S(1)} %get-tuple-element.107, s32[]{:T(128)S(6)} %axis_index.25, s32[]{:T(128)S(6)} %axis_index.22, pred[]{:T(512)S(6)} %ne.67, pred[]{:T(512)S(6)} %ne.66, s32[1,128]{1,0:T(1,128)S(1)} %get-tuple-element.110, ...), kind=kLoop, calls=%fused_computation.23 | loop fusion | flops 38912 | bytes 8202 | tf_op jit(solution)/shard_map/jit(_where)/select_n | solution.py:259
  11.6 1.0 %copy-done = f32[128,1024]{1,0:T(8,128)S(1)} copy-done((f32[128,1024]{1,0:T(8,128)S(1)}, f32[128,1024]{1,0:T(8,128)}, u32[]{:S(2)}) %copy-start) | copy-done | bytes 524312
  12.6 0.9 %copy-done.1 = f32[64,1024]{1,0:T(8,128)S(1)} copy-done((f32[64,1024]{1,0:T(8,128)S(1)}, f32[64,1024]{1,0:T(8,128)}, u32[]{:S(2)}) %copy-start.1) | copy-done | bytes 262168
  13.8 5.4 %collective-permute-done.7.refs_7_ = f32[64,1024]{1,0:T(8,128)S(1)} collective-permute-done((f32[64,1024]{1,0:T(8,128)}, f32[64,1024]{1,0:T(8,128)S(1)}, u32[]{:S(2)}, u32[]{:S(2)}) %collective-permute-start.7) | collective-permute-done | bytes 262176 | tf_op jit(solution)/shard_map/ppermute | solution.py:218
  19.2 0.7 collective-permute-start.9
  19.9 0.7 collective-permute-done.refs_4_
  20.6 1.3 %collective-permute-start.10 = (f32[64,1024]{1,0:T(8,128)S(1)}, f32[64,1024]{1,0:T(8,128)S(1)}, u32[]{:S(2)}, u32[]{:S(2)}) collective-permute-start(f32[64,1024]{1,0:T(8,128)S(1)} %collective-permute-done.7.refs_7_), channel_id=1, source_target_pairs={{8,0},{9,1},{10,2},{11,3},{12,4},{13,5},{14,6},{15,7},{16,24},{17,... | collective-permute-start | bytes 786440 | tf_op jit(solution)/shard_map/ppermute | solution.py:218
  21.9 1.6 %collective-permute-start.2 = (f32[64,1024]{1,0:T(8,128)S(1)}, f32[64,1024]{1,0:T(8,128)S(1)}, u32[]{:S(2)}, u32[]{:S(2)}) collective-permute-start(f32[64,1024]{1,0:T(8,128)S(1)} %slice.84), channel_id=1, source_target_pairs={{0,2},{1,3},{2,0},{3,1},{4,6},{5,7},{6,4},{7,5},{8,10},{9,11},{10,... | collective-permute-start | bytes 786440 | tf_op jit(solution)/shard_map/ppermute | solution.py:218
  23.5 1.6 %collective-permute-start.4 = (f32[64,1024]{1,0:T(8,128)S(1)}, f32[64,1024]{1,0:T(8,128)S(1)}, u32[]{:S(2)}, u32[]{:S(2)}) collective-permute-start(f32[64,1024]{1,0:T(8,128)S(1)} %slice.85), channel_id=1, source_target_pairs={{0,1},{1,0},{2,3},{3,2},{4,5},{5,4},{6,7},{7,6},{8,9},{9,8},{10,11... | collective-permute-start | bytes 786440 | tf_op jit(solution)/shard_map/ppermute | solution.py:218
  25.1 5.4 %collective-permute-done.10 = f32[64,1024]{1,0:T(8,128)S(1)} collective-permute-done((f32[64,1024]{1,0:T(8,128)S(1)}, f32[64,1024]{1,0:T(8,128)S(1)}, u32[]{:S(2)}, u32[]{:S(2)}) %collective-permute-start.10) | collective-permute-done | bytes 262176 | tf_op jit(solution)/shard_map/ppermute | solution.py:218
  30.6 1.8 %shard_map.59 = (f32[256,384]{1,0:T(8,128)S(1)}, f32[8,384]{1,0:T(8,128)S(1)}, bf16[384,1024]{1,0:T(8,128)(2,1)S(1)}, bf16[384,1024]{1,0:T(8,128)(2,1)S(1)}, bf1...) custom-call(bf16[128,1024]{1,0:T(8,128)(2,1)S(1)} %get-tuple-element.54.refs_0_, ...), custom_call_target="tpu_custom_call" | custom-call | flops 1006632960 | bytes 8388608 | tf_op jit(solution)/shard_map/pallas_call | solution.py:17
  32.5 1.7 %shard_map.60 = (f32[512,512]{1,0:T(8,128)S(1)}, f32[8,512]{1,0:T(8,128)S(1)}, bf16[512,1024]{1,0:T(8,128)(2,1)S(1)}, bf16[512,1024]{1,0:T(8,128)(2,1)S(1)}, bf1...) custom-call(f32[64,1024]{1,0:T(8,128)S(1)} %collective-permute-done.2.refs_0_, ...), custom_call_target="tpu_custom_call" | custom-call | flops 805306368 | bytes 8388608 | tf_op jit(solution)/shard_map/pallas_call | solution.py:17
  34.2 2.5 %collective-permute-start.14 = (f32[8,512]{1,0:T(8,128)S(1)}, f32[8,512]{1,0:T(8,128)S(1)}, u32[]{:S(2)}, u32[]{:S(2)}) collective-permute-start(f32[8,512]{1,0:T(8,128)S(1)} %get-tuple-element.69.refs_0_), channel_id=1, source_target_pairs={{0,3},{1,2},{2,1},{3,0},{4,7},{5,6},{6,5},{7,4},{8,11},{9,10},{10,... | collective-permute-start | bytes 49160 | tf_op jit(solution)/shard_map/ppermute | solution.py:218
  37.7 2.4 %shard_map.61 = (f32[512,1024]{1,0:T(8,128)S(1)}, f32[512,1024]{1,0:T(8,128)S(1)}) custom-call(f32[512,512]{1,0:T(8,128)S(1)} %get-tuple-element.74.et.refs_4_, s32[1,512]{1,0:T(1,128)S(1)} %bitcast.37, bf16[256,1024]{1,0:T(8,128)(2,1)S(1)} %get-tuple-element.66.refs_11_.refs_0_, bf16[256,1024]{1,0:T(8,128)(2,1)S(1)} %get-tuple-element.71.refs_1_, ...), custom_call_target="tpu_custom_call" | custom-call | flops 2147483648 | bytes 8388608 | tf_op jit(solution)/shard_map/pallas_call | solution.py:17
  40.9 1.8 %shard_map.62 = (f32[192,1024]{1,0:T(8,128)S(1)}, f32[256,1024]{1,0:T(8,128)S(1)}, f32[64,1024]{1,0:T(8,128)S(1)}) custom-call(f32[8,512]{1,0:T(8,128)S(1)} %get-tuple-element.69.refs_0_, f32[8,512]{1,0:T(8,128)S(1)} %collective-permute-done.12.refs_1_, f32[8,512]{1,0:T(8,128)S(1)} %collective-permute-done.13.refs_2_, ...), custom_call_target="tpu_custom_call" | custom-call | flops 1610612736 | bytes 8388608 | tf_op jit(solution)/shard_map/pallas_call | solution.py:17
  43.2 0.8 %collective-permute-start.15 = (f32[96,1024]{1,0:T(8,128)S(1)}, f32[96,1024]{1,0:T(8,128)S(1)}, u32[]{:S(2)}, u32[]{:S(2)}) collective-permute-start(f32[96,1024]{1,0:T(8,128)S(1)} %get-tuple-element.86), channel_id=1, source_target_pairs={{0,1},{1,0},{2,3},{3,2},{4,5},{5,4},{6,7},{7,6},{8,9},{9,8},{10,11... | collective-permute-start | bytes 1179656 | tf_op jit(solution)/shard_map/ppermute | solution.py:218
  44.0 1.5 %collective-permute-start.16 = (f32[96,1024]{1,0:T(8,128)S(1)}, f32[96,1024]{1,0:T(8,128)S(1)}, u32[]{:S(2)}, u32[]{:S(2)}) collective-permute-start(f32[96,1024]{1,0:T(8,128)S(1)} %get-tuple-element.87), channel_id=1, source_target_pairs={{0,2},{1,3},{2,0},{3,1},{4,6},{5,7},{6,4},{7,5},{8,10},{9,11},{10,... | collective-permute-start | bytes 1179656 | tf_op jit(solution)/shard_map/ppermute | solution.py:218
  45.6 0.7 collective-permute-start.21
  46.3 5.9 %collective-permute-start.18 = (f32[64,1024]{1,0:T(8,128)S(1)}, f32[64,1024]{1,0:T(8,128)S(1)}, u32[]{:S(2)}, u32[]{:S(2)}) collective-permute-start(f32[64,1024]{1,0:T(8,128)S(1)} %get-tuple-element.92), channel_id=1, source_target_pairs={{0,8},{1,9},{2,10},{3,11},{4,12},{5,13},{6,14},{7,15},{24,16},{25,... | collective-permute-start | bytes 786440 | tf_op jit(solution)/shard_map/ppermute | solution.py:218
  52.2 5.5 %collective-permute-done.18.b = f32[64,1024]{1,0:T(8,128)S(1)} collective-permute-done((f32[64,1024]{1,0:T(8,128)S(1)}, f32[64,1024]{1,0:T(8,128)S(1)}, u32[]{:S(2)}, u32[]{:S(2)}) %collective-permute-start.18) | collective-permute-done | bytes 262176 | tf_op jit(solution)/shard_map/ppermute | solution.py:218
  57.8 2.4 %collective-permute-start.23 = (f32[64,1024]{1,0:T(8,128)S(1)}, f32[64,1024]{1,0:T(8,128)S(1)}, u32[]{:S(2)}, u32[]{:S(2)}) collective-permute-start(f32[64,1024]{1,0:T(8,128)S(1)} %shard_map.65), channel_id=1, source_target_pairs={{0,16},{1,17},{2,18},{3,19},{4,20},{5,21},{6,22},{7,23},{8,24},{9,... | collective-permute-start | bytes 786440 | tf_op jit(solution)/shard_map/ppermute | solution.py:218
  60.5 0.8 %collective-permute-start.19 = (f32[96,1024]{1,0:T(8,128)S(1)}, f32[96,1024]{1,0:T(8,128)S(1)}, u32[]{:S(2)}, u32[]{:S(2)}) collective-permute-start(f32[96,1024]{1,0:T(8,128)S(1)} %get-tuple-element.95), channel_id=1, source_target_pairs={{0,1},{1,0},{2,3},{3,2},{4,5},{5,4},{6,7},{7,6},{8,9},{9,8},{10,11... | collective-permute-start | bytes 1179656 | tf_op jit(solution)/shard_map/ppermute | solution.py:218
  61.3 1.0 %collective-permute-start.20 = (f32[96,1024]{1,0:T(8,128)S(1)}, f32[96,1024]{1,0:T(8,128)S(1)}, u32[]{:S(2)}, u32[]{:S(2)}) collective-permute-start(f32[96,1024]{1,0:T(8,128)S(1)} %get-tuple-element.96), channel_id=1, source_target_pairs={{0,2},{1,3},{2,0},{3,1},{4,6},{5,7},{6,4},{7,5},{8,10},{9,11},{10,... | collective-permute-start | bytes 1179656 | tf_op jit(solution)/shard_map/ppermute | solution.py:218
  62.9 7.8 %collective-permute-done.22.r1 = f32[64,1024]{1,0:T(8,128)S(1)} collective-permute-done((f32[64,1024]{1,0:T(8,128)S(1)}, f32[64,1024]{1,0:T(8,128)S(1)}, u32[]{:S(2)}, u32[]{:S(2)}) %collective-permute-start.22) | collective-permute-done | bytes 262176 | tf_op jit(solution)/shard_map/ppermute | solution.py:218
  70.6 1.0 %collective-permute-done.23.r2 = f32[64,1024]{1,0:T(8,128)S(1)} collective-permute-done((f32[64,1024]{1,0:T(8,128)S(1)}, f32[64,1024]{1,0:T(8,128)S(1)}, u32[]{:S(2)}, u32[]{:S(2)}) %collective-permute-start.23) | collective-permute-done | bytes 262176 | tf_op jit(solution)/shard_map/ppermute | solution.py:218
  71.6 1.3 %shard_map.67 = (f32[128,1024]{1,0:T(8,128)}, f32[64,1024]{1,0:T(8,128)}) custom-call(f32[128,1024]{1,0:T(8,128)S(1)} %get-tuple-element.81.qn, f32[128,128]{1,0:T(8,128)S(1)} %get-tuple-element.82.qs, f32[64,1024]{1,0:T(8,128)S(1)} %get-tuple-element.83.pn, f32[64,128]{1,0:T(8,128)S(1)} %get-tuple-element.84.ps, f32[128,1024]{1,0:T(8,128)S(1)} %get-tuple-element.85.own, ...), custom_call_target="tpu_custom_call" | custom-call | flops 1572864 | bytes 8388608 | tf_op jit(solution)/shard_map/pallas_call | solution.py:17
  (41 shorter events, 3.8 us)
Async XLA Ops:
  0.6 18.6 %collective-permute-start.5 = (f32[64,1024]{1,0:T(8,128)}, f32[64,1024]{1,0:T(8,128)S(1)}, u32[]{:S(2)}, u32[]{:S(2)}) collective-permute-start(f32[64,1024]{1,0:T(8,128)} %passages.1), channel_id=1, source_target_pairs={{0,8},{1,9},{2,10},{3,11},{4,12},{5,13},{6,14},{7,15},{8,0},{9,1},... | collective-permute-start | bytes 786440 | tf_op jit(solution)/shard_map/ppermute | solution.py:218
  3.7 18.2 %collective-permute-start.1 = (f32[64,1024]{1,0:T(8,128)}, f32[64,1024]{1,0:T(8,128)S(1)}, u32[]{:S(2)}, u32[]{:S(2)}) collective-permute-start(f32[64,1024]{1,0:T(8,128)} %passages.1), channel_id=1, source_target_pairs={{0,4},{1,5},{2,6},{3,7},{4,0},{5,1},{6,2},{7,3},{8,12},{9,13},{10,... | collective-permute-start | bytes 786440 | tf_op jit(solution)/shard_map/ppermute | solution.py:218
  3.7 15.5 %collective-permute-start.7 = (f32[64,1024]{1,0:T(8,128)}, f32[64,1024]{1,0:T(8,128)S(1)}, u32[]{:S(2)}, u32[]{:S(2)}) collective-permute-start(f32[64,1024]{1,0:T(8,128)} %passages.1), channel_id=1, source_target_pairs={{0,16},{1,17},{2,18},{3,19},{4,20},{5,21},{6,22},{7,23},{8,24},{9,... | collective-permute-start | bytes 786440 | tf_op jit(solution)/shard_map/ppermute | solution.py:218
  6.3 14.3 %collective-permute-start = (f32[128,1024]{1,0:T(8,128)}, f32[128,1024]{1,0:T(8,128)S(1)}, u32[]{:S(2)}, u32[]{:S(2)}) collective-permute-start(f32[128,1024]{1,0:T(8,128)} %queries.1), channel_id=1, source_target_pairs={{0,1},{1,0},{2,3},{3,2},{4,5},{5,4},{6,7},{7,6},{8,9},{9,8},{10,11... | collective-permute-start | bytes 1572872 | tf_op jit(solution)/shard_map/ppermute | solution.py:218
  7.8 15.7 %collective-permute-start.3 = (f32[128,1024]{1,0:T(8,128)}, f32[128,1024]{1,0:T(8,128)S(1)}, u32[]{:S(2)}, u32[]{:S(2)}) collective-permute-start(f32[128,1024]{1,0:T(8,128)} %queries.1), channel_id=1, source_target_pairs={{0,2},{1,3},{2,0},{3,1},{4,6},{5,7},{6,4},{7,5},{8,10},{9,11},{10,... | collective-permute-start | bytes 1572872 | tf_op jit(solution)/shard_map/ppermute | solution.py:218
  11.6 1.0 %copy-start = (f32[128,1024]{1,0:T(8,128)S(1)}, f32[128,1024]{1,0:T(8,128)}, u32[]{:S(2)}) copy-start(f32[128,1024]{1,0:T(8,128)} %queries.1) | copy-start | bytes 1572868
  12.6 0.9 %copy-start.1 = (f32[64,1024]{1,0:T(8,128)S(1)}, f32[64,1024]{1,0:T(8,128)}, u32[]{:S(2)}) copy-start(f32[64,1024]{1,0:T(8,128)} %passages.1) | copy-start | bytes 786436
  19.2 5.9 %collective-permute-start.6 = (f32[64,1024]{1,0:T(8,128)S(1)}, f32[64,1024]{1,0:T(8,128)S(1)}, u32[]{:S(2)}, u32[]{:S(2)}) collective-permute-start(f32[64,1024]{1,0:T(8,128)S(1)} %collective-permute-done.5.refs_6_), channel_id=1, source_target_pairs={{0,4},{1,5},{2,6},{3,7},{4,0},{5,1},{6,2},{7,3},{8,12},{9,13},{10,... | collective-permute-start | bytes 786440 | tf_op jit(solution)/shard_map/ppermute | solution.py:218
  19.2 5.9 %collective-permute-start.9 = (f32[64,1024]{1,0:T(8,128)S(1)}, f32[64,1024]{1,0:T(8,128)S(1)}, u32[]{:S(2)}, u32[]{:S(2)}) collective-permute-start(f32[64,1024]{1,0:T(8,128)S(1)} %copy-done.1), channel_id=1, source_target_pairs={{8,16},{9,17},{10,18},{11,19},{12,20},{13,21},{14,22},{15,23},{16,... | collective-permute-start | bytes 786440 | tf_op jit(solution)/shard_map/ppermute | solution.py:218
  20.6 9.9 %collective-permute-start.10 = (f32[64,1024]{1,0:T(8,128)S(1)}, f32[64,1024]{1,0:T(8,128)S(1)}, u32[]{:S(2)}, u32[]{:S(2)}) collective-permute-start(f32[64,1024]{1,0:T(8,128)S(1)} %collective-permute-done.7.refs_7_), channel_id=1, source_target_pairs={{8,0},{9,1},{10,2},{11,3},{12,4},{13,5},{14,6},{15,7},{16,24},{17,... | collective-permute-start | bytes 786440 | tf_op jit(solution)/shard_map/ppermute | solution.py:218
  21.9 10.6 %collective-permute-start.2 = (f32[64,1024]{1,0:T(8,128)S(1)}, f32[64,1024]{1,0:T(8,128)S(1)}, u32[]{:S(2)}, u32[]{:S(2)}) collective-permute-start(f32[64,1024]{1,0:T(8,128)S(1)} %slice.84), channel_id=1, source_target_pairs={{0,2},{1,3},{2,0},{3,1},{4,6},{5,7},{6,4},{7,5},{8,10},{9,11},{10,... | collective-permute-start | bytes 786440 | tf_op jit(solution)/shard_map/ppermute | solution.py:218
  23.5 9.0 %collective-permute-start.4 = (f32[64,1024]{1,0:T(8,128)S(1)}, f32[64,1024]{1,0:T(8,128)S(1)}, u32[]{:S(2)}, u32[]{:S(2)}) collective-permute-start(f32[64,1024]{1,0:T(8,128)S(1)} %slice.85), channel_id=1, source_target_pairs={{0,1},{1,0},{2,3},{3,2},{4,5},{5,4},{6,7},{7,6},{8,9},{9,8},{10,11... | collective-permute-start | bytes 786440 | tf_op jit(solution)/shard_map/ppermute | solution.py:218
  25.1 7.4 %collective-permute-start.8 = (f32[64,1024]{1,0:T(8,128)S(1)}, f32[64,1024]{1,0:T(8,128)S(1)}, u32[]{:S(2)}, u32[]{:S(2)}) collective-permute-start(f32[64,1024]{1,0:T(8,128)S(1)} %collective-permute-done.7.refs_7_), channel_id=1, source_target_pairs={{0,4},{1,5},{2,6},{3,7},{4,0},{5,1},{6,2},{7,3},{8,12},{9,13},{10,... | collective-permute-start | bytes 786440 | tf_op jit(solution)/shard_map/ppermute | solution.py:218
  30.6 1.9 %collective-permute-start.11 = (f32[64,1024]{1,0:T(8,128)S(1)}, f32[64,1024]{1,0:T(8,128)S(1)}, u32[]{:S(2)}, u32[]{:S(2)}) collective-permute-start(f32[64,1024]{1,0:T(8,128)S(1)} %add.39.refs_5_), channel_id=1, source_target_pairs={{0,4},{1,5},{2,6},{3,7},{4,0},{5,1},{6,2},{7,3},{8,12},{9,13},{10,... | collective-permute-start | bytes 786440 | tf_op jit(solution)/shard_map/ppermute | solution.py:218
  34.2 5.9 %collective-permute-start.14 = (f32[8,512]{1,0:T(8,128)S(1)}, f32[8,512]{1,0:T(8,128)S(1)}, u32[]{:S(2)}, u32[]{:S(2)}) collective-permute-start(f32[8,512]{1,0:T(8,128)S(1)} %get-tuple-element.69.refs_0_), channel_id=1, source_target_pairs={{0,3},{1,2},{2,1},{3,0},{4,7},{5,6},{6,5},{7,4},{8,11},{9,10},{10,... | collective-permute-start | bytes 49160 | tf_op jit(solution)/shard_map/ppermute | solution.py:218
  36.7 3.7 %collective-permute-start.13 = (f32[8,512]{1,0:T(8,128)S(1)}, f32[8,512]{1,0:T(8,128)S(1)}, u32[]{:S(2)}, u32[]{:S(2)}) collective-permute-start(f32[8,512]{1,0:T(8,128)S(1)} %get-tuple-element.69.refs_0_), channel_id=1, source_target_pairs={{0,2},{1,3},{2,0},{3,1},{4,6},{5,7},{6,4},{7,5},{8,10},{9,11},{10,... | collective-permute-start | bytes 49160 | tf_op jit(solution)/shard_map/ppermute | solution.py:218
  37.2 3.7 %collective-permute-start.12 = (f32[8,512]{1,0:T(8,128)S(1)}, f32[8,512]{1,0:T(8,128)S(1)}, u32[]{:S(2)}, u32[]{:S(2)}) collective-permute-start(f32[8,512]{1,0:T(8,128)S(1)} %get-tuple-element.69.refs_0_), channel_id=1, source_target_pairs={{0,1},{1,0},{2,3},{3,2},{4,5},{5,4},{6,7},{7,6},{8,9},{9,8},{10,11... | collective-permute-start | bytes 49160 | tf_op jit(solution)/shard_map/ppermute | solution.py:218
  42.7 2.8 %collective-permute-start.17 = (f32[256,1024]{1,0:T(8,128)S(1)}, f32[256,1024]{1,0:T(8,128)S(1)}, u32[]{:S(2)}, u32[]{:S(2)}) collective-permute-start(f32[256,1024]{1,0:T(8,128)S(1)} %get-tuple-element.77), channel_id=1, source_target_pairs={{0,4},{1,5},{2,6},{3,7},{4,0},{5,1},{6,2},{7,3},{8,12},{9,13},{10,... | collective-permute-start | bytes 3145736 | tf_op jit(solution)/shard_map/ppermute | solution.py:218
  43.2 17.2 %collective-permute-start.15 = (f32[96,1024]{1,0:T(8,128)S(1)}, f32[96,1024]{1,0:T(8,128)S(1)}, u32[]{:S(2)}, u32[]{:S(2)}) collective-permute-start(f32[96,1024]{1,0:T(8,128)S(1)} %get-tuple-element.86), channel_id=1, source_target_pairs={{0,1},{1,0},{2,3},{3,2},{4,5},{5,4},{6,7},{7,6},{8,9},{9,8},{10,11... | collective-permute-start | bytes 1179656 | tf_op jit(solution)/shard_map/ppermute | solution.py:218
  44.0 16.4 %collective-permute-start.16 = (f32[96,1024]{1,0:T(8,128)S(1)}, f32[96,1024]{1,0:T(8,128)S(1)}, u32[]{:S(2)}, u32[]{:S(2)}) collective-permute-start(f32[96,1024]{1,0:T(8,128)S(1)} %get-tuple-element.87), channel_id=1, source_target_pairs={{0,2},{1,3},{2,0},{3,1},{4,6},{5,7},{6,4},{7,5},{8,10},{9,11},{10,... | collective-permute-start | bytes 1179656 | tf_op jit(solution)/shard_map/ppermute | solution.py:218
  45.6 14.6 %collective-permute-start.21 = (f32[64,1024]{1,0:T(8,128)S(1)}, f32[64,1024]{1,0:T(8,128)S(1)}, u32[]{:S(2)}, u32[]{:S(2)}) collective-permute-start(f32[64,1024]{1,0:T(8,128)S(1)} %get-tuple-element.92), channel_id=1, source_target_pairs={{8,16},{9,17},{10,18},{11,19},{12,20},{13,21},{14,22},{15,23},{16,... | collective-permute-start | bytes 786440 | tf_op jit(solution)/shard_map/ppermute | solution.py:218
  46.3 11.5 %collective-permute-start.18 = (f32[64,1024]{1,0:T(8,128)S(1)}, f32[64,1024]{1,0:T(8,128)S(1)}, u32[]{:S(2)}, u32[]{:S(2)}) collective-permute-start(f32[64,1024]{1,0:T(8,128)S(1)} %get-tuple-element.92), channel_id=1, source_target_pairs={{0,8},{1,9},{2,10},{3,11},{4,12},{5,13},{6,14},{7,15},{24,16},{25,... | collective-permute-start | bytes 786440 | tf_op jit(solution)/shard_map/ppermute | solution.py:218
  57.8 13.8 %collective-permute-start.23 = (f32[64,1024]{1,0:T(8,128)S(1)}, f32[64,1024]{1,0:T(8,128)S(1)}, u32[]{:S(2)}, u32[]{:S(2)}) collective-permute-start(f32[64,1024]{1,0:T(8,128)S(1)} %shard_map.65), channel_id=1, source_target_pairs={{0,16},{1,17},{2,18},{3,19},{4,20},{5,21},{6,22},{7,23},{8,24},{9,... | collective-permute-start | bytes 786440 | tf_op jit(solution)/shard_map/ppermute | solution.py:218
  60.2 10.4 %collective-permute-start.22 = (f32[64,1024]{1,0:T(8,128)S(1)}, f32[64,1024]{1,0:T(8,128)S(1)}, u32[]{:S(2)}, u32[]{:S(2)}) collective-permute-start(f32[64,1024]{1,0:T(8,128)S(1)} %get-tuple-element.98), channel_id=1, source_target_pairs={{0,8},{1,9},{2,10},{3,11},{4,12},{5,13},{6,14},{7,15},{8,0},{9,1},... | collective-permute-start | bytes 786440 | tf_op jit(solution)/shard_map/ppermute | solution.py:218
  60.5 11.1 %collective-permute-start.19 = (f32[96,1024]{1,0:T(8,128)S(1)}, f32[96,1024]{1,0:T(8,128)S(1)}, u32[]{:S(2)}, u32[]{:S(2)}) collective-permute-start(f32[96,1024]{1,0:T(8,128)S(1)} %get-tuple-element.95), channel_id=1, source_target_pairs={{0,1},{1,0},{2,3},{3,2},{4,5},{5,4},{6,7},{7,6},{8,9},{9,8},{10,11... | collective-permute-start | bytes 1179656 | tf_op jit(solution)/shard_map/ppermute | solution.py:218
  61.3 10.3 %collective-permute-start.20 = (f32[96,1024]{1,0:T(8,128)S(1)}, f32[96,1024]{1,0:T(8,128)S(1)}, u32[]{:S(2)}, u32[]{:S(2)}) collective-permute-start(f32[96,1024]{1,0:T(8,128)S(1)} %get-tuple-element.96), channel_id=1, source_target_pairs={{0,2},{1,3},{2,0},{3,1},{4,6},{5,7},{6,4},{7,5},{8,10},{9,11},{10,... | collective-permute-start | bytes 1179656 | tf_op jit(solution)/shard_map/ppermute | solution.py:218

commit v4 on v3

--- a/solution.py
+++ b/solution.py
@@ -164,12 +164,12 @@
     stats = refs[:n_stats]
     et, pos, qh, ql, *outs = refs[n_stats:]
     weight = 1.0 / combine(stats)[0:1]
-    d = et[...] * weight - onehot(pos[...], et.shape, 0).astype(f32)
-    g = mm3(split(d), (qh[...], ql[...]), ((1,), (0,)))
+    d = [et[a:b] * weight - onehot(pos[...], (b - a, et.shape[1]), a).astype(f32) for a, b in cuts]
+    g = mm3(split(jnp.concatenate(d, axis=0)), (qh[...], ql[...]), ((1,), (0,)))
     at = 0
-    for out, n in zip(outs, cuts):
-        out[...] = g[at : at + n]
-        at += n
+    for out, (a, b) in zip(outs, cuts):
+        out[...] = g[at : at + b - a]
+        at += b - a
 
 
 def core_sum_kernel(g, tc, g3, t1, t2, t3):
@@ -197,14 +197,14 @@
     return scale * (g - xn * jnp.sum(xn * g, axis=1, keepdims=True))
 
 
-def last_kernel(qn, qs, pn, ps, own, x1, y1, x2, y2, g, tc, r1, rmid, r2, out_q, out_p):
+def last_kernel(qn, qs, pn, ps, own, x1, y1, x2, y2, g, tc, r1, r2, out_q, out_p):
     h, m = qn.shape[0] // 2, pn.shape[0]
     k = x1.shape[0] - h
     for at, n, p, pa, q, qa in ((0, k, x1, h, y2, 0), (k, h - k, x2, 0, y2, k), (h, k, y1, h, x2, h - k), (h + k, h - k, y2, h, x2, h)):
         if n:
             s = own[at : at + n] + p[pa : pa + n] + q[qa : qa + n]
             out_q[at : at + n] = project(s, qn[at : at + n], qs[at : at + n, 0:1])
-    out_p[...] = project(g[:m] + tc[:m] + r1[...] + rmid[...] + r2[...], pn[...], ps[:, 0:1])
+    out_p[...] = project(g[:m] + tc[:m] + r1[...] + r2[...], pn[...], ps[:, 0:1])
 
 
 def final_kernel(rows, g, out):
@@ -212,30 +212,13 @@
     out[...] = project(g[...], xn, scale)
 
 
-def flip(x, mask, only=None):
+def flip(x, mask):
     n = lax.axis_size("pb") * lax.axis_size("pa")
-    pairs = [(i, i ^ mask) for i in range(n) if only is None or only(i)]
-    return lax.ppermute(x, AXES, pairs)
-
-
-X, Y, C, Z1, Z2, Z3 = 1, 2, 4, 8, 16, 24
+    return lax.ppermute(x, AXES, [(i, i ^ mask) for i in range(n)])
+
+
+X, Y, C, Z1, Z2 = 1, 2, 4, 8, 16
 EARLY = 2
-
-
-def middle(i):
-    return (i // 8) in (1, 2)
-
-
-def ends(i):
-    return not middle(i)
-
-
-def rows_of(x, *cuts):
-    at, out = 0, []
-    for n in cuts:
-        out.append(lax.slice_in_dim(x, at, at + n, axis=0))
-        at += n
-    return out
 
 
 def after(x, *others):
@@ -263,13 +246,11 @@
     c0 = flip(passages, C)
     qn, qs, qh0, ql0, pn, ps, ph0, pl0 = own_rows(queries, passages)
     z2 = after(z2, qh0, pos)
-    far = flip(z2, Z1, middle)
-    mid = flip(after(passages, z2), Z3, middle)
+    z3 = flip(z2, Z1)
     da, db = flip(after(x[:h], c0), Y), flip(after(y[h:], c0), X)
     c1 = flip(after(z1, qh0, pos), C)
     c2 = flip(after(z2, c1), C)
     first = first_scores((qh0, ql0, ph0, pl0, x, y, z1, z2, c0), pos)
-    z3 = mid + far
     c3 = flip(z3, C)
 
     et, stats, qh, ql, ph2, pl2 = rest_scores([da, db], [c1, c2, c3, z3], pos, first)
@@ -280,18 +261,18 @@
     def part(k, n):
         return (k * n, k * n + n)
 
-    g, gc, g3 = passage_grads(both, after(et, u), pos, qh, ql, (3 * pr, 4 * pr, pr))
+    (gc,) = passage_grads(both, after(et, u), pos, qh, ql, ((3 * pr, 7 * pr),))
     tc = flip(gc, C)
+    g, g3 = passage_grads(both, after(et, gc), pos, qh, ql, ((0, 3 * pr), (7 * pr, 8 * pr)))
     k = EARLY * h // 4
     kx, ky = 2 * h + k, 5 * h + k
     cuts = ((part(6, h), (2 * h, kx)), (part(7, h), (5 * h, ky)), ((kx, 4 * h),), (part(4, h), (ky, 6 * h)), ((0, qr),))
-    losses, gx1, gy1, gx, gy, own = query_grads(both, after(u, gc), v, cuts)
+    losses, gx1, gy1, gx, gy, own = query_grads(both, after(u, g), v, cuts)
     x1, y1 = flip(gx1, X), flip(gy1, Y)
     t1, t2, t3 = core_sums(g, tc, g3)
-    ff = flip(t3, Z1, ends)
-    rmid = flip(t3, Z3, middle)
-    t2 = add(t2, ff)
-    r1, r2 = flip(after(t1, t2, rmid), Z1), flip(t2, Z2)
+    r3 = flip(t3, Z1)
+    t2 = add(t2, r3)
+    r1, r2 = flip(after(t1, t2), Z1), flip(t2, Z2)
     gx, gy = cross(after(gx, t2), gy, x1, y1)
     x2, y2 = flip(gx, X), flip(gy, Y)
 
@@ -300,7 +281,7 @@
         last_kernel,
         [(queries.shape, f32), (passages.shape, f32)],
         12 * queries.size,
-        *(qn, qs, pn, ps, own, x1, y1, x2, y2, g, tc, r1, rmid, r2),
+        *(qn, qs, pn, ps, own, x1, y1, x2, y2, g, tc, r1, r2),
         kept=False,
     )
     return losses, query_grad, passage_grad
@@ -371,8 +352,8 @@
     q, d = qh.shape
     return call(
         functools.partial(passage_kernel, len(both), cuts),
-        [((n, d), f32) for n in cuts],
-        6 * q * d * sum(cuts),
+        [((b - a, d), f32) for a, b in cuts],
+        6 * q * d * sum(b - a for a, b in cuts),
         *both,
         et,
         pos,
@@ -408,7 +389,7 @@
     both = [lax.psum(stats, "pa")]
     u, v = unscaled(et, pos, [ph], [pl_])
     losses, gq = query_grads(both, u, v, (((0, q_rows),),))
-    (gp,) = passage_grads(both, et, pos, qh, ql, (p_rows,))
+    (gp,) = passage_grads(both, et, pos, qh, ql, ((0, p_rows),))
     q_part = lax.psum_scatter(gq, "pa", scatter_dimension=0, tiled=True)
     p_part = lax.psum_scatter(gp, "pb", scatter_dimension=0, tiled=True)
     return losses.reshape(-1), finish(queries, q_part), finish(passages, p_part)

time: 73.2 us -> 66.3 us (0.906)
  starting transfers between devices: 30.7 us -> 22.6 us
  waiting for transfers between devices: 26.6 us -> 27.9 us
    ppermute x24 -> x22, starting transfers between devices: 30.7 us -> 22.6 us  [flip(): return lax.ppermute(x, AXES, [(i, i ^ mask) for i in range(n)])]
    ppermute x24 -> x22, waiting for transfers between devices: 26.6 us -> 27.9 us  [flip(): return lax.ppermute(x, AXES, [(i, i ^ mask) for i in range(n)])]
    pallas_call x10 -> x11, Pallas kernels: 9.73 us -> 9.85 us  [call(): pl.pallas_call(kernel, out_shape=[pltpu.VMEM(s, d) if kept else jax.Shape...]
  transfers between devices with their start and end apart: 24 -> 22, of which waited for: 8 -> 8; matrix products, arithmetic and copies ran while one was open for 4% -> 4% of each run, Pallas kernels for 7% -> 9%
where the time goes in v4:
time: 66.3 us; the launch traced here: 66.1 us
  waiting for transfers between devices  27.9 us (42%)
  starting transfers between devices  22.6 us (34%)
  Pallas kernels  9.85 us (15%)
  local copies, waits for them, and re-layouts  2.87 us (4%)
  other arithmetic  2.03 us (3%)
  between operations  0.78 us (1%)
    ppermute x22, waiting for transfers between devices, flip(): return lax.ppermute(x, AXES, [(i, i ^ mask) for i in range(n)])  27.9 us
    ppermute x22, starting transfers between devices, flip(): return lax.ppermute(x, AXES, [(i, i ^ mask) for i in range(n)])  22.6 us
    pallas_call x11, Pallas kernels, call(): pl.pallas_call(kernel, out_shape=[pltpu.VMEM(s, d) if kept else jax.Shape...  9.85 us
    unnamed x4, local copies, waits for them, and re-layouts  1.99 us
  transfers between devices with their start and end apart: 22, of which 8 were waited for; matrix products, arithmetic and copies ran while one was open for 4% of the time, Pallas kernels for 9%

profile of v4, /device:TPU:0, one launch (start us, length us, event | category | flops | bytes accessed | tf_op | source)
XLA Modules:
  0.0 66.1 jit_solution(7763010726090729217)
XLA Ops:
  0.6 3.1 %collective-permute-start.5 = (f32[64,1024]{1,0:T(8,128)}, f32[64,1024]{1,0:T(8,128)S(1)}, u32[]{:S(2)}, u32[]{:S(2)}) collective-permute-start(f32[64,1024]{1,0:T(8,128)} %passages.1), channel_id=1, source_target_pairs={{0,8},{1,9},{2,10},{3,11},{4,12},{5,13},{6,14},{7,15},{8,0},{9,1},... | collective-permute-start | bytes 786440 | tf_op jit(solution)/shard_map/ppermute | solution.py:217
  3.7 2.6 %collective-permute-start.7 = (f32[64,1024]{1,0:T(8,128)}, f32[64,1024]{1,0:T(8,128)S(1)}, u32[]{:S(2)}, u32[]{:S(2)}) collective-permute-start(f32[64,1024]{1,0:T(8,128)} %passages.1), channel_id=1, source_target_pairs={{0,16},{1,17},{2,18},{3,19},{4,20},{5,21},{6,22},{7,23},{8,24},{9,... | collective-permute-start | bytes 786440 | tf_op jit(solution)/shard_map/ppermute | solution.py:217
  6.3 1.5 %collective-permute-start = (f32[128,1024]{1,0:T(8,128)}, f32[128,1024]{1,0:T(8,128)S(1)}, u32[]{:S(2)}, u32[]{:S(2)}) collective-permute-start(f32[128,1024]{1,0:T(8,128)} %queries.1), channel_id=1, source_target_pairs={{0,1},{1,0},{2,3},{3,2},{4,5},{5,4},{6,7},{7,6},{8,9},{9,8},{10,11... | collective-permute-start | bytes 1572872 | tf_op jit(solution)/shard_map/ppermute | solution.py:217
  7.8 1.5 %collective-permute-start.3 = (f32[128,1024]{1,0:T(8,128)}, f32[128,1024]{1,0:T(8,128)S(1)}, u32[]{:S(2)}, u32[]{:S(2)}) collective-permute-start(f32[128,1024]{1,0:T(8,128)} %queries.1), channel_id=1, source_target_pairs={{0,2},{1,3},{2,0},{3,1},{4,6},{5,7},{6,4},{7,5},{8,10},{9,11},{10,... | collective-permute-start | bytes 1572872 | tf_op jit(solution)/shard_map/ppermute | solution.py:217
  9.3 0.8 %slice_bitcast_fusion.3 = (s32[1,128]{1,0:T(1,128)S(1)}, s32[1,128]{1,0:T(1,128)S(1)}, s32[1,128]{1,0:T(1,128)S(1)}, s32[1,128]{1,0:T(1,128)S(1)}) fusion(s32[512]{0:T(512)} %param.5), kind=kLoop, calls=%fused_computation.46 | loop fusion | bytes 4096 | tf_op jit(solution)/shard_map/slice | solution.py:229
  10.2 0.7 %bitcast_select_fusion.2 = s32[4,128]{1,0:T(4,128)S(1)} fusion(s32[512]{0:T(512)} %param.5, pred[]{:T(512)S(6)} %ne.67, s32[1,128]{1,0:T(1,128)S(1)} %get-tuple-element.108, s32[1,128]{1,0:T(1,128)S(1)} %get-tuple-element.109, s32[1,128]{1,0:T(1,128)S(1)} %get-tuple-element.110, s32[1,128]{1,0:T(1,128)S(1)} %get-tuple-element.107), kind=kLoop, calls=%fused_computation.33 | loop fusion | flops 2048 | bytes 6145 | tf_op jit(solution)/shard_map/jit(_where)/select_n | solution.py:229
  10.9 0.7 %fusion.7 = s32[512]{0:T(512)S(1)} fusion(s32[512]{0:T(512)} %param.5, s32[2,128]{1,0:T(2,128)S(1)} %get-tuple-element.106, s32[2,128]{1,0:T(2,128)S(1)} %get-tuple-element.105, s32[]{:T(128)S(6)} %axis_index.25, s32[]{:T(128)S(6)} %axis_index.22, pred[]{:T(512)S(6)} %ne.67, pred[]{:T(512)S(6)} %ne.66, s32[1,128]{1,0:T(1,128)S(1)} %get-tuple-element.108, ...), kind=kLoop, calls=%fused_computation.23 | loop fusion | flops 38912 | bytes 8202 | tf_op jit(solution)/shard_map/jit(_where)/select_n | solution.py:242
  11.6 1.0 %copy-done = f32[128,1024]{1,0:T(8,128)S(1)} copy-done((f32[128,1024]{1,0:T(8,128)S(1)}, f32[128,1024]{1,0:T(8,128)}, u32[]{:S(2)}) %copy-start) | copy-done | bytes 524312
  12.6 0.9 %copy-done.1 = f32[64,1024]{1,0:T(8,128)S(1)} copy-done((f32[64,1024]{1,0:T(8,128)S(1)}, f32[64,1024]{1,0:T(8,128)}, u32[]{:S(2)}) %copy-start.1) | copy-done | bytes 262168
  13.8 1.0 %collective-permute-done.5.refs_6_ = f32[64,1024]{1,0:T(8,128)S(1)} collective-permute-done((f32[64,1024]{1,0:T(8,128)}, f32[64,1024]{1,0:T(8,128)S(1)}, u32[]{:S(2)}, u32[]{:S(2)}) %collective-permute-start.5) | collective-permute-done | bytes 262176 | tf_op jit(solution)/shard_map/ppermute | solution.py:217
  14.8 4.4 %collective-permute-done.7.refs_7_ = f32[64,1024]{1,0:T(8,128)S(1)} collective-permute-done((f32[64,1024]{1,0:T(8,128)}, f32[64,1024]{1,0:T(8,128)S(1)}, u32[]{:S(2)}, u32[]{:S(2)}) %collective-permute-start.7) | collective-permute-done | bytes 262176 | tf_op jit(solution)/shard_map/ppermute | solution.py:217
  19.2 1.4 %collective-permute-done.refs_4_ = f32[128,1024]{1,0:T(8,128)S(1)} collective-permute-done((f32[128,1024]{1,0:T(8,128)}, f32[128,1024]{1,0:T(8,128)S(1)}, u32[]{:S(2)}, u32[]{:S(2)}) %collective-permute-start) | collective-permute-done | bytes 524320 | tf_op jit(solution)/shard_map/ppermute | solution.py:217
  20.6 1.6 %collective-permute-start.2 = (f32[64,1024]{1,0:T(8,128)S(1)}, f32[64,1024]{1,0:T(8,128)S(1)}, u32[]{:S(2)}, u32[]{:S(2)}) collective-permute-start(f32[64,1024]{1,0:T(8,128)S(1)} %slice.84), channel_id=1, source_target_pairs={{0,2},{1,3},{2,0},{3,1},{4,6},{5,7},{6,4},{7,5},{8,10},{9,11},{10,... | collective-permute-start | bytes 786440 | tf_op jit(solution)/shard_map/ppermute | solution.py:217
  22.2 1.6 %collective-permute-start.4 = (f32[64,1024]{1,0:T(8,128)S(1)}, f32[64,1024]{1,0:T(8,128)S(1)}, u32[]{:S(2)}, u32[]{:S(2)}) collective-permute-start(f32[64,1024]{1,0:T(8,128)S(1)} %slice.85), channel_id=1, source_target_pairs={{0,1},{1,0},{2,3},{3,2},{4,5},{5,4},{6,7},{7,6},{8,9},{9,8},{10,11... | collective-permute-start | bytes 786440 | tf_op jit(solution)/shard_map/ppermute | solution.py:217
  23.8 3.4 %collective-permute-done.9.refs_5_ = f32[64,1024]{1,0:T(8,128)S(1)} collective-permute-done((f32[64,1024]{1,0:T(8,128)S(1)}, f32[64,1024]{1,0:T(8,128)S(1)}, u32[]{:S(2)}, u32[]{:S(2)}) %collective-permute-start.9) | collective-permute-done | bytes 262176 | tf_op jit(solution)/shard_map/ppermute | solution.py:217
  27.2 1.8 %shard_map.59 = (f32[256,384]{1,0:T(8,128)S(1)}, f32[8,384]{1,0:T(8,128)S(1)}, bf16[384,1024]{1,0:T(8,128)(2,1)S(1)}, bf16[384,1024]{1,0:T(8,128)(2,1)S(1)}, bf1...) custom-call(bf16[128,1024]{1,0:T(8,128)(2,1)S(1)} %get-tuple-element.53.refs_0_, ...), custom_call_target="tpu_custom_call" | custom-call | flops 1006632960 | bytes 8388608 | tf_op jit(solution)/shard_map/pallas_call | solution.py:17
  29.0 0.7 %collective-permute-done.4.refs_1_ = f32[64,1024]{1,0:T(8,128)S(1)} collective-permute-done((f32[64,1024]{1,0:T(8,128)S(1)}, f32[64,1024]{1,0:T(8,128)S(1)}, u32[]{:S(2)}, u32[]{:S(2)}) %collective-permute-start.4) | collective-permute-done | bytes 262176 | tf_op jit(solution)/shard_map/ppermute | solution.py:217
  29.6 1.6 %shard_map.60 = (f32[512,512]{1,0:T(8,128)S(1)}, f32[8,512]{1,0:T(8,128)S(1)}, bf16[512,1024]{1,0:T(8,128)(2,1)S(1)}, bf16[512,1024]{1,0:T(8,128)(2,1)S(1)}, bf1...) custom-call(f32[64,1024]{1,0:T(8,128)S(1)} %collective-permute-done.2.refs_0_, ...), custom_call_target="tpu_custom_call" | custom-call | flops 805306368 | bytes 8388608 | tf_op jit(solution)/shard_map/pallas_call | solution.py:17
  31.3 1.9 %collective-permute-start.13 = (f32[8,512]{1,0:T(8,128)S(1)}, f32[8,512]{1,0:T(8,128)S(1)}, u32[]{:S(2)}, u32[]{:S(2)}) collective-permute-start(f32[8,512]{1,0:T(8,128)S(1)} %get-tuple-element.67.refs_0_), channel_id=1, source_target_pairs={{0,3},{1,2},{2,1},{3,0},{4,7},{5,6},{6,5},{7,4},{8,11},{9,10},{10,... | collective-permute-start | bytes 49160 | tf_op jit(solution)/shard_map/ppermute | solution.py:217
  33.1 1.1 %collective-permute-start.12 = (f32[8,512]{1,0:T(8,128)S(1)}, f32[8,512]{1,0:T(8,128)S(1)}, u32[]{:S(2)}, u32[]{:S(2)}) collective-permute-start(f32[8,512]{1,0:T(8,128)S(1)} %get-tuple-element.67.refs_0_), channel_id=1, source_target_pairs={{0,2},{1,3},{2,0},{3,1},{4,6},{5,7},{6,4},{7,5},{8,10},{9,11},{10,... | collective-permute-start | bytes 49160 | tf_op jit(solution)/shard_map/ppermute | solution.py:217
  34.8 2.4 %shard_map.61 = (f32[512,1024]{1,0:T(8,128)S(1)}, f32[512,1024]{1,0:T(8,128)S(1)}) custom-call(f32[512,512]{1,0:T(8,128)S(1)} %get-tuple-element.75.et.refs_4_, s32[1,512]{1,0:T(1,128)S(1)} %bitcast.35, bf16[256,1024]{1,0:T(8,128)(2,1)S(1)} %get-tuple-element.64.refs_11_.refs_0_, bf16[256,1024]{1,0:T(8,128)(2,1)S(1)} %get-tuple-element.69.refs_1_, ...), custom_call_target="tpu_custom_call" | custom-call | flops 2147483648 | bytes 8388608 | tf_op jit(solution)/shard_map/pallas_call | solution.py:17
  37.2 0.8 %collective-permute-done.11.refs_1_ = f32[8,512]{1,0:T(8,128)S(1)} collective-permute-done((f32[8,512]{1,0:T(8,128)S(1)}, f32[8,512]{1,0:T(8,128)S(1)}, u32[]{:S(2)}, u32[]{:S(2)}) %collective-permute-start.11) | collective-permute-done | bytes 16416 | tf_op jit(solution)/shard_map/ppermute | solution.py:217
  38.0 1.0 %shard_map.62 = f32[256,1024]{1,0:T(8,128)S(1)} custom-call(f32[8,512]{1,0:T(8,128)S(1)} %get-tuple-element.67.refs_0_, f32[8,512]{1,0:T(8,128)S(1)} %collective-permute-done.11.refs_1_, f32[8,512]{1,0:T(8,128)S(1)} %collective-permute-done.12.refs_2_, f32[8,512]{1,0:T(8,128)S(1)} %collective-permute-done.13.refs_3_, ...), custom_call_target="tpu_custom_call" | custom-call | flops 805306368 | bytes 8388608 | tf_op jit(solution)/shard_map/pallas_call | solution.py:17
  39.1 1.0 %shard_map.63 = (f32[192,1024]{1,0:T(8,128)S(1)}, f32[64,1024]{1,0:T(8,128)S(1)}) custom-call(f32[8,512]{1,0:T(8,128)S(1)} %get-tuple-element.67.refs_0_, f32[8,512]{1,0:T(8,128)S(1)} %collective-permute-done.11.refs_1_, f32[8,512]{1,0:T(8,128)S(1)} %collective-permute-done.12.refs_2_, f32[8,512]{1,0:T(8,128)S(1)} %collective-permute-done.13.refs_3_, ...), custom_call_target="tpu_custom_call" | custom-call | flops 805306368 | bytes 8388608 | tf_op jit(solution)/shard_map/pallas_call | solution.py:17
  40.5 0.8 %collective-permute-start.14 = (f32[96,1024]{1,0:T(8,128)S(1)}, f32[96,1024]{1,0:T(8,128)S(1)}, u32[]{:S(2)}, u32[]{:S(2)}) collective-permute-start(f32[96,1024]{1,0:T(8,128)S(1)} %get-tuple-element.85), channel_id=1, source_target_pairs={{0,1},{1,0},{2,3},{3,2},{4,5},{5,4},{6,7},{7,6},{8,9},{9,8},{10,11... | collective-permute-start | bytes 1179656 | tf_op jit(solution)/shard_map/ppermute | solution.py:217
  41.3 0.9 %collective-permute-start.15 = (f32[96,1024]{1,0:T(8,128)S(1)}, f32[96,1024]{1,0:T(8,128)S(1)}, u32[]{:S(2)}, u32[]{:S(2)}) collective-permute-start(f32[96,1024]{1,0:T(8,128)S(1)} %get-tuple-element.86), channel_id=1, source_target_pairs={{0,2},{1,3},{2,0},{3,1},{4,6},{5,7},{6,4},{7,5},{8,10},{9,11},{10,... | collective-permute-start | bytes 1179656 | tf_op jit(solution)/shard_map/ppermute | solution.py:217
  42.8 7.7 %collective-permute-done.17.b = f32[64,1024]{1,0:T(8,128)S(1)} collective-permute-done((f32[64,1024]{1,0:T(8,128)S(1)}, f32[64,1024]{1,0:T(8,128)S(1)}, u32[]{:S(2)}, u32[]{:S(2)}) %collective-permute-start.17) | collective-permute-done | bytes 262176 | tf_op jit(solution)/shard_map/ppermute | solution.py:217
  50.5 1.5 %collective-permute-start.21 = (f32[64,1024]{1,0:T(8,128)S(1)}, f32[64,1024]{1,0:T(8,128)S(1)}, u32[]{:S(2)}, u32[]{:S(2)}) collective-permute-start(f32[64,1024]{1,0:T(8,128)S(1)} %shard_map.66), channel_id=1, source_target_pairs={{0,16},{1,17},{2,18},{3,19},{4,20},{5,21},{6,22},{7,23},{8,24},{9,... | collective-permute-start | bytes 786440 | tf_op jit(solution)/shard_map/ppermute | solution.py:217
  52.1 1.6 %collective-permute-start.20 = (f32[64,1024]{1,0:T(8,128)S(1)}, f32[64,1024]{1,0:T(8,128)S(1)}, u32[]{:S(2)}, u32[]{:S(2)}) collective-permute-start(f32[64,1024]{1,0:T(8,128)S(1)} %get-tuple-element.96), channel_id=1, source_target_pairs={{0,8},{1,9},{2,10},{3,11},{4,12},{5,13},{6,14},{7,15},{8,0},{9,1},... | collective-permute-start | bytes 786440 | tf_op jit(solution)/shard_map/ppermute | solution.py:217
  53.7 1.4 %collective-permute-start.18 = (f32[96,1024]{1,0:T(8,128)S(1)}, f32[96,1024]{1,0:T(8,128)S(1)}, u32[]{:S(2)}, u32[]{:S(2)}) collective-permute-start(f32[96,1024]{1,0:T(8,128)S(1)} %get-tuple-element.93), channel_id=1, source_target_pairs={{0,1},{1,0},{2,3},{3,2},{4,5},{5,4},{6,7},{7,6},{8,9},{9,8},{10,11... | collective-permute-start | bytes 1179656 | tf_op jit(solution)/shard_map/ppermute | solution.py:217
  56.2 8.6 %collective-permute-done.20.r1 = f32[64,1024]{1,0:T(8,128)S(1)} collective-permute-done((f32[64,1024]{1,0:T(8,128)S(1)}, f32[64,1024]{1,0:T(8,128)S(1)}, u32[]{:S(2)}, u32[]{:S(2)}) %collective-permute-start.20) | collective-permute-done | bytes 262176 | tf_op jit(solution)/shard_map/ppermute | solution.py:217
  64.8 1.2 %shard_map.68 = (f32[128,1024]{1,0:T(8,128)}, f32[64,1024]{1,0:T(8,128)}) custom-call(f32[128,1024]{1,0:T(8,128)S(1)} %get-tuple-element.80.qn, f32[128,128]{1,0:T(8,128)S(1)} %get-tuple-element.81.qs, f32[64,1024]{1,0:T(8,128)S(1)} %get-tuple-element.82.pn, f32[64,128]{1,0:T(8,128)S(1)} %get-tuple-element.83.ps, f32[128,1024]{1,0:T(8,128)S(1)} %get-tuple-element.84.own, ...), custom_call_target="tpu_custom_call" | custom-call | flops 1572864 | bytes 8388608 | tf_op jit(solution)/shard_map/pallas_call | solution.py:17
  (37 shorter events, 3.2 us)
Async XLA Ops:
  0.6 14.2 %collective-permute-start.5 = (f32[64,1024]{1,0:T(8,128)}, f32[64,1024]{1,0:T(8,128)S(1)}, u32[]{:S(2)}, u32[]{:S(2)}) collective-permute-start(f32[64,1024]{1,0:T(8,128)} %passages.1), channel_id=1, source_target_pairs={{0,8},{1,9},{2,10},{3,11},{4,12},{5,13},{6,14},{7,15},{8,0},{9,1},... | collective-permute-start | bytes 786440 | tf_op jit(solution)/shard_map/ppermute | solution.py:217
  3.7 16.9 %collective-permute-start.1 = (f32[64,1024]{1,0:T(8,128)}, f32[64,1024]{1,0:T(8,128)S(1)}, u32[]{:S(2)}, u32[]{:S(2)}) collective-permute-start(f32[64,1024]{1,0:T(8,128)} %passages.1), channel_id=1, source_target_pairs={{0,4},{1,5},{2,6},{3,7},{4,0},{5,1},{6,2},{7,3},{8,12},{9,13},{10,... | collective-permute-start | bytes 786440 | tf_op jit(solution)/shard_map/ppermute | solution.py:217
  3.7 15.5 %collective-permute-start.7 = (f32[64,1024]{1,0:T(8,128)}, f32[64,1024]{1,0:T(8,128)S(1)}, u32[]{:S(2)}, u32[]{:S(2)}) collective-permute-start(f32[64,1024]{1,0:T(8,128)} %passages.1), channel_id=1, source_target_pairs={{0,16},{1,17},{2,18},{3,19},{4,20},{5,21},{6,22},{7,23},{8,24},{9,... | collective-permute-start | bytes 786440 | tf_op jit(solution)/shard_map/ppermute | solution.py:217
  6.3 14.3 %collective-permute-start = (f32[128,1024]{1,0:T(8,128)}, f32[128,1024]{1,0:T(8,128)S(1)}, u32[]{:S(2)}, u32[]{:S(2)}) collective-permute-start(f32[128,1024]{1,0:T(8,128)} %queries.1), channel_id=1, source_target_pairs={{0,1},{1,0},{2,3},{3,2},{4,5},{5,4},{6,7},{7,6},{8,9},{9,8},{10,11... | collective-permute-start | bytes 1572872 | tf_op jit(solution)/shard_map/ppermute | solution.py:217
  7.8 14.4 %collective-permute-start.3 = (f32[128,1024]{1,0:T(8,128)}, f32[128,1024]{1,0:T(8,128)S(1)}, u32[]{:S(2)}, u32[]{:S(2)}) collective-permute-start(f32[128,1024]{1,0:T(8,128)} %queries.1), channel_id=1, source_target_pairs={{0,2},{1,3},{2,0},{3,1},{4,6},{5,7},{6,4},{7,5},{8,10},{9,11},{10,... | collective-permute-start | bytes 1572872 | tf_op jit(solution)/shard_map/ppermute | solution.py:217
  11.6 1.0 %copy-start = (f32[128,1024]{1,0:T(8,128)S(1)}, f32[128,1024]{1,0:T(8,128)}, u32[]{:S(2)}) copy-start(f32[128,1024]{1,0:T(8,128)} %queries.1) | copy-start | bytes 1572868
  12.6 0.9 %copy-start.1 = (f32[64,1024]{1,0:T(8,128)S(1)}, f32[64,1024]{1,0:T(8,128)}, u32[]{:S(2)}) copy-start(f32[64,1024]{1,0:T(8,128)} %passages.1) | copy-start | bytes 786436
  14.8 9.0 %collective-permute-start.6 = (f32[64,1024]{1,0:T(8,128)S(1)}, f32[64,1024]{1,0:T(8,128)S(1)}, u32[]{:S(2)}, u32[]{:S(2)}) collective-permute-start(f32[64,1024]{1,0:T(8,128)S(1)} %collective-permute-done.5.refs_6_), channel_id=1, source_target_pairs={{0,4},{1,5},{2,6},{3,7},{4,0},{5,1},{6,2},{7,3},{8,12},{9,13},{10,... | collective-permute-start | bytes 786440 | tf_op jit(solution)/shard_map/ppermute | solution.py:217
  19.2 7.9 %collective-permute-start.9 = (f32[64,1024]{1,0:T(8,128)S(1)}, f32[64,1024]{1,0:T(8,128)S(1)}, u32[]{:S(2)}, u32[]{:S(2)}) collective-permute-start(f32[64,1024]{1,0:T(8,128)S(1)} %collective-permute-done.7.refs_7_), channel_id=1, source_target_pairs={{0,8},{1,9},{2,10},{3,11},{4,12},{5,13},{6,14},{7,15},{8,0},{9,1},... | collective-permute-start | bytes 786440 | tf_op jit(solution)/shard_map/ppermute | solution.py:217
  20.6 8.3 %collective-permute-start.2 = (f32[64,1024]{1,0:T(8,128)S(1)}, f32[64,1024]{1,0:T(8,128)S(1)}, u32[]{:S(2)}, u32[]{:S(2)}) collective-permute-start(f32[64,1024]{1,0:T(8,128)S(1)} %slice.84), channel_id=1, source_target_pairs={{0,2},{1,3},{2,0},{3,1},{4,6},{5,7},{6,4},{7,5},{8,10},{9,11},{10,... | collective-permute-start | bytes 786440 | tf_op jit(solution)/shard_map/ppermute | solution.py:217
  22.2 7.4 %collective-permute-start.4 = (f32[64,1024]{1,0:T(8,128)S(1)}, f32[64,1024]{1,0:T(8,128)S(1)}, u32[]{:S(2)}, u32[]{:S(2)}) collective-permute-start(f32[64,1024]{1,0:T(8,128)S(1)} %slice.85), channel_id=1, source_target_pairs={{0,1},{1,0},{2,3},{3,2},{4,5},{5,4},{6,7},{7,6},{8,9},{9,8},{10,11... | collective-permute-start | bytes 786440 | tf_op jit(solution)/shard_map/ppermute | solution.py:217
  23.8 5.8 %collective-permute-start.8 = (f32[64,1024]{1,0:T(8,128)S(1)}, f32[64,1024]{1,0:T(8,128)S(1)}, u32[]{:S(2)}, u32[]{:S(2)}) collective-permute-start(f32[64,1024]{1,0:T(8,128)S(1)} %collective-permute-done.7.refs_7_), channel_id=1, source_target_pairs={{0,4},{1,5},{2,6},{3,7},{4,0},{5,1},{6,2},{7,3},{8,12},{9,13},{10,... | collective-permute-start | bytes 786440 | tf_op jit(solution)/shard_map/ppermute | solution.py:217
  27.1 2.5 %collective-permute-start.10 = (f32[64,1024]{1,0:T(8,128)S(1)}, f32[64,1024]{1,0:T(8,128)S(1)}, u32[]{:S(2)}, u32[]{:S(2)}) collective-permute-start(f32[64,1024]{1,0:T(8,128)S(1)} %collective-permute-done.9.refs_5_), channel_id=1, source_target_pairs={{0,4},{1,5},{2,6},{3,7},{4,0},{5,1},{6,2},{7,3},{8,12},{9,13},{10,... | collective-permute-start | bytes 786440 | tf_op jit(solution)/shard_map/ppermute | solution.py:217
  31.3 5.9 %collective-permute-start.13 = (f32[8,512]{1,0:T(8,128)S(1)}, f32[8,512]{1,0:T(8,128)S(1)}, u32[]{:S(2)}, u32[]{:S(2)}) collective-permute-start(f32[8,512]{1,0:T(8,128)S(1)} %get-tuple-element.67.refs_0_), channel_id=1, source_target_pairs={{0,3},{1,2},{2,1},{3,0},{4,7},{5,6},{6,5},{7,4},{8,11},{9,10},{10,... | collective-permute-start | bytes 49160 | tf_op jit(solution)/shard_map/ppermute | solution.py:217
  33.1 4.1 %collective-permute-start.12 = (f32[8,512]{1,0:T(8,128)S(1)}, f32[8,512]{1,0:T(8,128)S(1)}, u32[]{:S(2)}, u32[]{:S(2)}) collective-permute-start(f32[8,512]{1,0:T(8,128)S(1)} %get-tuple-element.67.refs_0_), channel_id=1, source_target_pairs={{0,2},{1,3},{2,0},{3,1},{4,6},{5,7},{6,4},{7,5},{8,10},{9,11},{10,... | collective-permute-start | bytes 49160 | tf_op jit(solution)/shard_map/ppermute | solution.py:217
  34.3 3.7 %collective-permute-start.11 = (f32[8,512]{1,0:T(8,128)S(1)}, f32[8,512]{1,0:T(8,128)S(1)}, u32[]{:S(2)}, u32[]{:S(2)}) collective-permute-start(f32[8,512]{1,0:T(8,128)S(1)} %get-tuple-element.67.refs_0_), channel_id=1, source_target_pairs={{0,1},{1,0},{2,3},{3,2},{4,5},{5,4},{6,7},{7,6},{8,9},{9,8},{10,11... | collective-permute-start | bytes 49160 | tf_op jit(solution)/shard_map/ppermute | solution.py:217
  39.0 3.2 %collective-permute-start.16 = (f32[256,1024]{1,0:T(8,128)S(1)}, f32[256,1024]{1,0:T(8,128)S(1)}, u32[]{:S(2)}, u32[]{:S(2)}) collective-permute-start(f32[256,1024]{1,0:T(8,128)S(1)} %shard_map.62), channel_id=1, source_target_pairs={{0,4},{1,5},{2,6},{3,7},{4,0},{5,1},{6,2},{7,3},{8,12},{9,13},{10,... | collective-permute-start | bytes 3145736 | tf_op jit(solution)/shard_map/ppermute | solution.py:217
  40.5 13.1 %collective-permute-start.14 = (f32[96,1024]{1,0:T(8,128)S(1)}, f32[96,1024]{1,0:T(8,128)S(1)}, u32[]{:S(2)}, u32[]{:S(2)}) collective-permute-start(f32[96,1024]{1,0:T(8,128)S(1)} %get-tuple-element.85), channel_id=1, source_target_pairs={{0,1},{1,0},{2,3},{3,2},{4,5},{5,4},{6,7},{7,6},{8,9},{9,8},{10,11... | collective-permute-start | bytes 1179656 | tf_op jit(solution)/shard_map/ppermute | solution.py:217
  41.3 12.3 %collective-permute-start.15 = (f32[96,1024]{1,0:T(8,128)S(1)}, f32[96,1024]{1,0:T(8,128)S(1)}, u32[]{:S(2)}, u32[]{:S(2)}) collective-permute-start(f32[96,1024]{1,0:T(8,128)S(1)} %get-tuple-element.86), channel_id=1, source_target_pairs={{0,2},{1,3},{2,0},{3,1},{4,6},{5,7},{6,4},{7,5},{8,10},{9,11},{10,... | collective-permute-start | bytes 1179656 | tf_op jit(solution)/shard_map/ppermute | solution.py:217
  42.3 8.2 %collective-permute-start.17 = (f32[64,1024]{1,0:T(8,128)S(1)}, f32[64,1024]{1,0:T(8,128)S(1)}, u32[]{:S(2)}, u32[]{:S(2)}) collective-permute-start(f32[64,1024]{1,0:T(8,128)S(1)} %get-tuple-element.90), channel_id=1, source_target_pairs={{0,8},{1,9},{2,10},{3,11},{4,12},{5,13},{6,14},{7,15},{8,0},{9,1},... | collective-permute-start | bytes 786440 | tf_op jit(solution)/shard_map/ppermute | solution.py:217
  50.5 14.3 %collective-permute-start.21 = (f32[64,1024]{1,0:T(8,128)S(1)}, f32[64,1024]{1,0:T(8,128)S(1)}, u32[]{:S(2)}, u32[]{:S(2)}) collective-permute-start(f32[64,1024]{1,0:T(8,128)S(1)} %shard_map.66), channel_id=1, source_target_pairs={{0,16},{1,17},{2,18},{3,19},{4,20},{5,21},{6,22},{7,23},{8,24},{9,... | collective-permute-start | bytes 786440 | tf_op jit(solution)/shard_map/ppermute | solution.py:217
  52.1 12.7 %collective-permute-start.20 = (f32[64,1024]{1,0:T(8,128)S(1)}, f32[64,1024]{1,0:T(8,128)S(1)}, u32[]{:S(2)}, u32[]{:S(2)}) collective-permute-start(f32[64,1024]{1,0:T(8,128)S(1)} %get-tuple-element.96), channel_id=1, source_target_pairs={{0,8},{1,9},{2,10},{3,11},{4,12},{5,13},{6,14},{7,15},{8,0},{9,1},... | collective-permute-start | bytes 786440 | tf_op jit(solution)/shard_map/ppermute | solution.py:217
  53.7 11.1 %collective-permute-start.18 = (f32[96,1024]{1,0:T(8,128)S(1)}, f32[96,1024]{1,0:T(8,128)S(1)}, u32[]{:S(2)}, u32[]{:S(2)}) collective-permute-start(f32[96,1024]{1,0:T(8,128)S(1)} %get-tuple-element.93), channel_id=1, source_target_pairs={{0,1},{1,0},{2,3},{3,2},{4,5},{5,4},{6,7},{7,6},{8,9},{9,8},{10,11... | collective-permute-start | bytes 1179656 | tf_op jit(solution)/shard_map/ppermute | solution.py:217
  55.1 9.7 %collective-permute-start.19 = (f32[96,1024]{1,0:T(8,128)S(1)}, f32[96,1024]{1,0:T(8,128)S(1)}, u32[]{:S(2)}, u32[]{:S(2)}) collective-permute-start(f32[96,1024]{1,0:T(8,128)S(1)} %get-tuple-element.94), channel_id=1, source_target_pairs={{0,2},{1,3},{2,0},{3,1},{4,6},{5,7},{6,4},{7,5},{8,10},{9,11},{10,... | collective-permute-start | bytes 1179656 | tf_op jit(solution)/shard_map/ppermute | solution.py:217

commit v5 on v4

--- a/solution.py
+++ b/solution.py
@@ -11,6 +11,8 @@
 f32 = jnp.float32
 bf16 = jnp.bfloat16
 AXES = ("pb", "pa")
+X, Y, C, Z1, Z2 = 1, 2, 4, 8, 16
+EARLY = 2
 
 
 def call(kernel, outs, flops, *args, kept=True):
@@ -88,52 +90,54 @@
     return mm(o, pl_[...], ((1,), (0,))) + mm(o, ph[...], ((1,), (0,)))
 
 
+def write_scores(et, stats, p, q, pos, first, new=False):
+    st = product(p, q)
+    e = jnp.exp(st)
+    et[...] = e
+    total = jnp.sum(e, axis=0, keepdims=True)
+    spos = jnp.sum(jnp.where(onehot(pos, st.shape, first), st, 0.0), axis=0, keepdims=True)
+    if new:
+        stats[...] = jnp.zeros(stats.shape, f32)
+        stats[0:1], stats[1:2] = total, spos
+    else:
+        stats[0:1] += total
+        stats[1:2] += spos
+
+
 def first_scores_kernel(*refs):
-    qh0, ql0, ph0, pl0, x, y, *ps, pos, et, stats, qh, ql, ph, pl_, v = refs
+    qh0, ql0, ph0, pl0, x, y, z1, z2, c0, c1, c2, pos, et, stats, qh, ql, ph1, pl1, ph2, pl2, v = refs
     load([(qh0, ql0), x, y], qh, ql)
-    load([(ph0, pl0), *ps], ph, pl_)
-    st = product((ph, pl_), (qh, ql))
-    write_stats(stats, et, st, pos[:, : st.shape[1]], 0)
-    v[...] = positives(pos, ph, pl_, 0)
+    load([(ph0, pl0), z1, z2, c0], ph1, pl1)
+    load([c1, c2], ph2, pl2)
+    m = ph1.shape[0]
+    write_scores(et.at[:m], stats, (ph1, pl1), (qh, ql), pos[:, : et.shape[1]], 0, True)
+    write_scores(et.at[m:], stats, (ph2, pl2), (qh, ql), pos[:, : et.shape[1]], m)
+    v[...] = positives(pos, ph1, pl1, 0)
+
+
+def rest_scores_kernel(da, db, c3, z3, pos, et1, stats1, qh1, ql1, ph1, pl1, phc, plc, et, stats, qh, ql, ph2, pl2):
+    n, m, k, r = qh1.shape[0], ph1.shape[0], phc.shape[0], et1.shape[0]
+    qh[:n], ql[:n] = qh1[...], ql1[...]
+    ph2[:k], pl2[:k] = phc[...], plc[...]
+    load([da, db], qh.at[n:], ql.at[n:])
+    load([c3, z3], ph2.at[k:], pl2.at[k:])
+    et[:r, :n] = et1[...]
+    stats[:, :n] = stats1[...]
+    last = (qh.at[n:], ql.at[n:])
+    write_scores(et.at[:m, n:], stats.at[:, n:], (ph1, pl1), last, pos[:, n:], 0, True)
+    write_scores(et.at[m:r, n:], stats.at[:, n:], (phc, plc), last, pos[:, n:], m)
+    write_scores(et.at[r:], stats, (ph2.at[k:], pl2.at[k:]), (qh, ql), pos[...], r)
 
 
 def all_scores_kernel(q, p, pos, et, stats, qh, ql, ph, pl_):
     load([q], qh, ql)
     load([p], ph, pl_)
-    write_stats(stats, et, product((ph, pl_), (qh, ql)), pos[...], 0)
-
-
-def write_stats(stats, et, st, pos, first):
-    e = jnp.exp(st)
-    et[...] = e
-    stats[...] = jnp.zeros(stats.shape, f32)
-    stats[0:1] = jnp.sum(e, axis=0, keepdims=True)
-    stats[1:2] = jnp.sum(jnp.where(onehot(pos, st.shape, first), st, 0.0), axis=0, keepdims=True)
-
-
-def rest_scores_kernel(n_q, n_p, *refs):
-    qs, ps = refs[:n_q], refs[n_q : n_q + n_p]
-    pos, et1, stats1, qh1, ql1, ph1, pl1, v1, et, stats, qh, ql, ph, pl_ = refs[n_q + n_p :]
-    n, m = qh1.shape[0], ph1.shape[0]
-    del v1
-    qh[:n] = qh1[...]
-    ql[:n] = ql1[...]
-    load(qs, qh.at[n:], ql.at[n:])
-    load(ps, ph, pl_)
-    top = product((ph1, pl1), (qh.at[n:], ql.at[n:]))
-    low = product((ph, pl_), (qh, ql))
-    e_top, e_low = jnp.exp(top), jnp.exp(low)
-    et[:m, :n] = et1[...]
-    et[:m, n:] = e_top
-    et[m:, :] = e_low
-    o_top, o_low = onehot(pos[:, n:], top.shape, 0), onehot(pos[...], low.shape, m)
-    sum_low = jnp.sum(e_low, axis=0, keepdims=True)
-    pos_low = jnp.sum(jnp.where(o_low, low, 0.0), axis=0, keepdims=True)
-    stats[...] = jnp.zeros(stats.shape, f32)
-    stats[0:1, :n] = stats1[0:1] + sum_low[:, :n]
-    stats[1:2, :n] = stats1[1:2] + pos_low[:, :n]
-    stats[0:1, n:] = jnp.sum(e_top, axis=0, keepdims=True) + sum_low[:, n:]
-    stats[1:2, n:] = jnp.sum(jnp.where(o_top, top, 0.0), axis=0, keepdims=True) + pos_low[:, n:]
+    write_scores(et, stats, (ph, pl_), (qh, ql), pos[...], 0, True)
+
+
+def others(et, pos, first, n):
+    rows = et[first : first + n]
+    return split(jnp.where(onehot(pos[...], rows.shape, first), 0.0, rows).T)
 
 
 def unscaled_kernel(n_p, et, pos, *refs):
@@ -141,7 +145,7 @@
     at = 0
     for ph, pl_ in zip(ps[:n_p], ps[n_p:]):
         n = ph.shape[0]
-        part_u = mm3(split(et[at : at + n].T), (ph[...], pl_[...]), ((1,), (0,)))
+        part_u = mm3(others(et, pos, at, n), (ph[...], pl_[...]), ((1,), (0,)))
         u[...] = part_u if at == 0 else u[...] + part_u
         at += n
     v[...] = positives(pos, ph, pl_, at - n) + (v1[0][...] if v1 else 0.0)
@@ -151,12 +155,14 @@
     stats = refs[:n_stats]
     u, v, losses, *outs = refs[n_stats:]
     both = combine(stats)
-    losses[...] = jnp.log(both[0:1]) - both[1:2]
-    inv = (1.0 / both).T[:, 0:1]
+    total, spos = both[0:1], both[1:2]
+    losses[...] = jnp.log(total) - spos
+    weight = 1.0 / total
+    scales = jnp.concatenate([weight, jnp.exp(spos) * weight - 1.0, both[2:]], axis=0).T
     for out, ranges in zip(outs, cuts):
         at = 0
         for a, b in ranges:
-            out[at : at + b - a] = u[a:b] * inv[a:b] - v[a:b]
+            out[at : at + b - a] = u[a:b] * scales[a:b, 0:1] + v[a:b] * scales[a:b, 1:2]
             at += b - a
 
 
@@ -217,10 +223,6 @@
     return lax.ppermute(x, AXES, [(i, i ^ mask) for i in range(n)])
 
 
-X, Y, C, Z1, Z2 = 1, 2, 4, 8, 16
-EARLY = 2
-
-
 def after(x, *others):
     return lax.optimization_barrier((x,) + others)[0]
 
@@ -250,11 +252,11 @@
     da, db = flip(after(x[:h], c0), Y), flip(after(y[h:], c0), X)
     c1 = flip(after(z1, qh0, pos), C)
     c2 = flip(after(z2, c1), C)
-    first = first_scores((qh0, ql0, ph0, pl0, x, y, z1, z2, c0), pos)
+    *first, v1 = first_scores(qh0, ql0, ph0, pl0, x, y, z1, z2, c0, c1, c2, pos)
     c3 = flip(z3, C)
-
-    et, stats, qh, ql, ph2, pl2 = rest_scores([da, db], [c1, c2, c3, z3], pos, first)
-    ph1, pl1, v1 = first[4:]
+    et, stats, qh, ql, ph2, pl2 = rest_scores(da, db, c3, z3, pos, *first)
+    ph1, pl1 = first[4:6]
+
     both = [stats, flip(stats, X), flip(stats, Y), flip(stats, X + Y)]
     u, v = unscaled(et, pos, (ph1, ph2), (pl1, pl2), (v1,))
 
@@ -302,31 +304,23 @@
     return [((p, q), f32), ((8, q), f32), ((q, d), bf16), ((q, d), bf16), ((p, d), bf16), ((p, d), bf16)]
 
 
-def first_scores(parts, pos):
-    qh0, _, ph0, _, x, y, *ps = parts
-    q, p, d = rows([qh0, x, y]), rows([ph0] + ps), x.shape[1]
-    return call(
-        first_scores_kernel, scores_outs(q, p, d) + [((pos.shape[1], d), f32)], 10 * q * p * d, *parts, pos
-    )
+def first_scores(qh0, ql0, ph0, pl0, x, y, z1, z2, c0, c1, c2, pos):
+    q, p, d = rows([qh0, x, y]), rows([ph0, z1, z2, c0]), x.shape[1]
+    k = rows([c1, c2])
+    outs = [((p + k, q), f32), ((8, q), f32)] + [((n, d), bf16) for n in (q, q, p, p, k, k)] + [((pos.shape[1], d), f32)]
+    return call(first_scores_kernel, outs, 10 * q * p * d, qh0, ql0, ph0, pl0, x, y, z1, z2, c0, c1, c2, pos)
+
+
+def rest_scores(da, db, c3, z3, pos, et1, stats1, qh1, ql1, ph1, pl1, phc, plc):
+    q, p, d = rows([qh1, da, db]), rows([phc, c3, z3]), da.shape[1]
+    outs = [((rows([ph1]) + p, q), f32), ((8, q), f32)] + [((n, d), bf16) for n in (q, q, p, p)]
+    args = (da, db, c3, z3, pos, et1, stats1, qh1, ql1, ph1, pl1, phc, plc)
+    return call(rest_scores_kernel, outs, 6 * q * p * d, *args)
 
 
 def all_scores(q, p, pos):
     work = 6 * q.size * p.shape[0]
     return call(all_scores_kernel, scores_outs(q.shape[0], p.shape[0], q.shape[1]), work, q, p, pos)
-
-
-def rest_scores(q_parts, p_parts, pos, first):
-    p1, q1 = first[0].shape
-    q, p, d = q1 + rows(q_parts), rows(p_parts), q_parts[0].shape[1]
-    return call(
-        functools.partial(rest_scores_kernel, len(q_parts), len(p_parts)),
-        [((p1 + p, q), f32)] + scores_outs(q, p, d)[1:],
-        6 * q * p * d,
-        *q_parts,
-        *p_parts,
-        pos,
-        *first,
-    )
 
 
 def unscaled(et, pos, hi, lo, v=()):

time: 66.3 us -> 65.5 us (0.988)
  waiting for transfers between devices: 27.9 us -> 23.7 us
  starting transfers between devices: 22.6 us -> 25.3 us
    ppermute x22, waiting for transfers between devices: 27.9 us -> 23.7 us  [flip(): return lax.ppermute(x, AXES, [(i, i ^ mask) for i in range(n)])]
    ppermute x22, starting transfers between devices: 22.6 us -> 25.3 us  [flip(): return lax.ppermute(x, AXES, [(i, i ^ mask) for i in range(n)])]
  transfers between devices with their start and end apart: 22 -> 22, of which waited for: 8 -> 9; matrix products, arithmetic and copies ran while one was open for 4% -> 4% of each run, Pallas kernels for 9% -> 10%
where the time goes in v5:
time: 65.5 us; the launch traced here: 65.2 us
  starting transfers between devices  25.3 us (39%)
  waiting for transfers between devices  23.7 us (36%)
  Pallas kernels  10.5 us (16%)
  local copies, waits for them, and re-layouts  2.87 us (4%)
  other arithmetic  2.03 us (3%)
  between operations  0.77 us (1%)
    ppermute x22, starting transfers between devices, flip(): return lax.ppermute(x, AXES, [(i, i ^ mask) for i in range(n)])  25.3 us
    ppermute x22, waiting for transfers between devices, flip(): return lax.ppermute(x, AXES, [(i, i ^ mask) for i in range(n)])  23.7 us
    pallas_call x11, Pallas kernels, call(): pl.pallas_call(kernel, out_shape=[pltpu.VMEM(s, d) if kept else jax.Shape...  10.5 us
    unnamed x4, local copies, waits for them, and re-layouts  1.99 us
  transfers between devices with their start and end apart: 22, of which 9 were waited for; matrix products, arithmetic and copies ran while one was open for 4% of the time, Pallas kernels for 10%

profile of v5, /device:TPU:0, one launch (start us, length us, event | category | flops | bytes accessed | tf_op | source)
XLA Modules:
  0.0 65.2 jit_solution(1437951376947962063)
XLA Ops:
  0.6 4.1 %collective-permute-start.5 = (f32[64,1024]{1,0:T(8,128)}, f32[64,1024]{1,0:T(8,128)S(1)}, u32[]{:S(2)}, u32[]{:S(2)}) collective-permute-start(f32[64,1024]{1,0:T(8,128)} %passages.1), channel_id=1, source_target_pairs={{0,16},{1,17},{2,18},{3,19},{4,20},{5,21},{6,22},{7,23},{8,24},{9,... | collective-permute-start | bytes 786440 | tf_op jit(solution)/shard_map/ppermute | solution.py:223
  4.7 1.6 %collective-permute-start.8 = (f32[64,1024]{1,0:T(8,128)}, f32[64,1024]{1,0:T(8,128)S(1)}, u32[]{:S(2)}, u32[]{:S(2)}) collective-permute-start(f32[64,1024]{1,0:T(8,128)} %passages.1), channel_id=1, source_target_pairs={{0,8},{1,9},{2,10},{3,11},{4,12},{5,13},{6,14},{7,15},{8,0},{9,1},... | collective-permute-start | bytes 786440 | tf_op jit(solution)/shard_map/ppermute | solution.py:223
  6.3 1.5 %collective-permute-start = (f32[128,1024]{1,0:T(8,128)}, f32[128,1024]{1,0:T(8,128)S(1)}, u32[]{:S(2)}, u32[]{:S(2)}) collective-permute-start(f32[128,1024]{1,0:T(8,128)} %queries.1), channel_id=1, source_target_pairs={{0,1},{1,0},{2,3},{3,2},{4,5},{5,4},{6,7},{7,6},{8,9},{9,8},{10,11... | collective-permute-start | bytes 1572872 | tf_op jit(solution)/shard_map/ppermute | solution.py:223
  7.8 1.5 %collective-permute-start.3 = (f32[128,1024]{1,0:T(8,128)}, f32[128,1024]{1,0:T(8,128)S(1)}, u32[]{:S(2)}, u32[]{:S(2)}) collective-permute-start(f32[128,1024]{1,0:T(8,128)} %queries.1), channel_id=1, source_target_pairs={{0,2},{1,3},{2,0},{3,1},{4,6},{5,7},{6,4},{7,5},{8,10},{9,11},{10,... | collective-permute-start | bytes 1572872 | tf_op jit(solution)/shard_map/ppermute | solution.py:223
  9.3 0.8 %slice_bitcast_fusion.3 = (s32[1,128]{1,0:T(1,128)S(1)}, s32[1,128]{1,0:T(1,128)S(1)}, s32[1,128]{1,0:T(1,128)S(1)}, s32[1,128]{1,0:T(1,128)S(1)}) fusion(s32[512]{0:T(512)} %param.5), kind=kLoop, calls=%fused_computation.46 | loop fusion | bytes 4096 | tf_op jit(solution)/shard_map/slice | solution.py:231
  10.2 0.7 %bitcast_select_fusion.2 = s32[4,128]{1,0:T(4,128)S(1)} fusion(s32[512]{0:T(512)} %param.5, pred[]{:T(512)S(6)} %ne.67, s32[1,128]{1,0:T(1,128)S(1)} %get-tuple-element.112, s32[1,128]{1,0:T(1,128)S(1)} %get-tuple-element.113, s32[1,128]{1,0:T(1,128)S(1)} %get-tuple-element.114, s32[1,128]{1,0:T(1,128)S(1)} %get-tuple-element.111), kind=kLoop, calls=%fused_computation.33 | loop fusion | flops 2048 | bytes 6145 | tf_op jit(solution)/shard_map/jit(_where)/select_n | solution.py:231
  10.9 1.0 %copy-done = f32[128,1024]{1,0:T(8,128)S(1)} copy-done((f32[128,1024]{1,0:T(8,128)S(1)}, f32[128,1024]{1,0:T(8,128)}, u32[]{:S(2)}) %copy-start) | copy-done | bytes 524312
  11.9 0.9 %copy-done.1 = f32[64,1024]{1,0:T(8,128)S(1)} copy-done((f32[64,1024]{1,0:T(8,128)S(1)}, f32[64,1024]{1,0:T(8,128)}, u32[]{:S(2)}) %copy-start.1) | copy-done | bytes 262168
  13.1 0.7 %fusion.7 = s32[512]{0:T(512)S(1)} fusion(s32[512]{0:T(512)} %param.5, s32[2,128]{1,0:T(2,128)S(1)} %get-tuple-element.110, s32[2,128]{1,0:T(2,128)S(1)} %get-tuple-element.109, s32[]{:T(128)S(6)} %axis_index.25, s32[]{:T(128)S(6)} %axis_index.22, pred[]{:T(512)S(6)} %ne.67, pred[]{:T(512)S(6)} %ne.66, s32[1,128]{1,0:T(1,128)S(1)} %get-tuple-element.112, ...), kind=kLoop, calls=%fused_computation.23 | loop fusion | flops 38912 | bytes 8202 | tf_op jit(solution)/shard_map/jit(_where)/select_n | solution.py:244
  13.8 3.3 %collective-permute-done.8.refs_6_ = f32[64,1024]{1,0:T(8,128)S(1)} collective-permute-done((f32[64,1024]{1,0:T(8,128)}, f32[64,1024]{1,0:T(8,128)S(1)}, u32[]{:S(2)}, u32[]{:S(2)}) %collective-permute-start.8) | collective-permute-done | bytes 262176 | tf_op jit(solution)/shard_map/ppermute | solution.py:223
  17.7 1.5 %collective-permute-start.6 = (f32[64,1024]{1,0:T(8,128)S(1)}, f32[64,1024]{1,0:T(8,128)S(1)}, u32[]{:S(2)}, u32[]{:S(2)}) collective-permute-start(f32[64,1024]{1,0:T(8,128)S(1)} %collective-permute-done.5.refs_7_), channel_id=1, source_target_pairs={{0,8},{1,9},{2,10},{3,11},{4,12},{5,13},{6,14},{7,15},{8,0},{9,1},... | collective-permute-start | bytes 786440 | tf_op jit(solution)/shard_map/ppermute | solution.py:223
  19.7 1.6 %collective-permute-start.2 = (f32[64,1024]{1,0:T(8,128)S(1)}, f32[64,1024]{1,0:T(8,128)S(1)}, u32[]{:S(2)}, u32[]{:S(2)}) collective-permute-start(f32[64,1024]{1,0:T(8,128)S(1)} %slice.84), channel_id=1, source_target_pairs={{0,2},{1,3},{2,0},{3,1},{4,6},{5,7},{6,4},{7,5},{8,10},{9,11},{10,... | collective-permute-start | bytes 786440 | tf_op jit(solution)/shard_map/ppermute | solution.py:223
  21.3 1.6 %collective-permute-start.4 = (f32[64,1024]{1,0:T(8,128)S(1)}, f32[64,1024]{1,0:T(8,128)S(1)}, u32[]{:S(2)}, u32[]{:S(2)}) collective-permute-start(f32[64,1024]{1,0:T(8,128)S(1)} %slice.85), channel_id=1, source_target_pairs={{0,1},{1,0},{2,3},{3,2},{4,5},{5,4},{6,7},{7,6},{8,9},{9,8},{10,11... | collective-permute-start | bytes 786440 | tf_op jit(solution)/shard_map/ppermute | solution.py:223
  22.8 3.1 %collective-permute-done.6.z3 = f32[64,1024]{1,0:T(8,128)S(1)} collective-permute-done((f32[64,1024]{1,0:T(8,128)S(1)}, f32[64,1024]{1,0:T(8,128)S(1)}, u32[]{:S(2)}, u32[]{:S(2)}) %collective-permute-start.6) | collective-permute-done | bytes 262176 | tf_op jit(solution)/shard_map/ppermute | solution.py:223
  25.9 2.3 %shard_map.59 = (f32[384,384]{1,0:T(8,128)S(1)}, f32[8,384]{1,0:T(8,128)S(1)}, bf16[384,1024]{1,0:T(8,128)(2,1)S(1)}, bf16[384,1024]{1,0:T(8,128)(2,1)S(1)}, bf1...) custom-call(bf16[128,1024]{1,0:T(8,128)(2,1)S(1)} %get-tuple-element, ...), custom_call_target="tpu_custom_call" | custom-call | flops 1006632960 | bytes 8388608 | tf_op jit(solution)/shard_map/pallas_call | solution.py:19
  28.2 1.1 %collective-permute-done.4.db = f32[64,1024]{1,0:T(8,128)S(1)} collective-permute-done((f32[64,1024]{1,0:T(8,128)S(1)}, f32[64,1024]{1,0:T(8,128)S(1)}, u32[]{:S(2)}, u32[]{:S(2)}) %collective-permute-start.4) | collective-permute-done | bytes 262176 | tf_op jit(solution)/shard_map/ppermute | solution.py:223
  29.3 1.6 %shard_map.60 = (f32[512,512]{1,0:T(8,128)S(1)}, f32[8,512]{1,0:T(8,128)S(1)}, bf16[512,1024]{1,0:T(8,128)(2,1)S(1)}, bf16[512,1024]{1,0:T(8,128)(2,1)S(1)}, bf1...) custom-call(f32[64,1024]{1,0:T(8,128)S(1)} %collective-permute-done.2.da, ...), custom_call_target="tpu_custom_call" | custom-call | flops 805306368 | bytes 8388608 | tf_op jit(solution)/shard_map/pallas_call | solution.py:19
  30.9 1.5 %collective-permute-start.13 = (f32[8,512]{1,0:T(8,128)S(1)}, f32[8,512]{1,0:T(8,128)S(1)}, u32[]{:S(2)}, u32[]{:S(2)}) collective-permute-start(f32[8,512]{1,0:T(8,128)S(1)} %get-tuple-element.70.refs_0_), channel_id=1, source_target_pairs={{0,3},{1,2},{2,1},{3,0},{4,7},{5,6},{6,5},{7,4},{8,11},{9,10},{10,... | collective-permute-start | bytes 49160 | tf_op jit(solution)/shard_map/ppermute | solution.py:223
  32.4 1.5 %collective-permute-start.12 = (f32[8,512]{1,0:T(8,128)S(1)}, f32[8,512]{1,0:T(8,128)S(1)}, u32[]{:S(2)}, u32[]{:S(2)}) collective-permute-start(f32[8,512]{1,0:T(8,128)S(1)} %get-tuple-element.70.refs_0_), channel_id=1, source_target_pairs={{0,2},{1,3},{2,0},{3,1},{4,6},{5,7},{6,4},{7,5},{8,10},{9,11},{10,... | collective-permute-start | bytes 49160 | tf_op jit(solution)/shard_map/ppermute | solution.py:223
  34.5 2.4 %shard_map.61 = (f32[512,1024]{1,0:T(8,128)S(1)}, f32[512,1024]{1,0:T(8,128)S(1)}) custom-call(f32[512,512]{1,0:T(8,128)S(1)} %get-tuple-element.79.et.refs_4_, s32[1,512]{1,0:T(1,128)S(1)} %bitcast.35, bf16[256,1024]{1,0:T(8,128)(2,1)S(1)} %get-tuple-element.66.ph1.refs_0_, bf16[256,1024]{1,0:T(8,128)(2,1)S(1)} %get-tuple-element.72.refs_1_, ...), custom_call_target="tpu_custom_call" | custom-call | flops 2147483648 | bytes 8388608 | tf_op jit(solution)/shard_map/pallas_call | solution.py:19
  36.9 0.8 %collective-permute-done.11.refs_1_ = f32[8,512]{1,0:T(8,128)S(1)} collective-permute-done((f32[8,512]{1,0:T(8,128)S(1)}, f32[8,512]{1,0:T(8,128)S(1)}, u32[]{:S(2)}, u32[]{:S(2)}) %collective-permute-start.11) | collective-permute-done | bytes 16416 | tf_op jit(solution)/shard_map/ppermute | solution.py:223
  37.7 1.0 %shard_map.62 = f32[256,1024]{1,0:T(8,128)S(1)} custom-call(f32[8,512]{1,0:T(8,128)S(1)} %get-tuple-element.70.refs_0_, f32[8,512]{1,0:T(8,128)S(1)} %collective-permute-done.11.refs_1_, f32[8,512]{1,0:T(8,128)S(1)} %collective-permute-done.12.refs_2_, f32[8,512]{1,0:T(8,128)S(1)} %collective-permute-done.13.refs_3_, ...), custom_call_target="tpu_custom_call" | custom-call | flops 805306368 | bytes 8388608 | tf_op jit(solution)/shard_map/pallas_call | solution.py:19
  38.8 1.0 %shard_map.63 = (f32[192,1024]{1,0:T(8,128)S(1)}, f32[64,1024]{1,0:T(8,128)S(1)}) custom-call(f32[8,512]{1,0:T(8,128)S(1)} %get-tuple-element.70.refs_0_, f32[8,512]{1,0:T(8,128)S(1)} %collective-permute-done.11.refs_1_, f32[8,512]{1,0:T(8,128)S(1)} %collective-permute-done.12.refs_2_, f32[8,512]{1,0:T(8,128)S(1)} %collective-permute-done.13.refs_3_, ...), custom_call_target="tpu_custom_call" | custom-call | flops 805306368 | bytes 8388608 | tf_op jit(solution)/shard_map/pallas_call | solution.py:19
  40.3 0.8 %collective-permute-start.14 = (f32[96,1024]{1,0:T(8,128)S(1)}, f32[96,1024]{1,0:T(8,128)S(1)}, u32[]{:S(2)}, u32[]{:S(2)}) collective-permute-start(f32[96,1024]{1,0:T(8,128)S(1)} %get-tuple-element.89), channel_id=1, source_target_pairs={{0,1},{1,0},{2,3},{3,2},{4,5},{5,4},{6,7},{7,6},{8,9},{9,8},{10,11... | collective-permute-start | bytes 1179656 | tf_op jit(solution)/shard_map/ppermute | solution.py:223
  41.7 1.5 %collective-permute-start.17 = (f32[64,1024]{1,0:T(8,128)S(1)}, f32[64,1024]{1,0:T(8,128)S(1)}, u32[]{:S(2)}, u32[]{:S(2)}) collective-permute-start(f32[64,1024]{1,0:T(8,128)S(1)} %get-tuple-element.94), channel_id=1, source_target_pairs={{0,8},{1,9},{2,10},{3,11},{4,12},{5,13},{6,14},{7,15},{8,0},{9,1},... | collective-permute-start | bytes 786440 | tf_op jit(solution)/shard_map/ppermute | solution.py:223
  43.2 6.8 %collective-permute-done.17.b = f32[64,1024]{1,0:T(8,128)S(1)} collective-permute-done((f32[64,1024]{1,0:T(8,128)S(1)}, f32[64,1024]{1,0:T(8,128)S(1)}, u32[]{:S(2)}, u32[]{:S(2)}) %collective-permute-start.17) | collective-permute-done | bytes 262176 | tf_op jit(solution)/shard_map/ppermute | solution.py:223
  50.0 1.9 %collective-permute-start.21 = (f32[64,1024]{1,0:T(8,128)S(1)}, f32[64,1024]{1,0:T(8,128)S(1)}, u32[]{:S(2)}, u32[]{:S(2)}) collective-permute-start(f32[64,1024]{1,0:T(8,128)S(1)} %shard_map.66), channel_id=1, source_target_pairs={{0,16},{1,17},{2,18},{3,19},{4,20},{5,21},{6,22},{7,23},{8,24},{9,... | collective-permute-start | bytes 786440 | tf_op jit(solution)/shard_map/ppermute | solution.py:223
  51.8 1.4 %collective-permute-start.20 = (f32[64,1024]{1,0:T(8,128)S(1)}, f32[64,1024]{1,0:T(8,128)S(1)}, u32[]{:S(2)}, u32[]{:S(2)}) collective-permute-start(f32[64,1024]{1,0:T(8,128)S(1)} %get-tuple-element.100), channel_id=1, source_target_pairs={{0,8},{1,9},{2,10},{3,11},{4,12},{5,13},{6,14},{7,15},{8,0},{9,1},... | collective-permute-start | bytes 786440 | tf_op jit(solution)/shard_map/ppermute | solution.py:223
  53.3 1.4 %collective-permute-start.18 = (f32[96,1024]{1,0:T(8,128)S(1)}, f32[96,1024]{1,0:T(8,128)S(1)}, u32[]{:S(2)}, u32[]{:S(2)}) collective-permute-start(f32[96,1024]{1,0:T(8,128)S(1)} %get-tuple-element.97), channel_id=1, source_target_pairs={{0,1},{1,0},{2,3},{3,2},{4,5},{5,4},{6,7},{7,6},{8,9},{9,8},{10,11... | collective-permute-start | bytes 1179656 | tf_op jit(solution)/shard_map/ppermute | solution.py:223
  55.8 6.6 %collective-permute-done.20.r1 = f32[64,1024]{1,0:T(8,128)S(1)} collective-permute-done((f32[64,1024]{1,0:T(8,128)S(1)}, f32[64,1024]{1,0:T(8,128)S(1)}, u32[]{:S(2)}, u32[]{:S(2)}) %collective-permute-start.20) | collective-permute-done | bytes 262176 | tf_op jit(solution)/shard_map/ppermute | solution.py:223
  62.3 1.5 %collective-permute-done.21.r2 = f32[64,1024]{1,0:T(8,128)S(1)} collective-permute-done((f32[64,1024]{1,0:T(8,128)S(1)}, f32[64,1024]{1,0:T(8,128)S(1)}, u32[]{:S(2)}, u32[]{:S(2)}) %collective-permute-start.21) | collective-permute-done | bytes 262176 | tf_op jit(solution)/shard_map/ppermute | solution.py:223
  63.9 1.3 %shard_map.68 = (f32[128,1024]{1,0:T(8,128)}, f32[64,1024]{1,0:T(8,128)}) custom-call(f32[128,1024]{1,0:T(8,128)S(1)} %get-tuple-element.84.qn, f32[128,128]{1,0:T(8,128)S(1)} %get-tuple-element.85.qs, f32[64,1024]{1,0:T(8,128)S(1)} %get-tuple-element.86.pn, f32[64,128]{1,0:T(8,128)S(1)} %get-tuple-element.87.ps, f32[128,1024]{1,0:T(8,128)S(1)} %get-tuple-element.88.own, ...), custom_call_target="tpu_custom_call" | custom-call | flops 1572864 | bytes 8388608 | tf_op jit(solution)/shard_map/pallas_call | solution.py:19
  (37 shorter events, 4.3 us)
Async XLA Ops:
  0.6 17.0 %collective-permute-start.5 = (f32[64,1024]{1,0:T(8,128)}, f32[64,1024]{1,0:T(8,128)S(1)}, u32[]{:S(2)}, u32[]{:S(2)}) collective-permute-start(f32[64,1024]{1,0:T(8,128)} %passages.1), channel_id=1, source_target_pairs={{0,16},{1,17},{2,18},{3,19},{4,20},{5,21},{6,22},{7,23},{8,24},{9,... | collective-permute-start | bytes 786440 | tf_op jit(solution)/shard_map/ppermute | solution.py:223
  4.7 12.4 %collective-permute-start.8 = (f32[64,1024]{1,0:T(8,128)}, f32[64,1024]{1,0:T(8,128)S(1)}, u32[]{:S(2)}, u32[]{:S(2)}) collective-permute-start(f32[64,1024]{1,0:T(8,128)} %passages.1), channel_id=1, source_target_pairs={{0,8},{1,9},{2,10},{3,11},{4,12},{5,13},{6,14},{7,15},{8,0},{9,1},... | collective-permute-start | bytes 786440 | tf_op jit(solution)/shard_map/ppermute | solution.py:223
  6.3 13.3 %collective-permute-start = (f32[128,1024]{1,0:T(8,128)}, f32[128,1024]{1,0:T(8,128)S(1)}, u32[]{:S(2)}, u32[]{:S(2)}) collective-permute-start(f32[128,1024]{1,0:T(8,128)} %queries.1), channel_id=1, source_target_pairs={{0,1},{1,0},{2,3},{3,2},{4,5},{5,4},{6,7},{7,6},{8,9},{9,8},{10,11... | collective-permute-start | bytes 1572872 | tf_op jit(solution)/shard_map/ppermute | solution.py:223
  7.8 13.4 %collective-permute-start.3 = (f32[128,1024]{1,0:T(8,128)}, f32[128,1024]{1,0:T(8,128)S(1)}, u32[]{:S(2)}, u32[]{:S(2)}) collective-permute-start(f32[128,1024]{1,0:T(8,128)} %queries.1), channel_id=1, source_target_pairs={{0,2},{1,3},{2,0},{3,1},{4,6},{5,7},{6,4},{7,5},{8,10},{9,11},{10,... | collective-permute-start | bytes 1572872 | tf_op jit(solution)/shard_map/ppermute | solution.py:223
  10.9 1.0 %copy-start = (f32[128,1024]{1,0:T(8,128)S(1)}, f32[128,1024]{1,0:T(8,128)}, u32[]{:S(2)}) copy-start(f32[128,1024]{1,0:T(8,128)} %queries.1) | copy-start | bytes 1572868
  11.9 0.9 %copy-start.1 = (f32[64,1024]{1,0:T(8,128)S(1)}, f32[64,1024]{1,0:T(8,128)}, u32[]{:S(2)}) copy-start(f32[64,1024]{1,0:T(8,128)} %passages.1) | copy-start | bytes 786436
  17.2 2.0 %collective-permute-start.9 = (f32[64,1024]{1,0:T(8,128)S(1)}, f32[64,1024]{1,0:T(8,128)S(1)}, u32[]{:S(2)}, u32[]{:S(2)}) collective-permute-start(f32[64,1024]{1,0:T(8,128)S(1)} %collective-permute-done.8.refs_6_), channel_id=1, source_target_pairs={{0,4},{1,5},{2,6},{3,7},{4,0},{5,1},{6,2},{7,3},{8,12},{9,13},{10,... | collective-permute-start | bytes 786440 | tf_op jit(solution)/shard_map/ppermute | solution.py:223
  17.2 2.5 %collective-permute-start.1 = (f32[64,1024]{1,0:T(8,128)S(1)}, f32[64,1024]{1,0:T(8,128)S(1)}, u32[]{:S(2)}, u32[]{:S(2)}) collective-permute-start(f32[64,1024]{1,0:T(8,128)S(1)} %copy-done.1), channel_id=1, source_target_pairs={{0,4},{1,5},{2,6},{3,7},{4,0},{5,1},{6,2},{7,3},{8,12},{9,13},{10,... | collective-permute-start | bytes 786440 | tf_op jit(solution)/shard_map/ppermute | solution.py:223
  17.7 8.2 %collective-permute-start.6 = (f32[64,1024]{1,0:T(8,128)S(1)}, f32[64,1024]{1,0:T(8,128)S(1)}, u32[]{:S(2)}, u32[]{:S(2)}) collective-permute-start(f32[64,1024]{1,0:T(8,128)S(1)} %collective-permute-done.5.refs_7_), channel_id=1, source_target_pairs={{0,8},{1,9},{2,10},{3,11},{4,12},{5,13},{6,14},{7,15},{8,0},{9,1},... | collective-permute-start | bytes 786440 | tf_op jit(solution)/shard_map/ppermute | solution.py:223
  19.2 6.7 %collective-permute-start.10 = (f32[64,1024]{1,0:T(8,128)S(1)}, f32[64,1024]{1,0:T(8,128)S(1)}, u32[]{:S(2)}, u32[]{:S(2)}) collective-permute-start(f32[64,1024]{1,0:T(8,128)S(1)} %collective-permute-done.5.refs_7_), channel_id=1, source_target_pairs={{0,4},{1,5},{2,6},{3,7},{4,0},{5,1},{6,2},{7,3},{8,12},{9,13},{10,... | collective-permute-start | bytes 786440 | tf_op jit(solution)/shard_map/ppermute | solution.py:223
  19.7 8.5 %collective-permute-start.2 = (f32[64,1024]{1,0:T(8,128)S(1)}, f32[64,1024]{1,0:T(8,128)S(1)}, u32[]{:S(2)}, u32[]{:S(2)}) collective-permute-start(f32[64,1024]{1,0:T(8,128)S(1)} %slice.84), channel_id=1, source_target_pairs={{0,2},{1,3},{2,0},{3,1},{4,6},{5,7},{6,4},{7,5},{8,10},{9,11},{10,... | collective-permute-start | bytes 786440 | tf_op jit(solution)/shard_map/ppermute | solution.py:223
  21.3 8.1 %collective-permute-start.4 = (f32[64,1024]{1,0:T(8,128)S(1)}, f32[64,1024]{1,0:T(8,128)S(1)}, u32[]{:S(2)}, u32[]{:S(2)}) collective-permute-start(f32[64,1024]{1,0:T(8,128)S(1)} %slice.85), channel_id=1, source_target_pairs={{0,1},{1,0},{2,3},{3,2},{4,5},{5,4},{6,7},{7,6},{8,9},{9,8},{10,11... | collective-permute-start | bytes 786440 | tf_op jit(solution)/shard_map/ppermute | solution.py:223
  25.9 3.4 %collective-permute-start.7 = (f32[64,1024]{1,0:T(8,128)S(1)}, f32[64,1024]{1,0:T(8,128)S(1)}, u32[]{:S(2)}, u32[]{:S(2)}) collective-permute-start(f32[64,1024]{1,0:T(8,128)S(1)} %collective-permute-done.6.z3), channel_id=1, source_target_pairs={{0,4},{1,5},{2,6},{3,7},{4,0},{5,1},{6,2},{7,3},{8,12},{9,13},{10,... | collective-permute-start | bytes 786440 | tf_op jit(solution)/shard_map/ppermute | solution.py:223
  30.9 6.0 %collective-permute-start.13 = (f32[8,512]{1,0:T(8,128)S(1)}, f32[8,512]{1,0:T(8,128)S(1)}, u32[]{:S(2)}, u32[]{:S(2)}) collective-permute-start(f32[8,512]{1,0:T(8,128)S(1)} %get-tuple-element.70.refs_0_), channel_id=1, source_target_pairs={{0,3},{1,2},{2,1},{3,0},{4,7},{5,6},{6,5},{7,4},{8,11},{9,10},{10,... | collective-permute-start | bytes 49160 | tf_op jit(solution)/shard_map/ppermute | solution.py:223
  32.4 4.5 %collective-permute-start.12 = (f32[8,512]{1,0:T(8,128)S(1)}, f32[8,512]{1,0:T(8,128)S(1)}, u32[]{:S(2)}, u32[]{:S(2)}) collective-permute-start(f32[8,512]{1,0:T(8,128)S(1)} %get-tuple-element.70.refs_0_), channel_id=1, source_target_pairs={{0,2},{1,3},{2,0},{3,1},{4,6},{5,7},{6,4},{7,5},{8,10},{9,11},{10,... | collective-permute-start | bytes 49160 | tf_op jit(solution)/shard_map/ppermute | solution.py:223
  34.0 3.7 %collective-permute-start.11 = (f32[8,512]{1,0:T(8,128)S(1)}, f32[8,512]{1,0:T(8,128)S(1)}, u32[]{:S(2)}, u32[]{:S(2)}) collective-permute-start(f32[8,512]{1,0:T(8,128)S(1)} %get-tuple-element.70.refs_0_), channel_id=1, source_target_pairs={{0,1},{1,0},{2,3},{3,2},{4,5},{5,4},{6,7},{7,6},{8,9},{9,8},{10,11... | collective-permute-start | bytes 49160 | tf_op jit(solution)/shard_map/ppermute | solution.py:223
  38.7 2.9 %collective-permute-start.16 = (f32[256,1024]{1,0:T(8,128)S(1)}, f32[256,1024]{1,0:T(8,128)S(1)}, u32[]{:S(2)}, u32[]{:S(2)}) collective-permute-start(f32[256,1024]{1,0:T(8,128)S(1)} %shard_map.62), channel_id=1, source_target_pairs={{0,4},{1,5},{2,6},{3,7},{4,0},{5,1},{6,2},{7,3},{8,12},{9,13},{10,... | collective-permute-start | bytes 3145736 | tf_op jit(solution)/shard_map/ppermute | solution.py:223
  40.3 12.9 %collective-permute-start.14 = (f32[96,1024]{1,0:T(8,128)S(1)}, f32[96,1024]{1,0:T(8,128)S(1)}, u32[]{:S(2)}, u32[]{:S(2)}) collective-permute-start(f32[96,1024]{1,0:T(8,128)S(1)} %get-tuple-element.89), channel_id=1, source_target_pairs={{0,1},{1,0},{2,3},{3,2},{4,5},{5,4},{6,7},{7,6},{8,9},{9,8},{10,11... | collective-permute-start | bytes 1179656 | tf_op jit(solution)/shard_map/ppermute | solution.py:223
  41.1 12.1 %collective-permute-start.15 = (f32[96,1024]{1,0:T(8,128)S(1)}, f32[96,1024]{1,0:T(8,128)S(1)}, u32[]{:S(2)}, u32[]{:S(2)}) collective-permute-start(f32[96,1024]{1,0:T(8,128)S(1)} %get-tuple-element.90), channel_id=1, source_target_pairs={{0,2},{1,3},{2,0},{3,1},{4,6},{5,7},{6,4},{7,5},{8,10},{9,11},{10,... | collective-permute-start | bytes 1179656 | tf_op jit(solution)/shard_map/ppermute | solution.py:223
  41.7 8.2 %collective-permute-start.17 = (f32[64,1024]{1,0:T(8,128)S(1)}, f32[64,1024]{1,0:T(8,128)S(1)}, u32[]{:S(2)}, u32[]{:S(2)}) collective-permute-start(f32[64,1024]{1,0:T(8,128)S(1)} %get-tuple-element.94), channel_id=1, source_target_pairs={{0,8},{1,9},{2,10},{3,11},{4,12},{5,13},{6,14},{7,15},{8,0},{9,1},... | collective-permute-start | bytes 786440 | tf_op jit(solution)/shard_map/ppermute | solution.py:223
  50.0 13.9 %collective-permute-start.21 = (f32[64,1024]{1,0:T(8,128)S(1)}, f32[64,1024]{1,0:T(8,128)S(1)}, u32[]{:S(2)}, u32[]{:S(2)}) collective-permute-start(f32[64,1024]{1,0:T(8,128)S(1)} %shard_map.66), channel_id=1, source_target_pairs={{0,16},{1,17},{2,18},{3,19},{4,20},{5,21},{6,22},{7,23},{8,24},{9,... | collective-permute-start | bytes 786440 | tf_op jit(solution)/shard_map/ppermute | solution.py:223
  51.8 10.5 %collective-permute-start.20 = (f32[64,1024]{1,0:T(8,128)S(1)}, f32[64,1024]{1,0:T(8,128)S(1)}, u32[]{:S(2)}, u32[]{:S(2)}) collective-permute-start(f32[64,1024]{1,0:T(8,128)S(1)} %get-tuple-element.100), channel_id=1, source_target_pairs={{0,8},{1,9},{2,10},{3,11},{4,12},{5,13},{6,14},{7,15},{8,0},{9,1},... | collective-permute-start | bytes 786440 | tf_op jit(solution)/shard_map/ppermute | solution.py:223
  53.3 10.6 %collective-permute-start.18 = (f32[96,1024]{1,0:T(8,128)S(1)}, f32[96,1024]{1,0:T(8,128)S(1)}, u32[]{:S(2)}, u32[]{:S(2)}) collective-permute-start(f32[96,1024]{1,0:T(8,128)S(1)} %get-tuple-element.97), channel_id=1, source_target_pairs={{0,1},{1,0},{2,3},{3,2},{4,5},{5,4},{6,7},{7,6},{8,9},{9,8},{10,11... | collective-permute-start | bytes 1179656 | tf_op jit(solution)/shard_map/ppermute | solution.py:223
  54.7 9.3 %collective-permute-start.19 = (f32[96,1024]{1,0:T(8,128)S(1)}, f32[96,1024]{1,0:T(8,128)S(1)}, u32[]{:S(2)}, u32[]{:S(2)}) collective-permute-start(f32[96,1024]{1,0:T(8,128)S(1)} %get-tuple-element.98), channel_id=1, source_target_pairs={{0,2},{1,3},{2,0},{3,1},{4,6},{5,7},{6,4},{7,5},{8,10},{9,11},{10,... | collective-permute-start | bytes 1179656 | tf_op jit(solution)/shard_map/ppermute | solution.py:223

commit v6 on v5

--- a/solution.py
+++ b/solution.py
@@ -82,12 +82,23 @@
 
 
 def product(p, q):
+    if q[0].shape[0] <= 128:
+        return inv_temp * narrow(p, q)
+    if p[0].shape[0] <= 128:
+        return inv_temp * narrow(q, p).T
     return inv_temp * mm3((p[0][...], p[1][...]), (q[0][...], q[1][...]), ((1,), (1,)))
+
+
+def narrow(a, b):
+    n = b[0].shape[0]
+    bh = b[0][...]
+    both = mm(a[0][...], jnp.concatenate([bh, b[1][...]], axis=0), ((1,), (1,)))
+    return mm(a[1][...], bh, ((1,), (1,))) + both[:, n:] + both[:, :n]
 
 
 def positives(pos, ph, pl_, first):
     o = onehot(pos[...], (ph.shape[0], pos.shape[1]), first).astype(f32).T.astype(bf16)
-    return mm(o, pl_[...], ((1,), (0,))) + mm(o, ph[...], ((1,), (0,)))
+    return mm(o, pl_, ((1,), (0,))) + mm(o, ph, ((1,), (0,)))
 
 
 def write_scores(et, stats, p, q, pos, first, new=False):
@@ -105,28 +116,22 @@
 
 
 def first_scores_kernel(*refs):
-    qh0, ql0, ph0, pl0, x, y, z1, z2, c0, c1, c2, pos, et, stats, qh, ql, ph1, pl1, ph2, pl2, v = refs
+    qh0, ql0, ph0, pl0, x, y, z1, z2, c0, c1, c2, pos, et, stats, qh, ql, ph, pl_, v = refs
     load([(qh0, ql0), x, y], qh, ql)
-    load([(ph0, pl0), z1, z2, c0], ph1, pl1)
-    load([c1, c2], ph2, pl2)
-    m = ph1.shape[0]
-    write_scores(et.at[:m], stats, (ph1, pl1), (qh, ql), pos[:, : et.shape[1]], 0, True)
-    write_scores(et.at[m:], stats, (ph2, pl2), (qh, ql), pos[:, : et.shape[1]], m)
-    v[...] = positives(pos, ph1, pl1, 0)
-
-
-def rest_scores_kernel(da, db, c3, z3, pos, et1, stats1, qh1, ql1, ph1, pl1, phc, plc, et, stats, qh, ql, ph2, pl2):
-    n, m, k, r = qh1.shape[0], ph1.shape[0], phc.shape[0], et1.shape[0]
-    qh[:n], ql[:n] = qh1[...], ql1[...]
-    ph2[:k], pl2[:k] = phc[...], plc[...]
-    load([da, db], qh.at[n:], ql.at[n:])
-    load([c3, z3], ph2.at[k:], pl2.at[k:])
-    et[:r, :n] = et1[...]
+    load([(ph0, pl0), z1, z2, c0, c1, c2], ph, pl_)
+    write_scores(et, stats, (ph, pl_), (qh, ql), pos[:, : et.shape[1]], 0, True)
+    m = 2 * ph.shape[0] // 3
+    v[...] = positives(pos, ph[:m], pl_[:m], 0)
+
+
+def rest_scores_kernel(da, db, c3, z3, pos, stats1, qh1, ql1, ph1, pl1, et_p, et_q, stats, qh, ql, ph2, pl2):
+    n, r = qh1.shape[0], ph1.shape[0]
+    load([c3, z3], ph2, pl2)
     stats[:, :n] = stats1[...]
-    last = (qh.at[n:], ql.at[n:])
-    write_scores(et.at[:m, n:], stats.at[:, n:], (ph1, pl1), last, pos[:, n:], 0, True)
-    write_scores(et.at[m:r, n:], stats.at[:, n:], (phc, plc), last, pos[:, n:], m)
-    write_scores(et.at[r:], stats, (ph2.at[k:], pl2.at[k:]), (qh, ql), pos[...], r)
+    write_scores(et_p, stats.at[:, :n], (ph2, pl2), (qh1, ql1), pos[:, :n], r)
+    load([da, db], qh, ql)
+    write_scores(et_q.at[:r], stats.at[:, n:], (ph1, pl1), (qh, ql), pos[:, n:], 0, True)
+    write_scores(et_q.at[r:], stats.at[:, n:], (ph2, pl2), (qh, ql), pos[:, n:], r)
 
 
 def all_scores_kernel(q, p, pos, et, stats, qh, ql, ph, pl_):
@@ -140,15 +145,20 @@
     return split(jnp.where(onehot(pos[...], rows.shape, first), 0.0, rows).T)
 
 
-def unscaled_kernel(n_p, et, pos, *refs):
-    ps, v1, (u, v) = refs[: 2 * n_p], refs[2 * n_p : -2], refs[-2:]
-    at = 0
-    for ph, pl_ in zip(ps[:n_p], ps[n_p:]):
-        n = ph.shape[0]
-        part_u = mm3(others(et, pos, at, n), (ph[...], pl_[...]), ((1,), (0,)))
-        u[...] = part_u if at == 0 else u[...] + part_u
-        at += n
-    v[...] = positives(pos, ph, pl_, at - n) + (v1[0][...] if v1 else 0.0)
+def unscaled_kernel(et1, et_p, et_q, pos, qh1, ql1, qh2, ql2, ph1, pl1, phz, plz, v1, et, qh, ql, u, v):
+    r, n = et1.shape
+    et[:r, :n], et[r:, :n], et[:, n:] = et1[...], et_p[...], et_q[...]
+    qh[:n], ql[:n], qh[n:], ql[n:] = qh1[...], ql1[...], qh2[...], ql2[...]
+    m = 2 * r // 3
+    ph2, pl2 = (jnp.concatenate([a[m:], b[...]], axis=0) for a, b in ((ph1, phz), (pl1, plz)))
+    first = mm3(others(et, pos, 0, m), (ph1[:m], pl1[:m]), ((1,), (0,)))
+    u[...] = first + mm3(others(et, pos, m, ph2.shape[0]), (ph2, pl2), ((1,), (0,)))
+    v[...] = v1[...] + positives(pos, ph2, pl2, m)
+
+
+def all_unscaled_kernel(et, pos, ph, pl_, u, v):
+    u[...] = mm3(others(et, pos, 0, et.shape[0]), (ph[...], pl_[...]), ((1,), (0,)))
+    v[...] = positives(pos, ph[...], pl_[...], 0)
 
 
 def query_kernel(n_stats, cuts, *refs):
@@ -254,11 +264,12 @@
     c2 = flip(after(z2, c1), C)
     *first, v1 = first_scores(qh0, ql0, ph0, pl0, x, y, z1, z2, c0, c1, c2, pos)
     c3 = flip(z3, C)
-    et, stats, qh, ql, ph2, pl2 = rest_scores(da, db, c3, z3, pos, *first)
-    ph1, pl1 = first[4:6]
+    et1, stats, *first = first
+    et_p, et_q, stats, qh2, ql2, phz, plz = rest_scores(da, db, c3, z3, pos, stats, *first)
 
     both = [stats, flip(stats, X), flip(stats, Y), flip(stats, X + Y)]
-    u, v = unscaled(et, pos, (ph1, ph2), (pl1, pl2), (v1,))
+    qh1, ql1, *p_rest = first
+    et, qh, ql, u, v = unscaled(et1, et_p, et_q, pos, qh1, ql1, qh2, ql2, *p_rest, phz, plz, v1)
 
     def part(k, n):
         return (k * n, k * n + n)
@@ -305,17 +316,16 @@
 
 
 def first_scores(qh0, ql0, ph0, pl0, x, y, z1, z2, c0, c1, c2, pos):
-    q, p, d = rows([qh0, x, y]), rows([ph0, z1, z2, c0]), x.shape[1]
-    k = rows([c1, c2])
-    outs = [((p + k, q), f32), ((8, q), f32)] + [((n, d), bf16) for n in (q, q, p, p, k, k)] + [((pos.shape[1], d), f32)]
+    q, p, d = rows([qh0, x, y]), rows([ph0, z1, z2, c0, c1, c2]), x.shape[1]
+    outs = scores_outs(q, p, d) + [((pos.shape[1], d), f32)]
     return call(first_scores_kernel, outs, 10 * q * p * d, qh0, ql0, ph0, pl0, x, y, z1, z2, c0, c1, c2, pos)
 
 
-def rest_scores(da, db, c3, z3, pos, et1, stats1, qh1, ql1, ph1, pl1, phc, plc):
-    q, p, d = rows([qh1, da, db]), rows([phc, c3, z3]), da.shape[1]
-    outs = [((rows([ph1]) + p, q), f32), ((8, q), f32)] + [((n, d), bf16) for n in (q, q, p, p)]
-    args = (da, db, c3, z3, pos, et1, stats1, qh1, ql1, ph1, pl1, phc, plc)
-    return call(rest_scores_kernel, outs, 6 * q * p * d, *args)
+def rest_scores(da, db, c3, z3, pos, stats1, qh1, ql1, ph1, pl1):
+    q, p, d = rows([da, db]), rows([c3, z3]), da.shape[1]
+    r, n = ph1.shape[0], qh1.shape[0]
+    outs = [((p, n), f32), ((r + p, q), f32), ((8, n + q), f32)] + [((k, d), bf16) for k in (q, q, p, p)]
+    return call(rest_scores_kernel, outs, 6 * q * p * d, da, db, c3, z3, pos, stats1, qh1, ql1, ph1, pl1)
 
 
 def all_scores(q, p, pos):
@@ -323,11 +333,16 @@
     return call(all_scores_kernel, scores_outs(q.shape[0], p.shape[0], q.shape[1]), work, q, p, pos)
 
 
-def unscaled(et, pos, hi, lo, v=()):
+def unscaled(*args):
+    et_q, q, d = args[2], args[3].shape[1], args[4].shape[1]
+    p = et_q.shape[0]
+    outs = [((p, q), f32), ((q, d), bf16), ((q, d), bf16), ((q, d), f32), ((q, d), f32)]
+    return call(unscaled_kernel, outs, 8 * q * p * d, *args)
+
+
+def all_unscaled(et, pos, ph, pl_):
     p, q = et.shape
-    d = hi[0].shape[1]
-    kernel = functools.partial(unscaled_kernel, len(hi))
-    return call(kernel, [((q, d), f32)] * 2, 8 * q * p * d, et, pos, *hi, *lo, *v)
+    return call(all_unscaled_kernel, [((q, ph.shape[1]), f32)] * 2, 8 * q * ph.size, et, pos, ph, pl_)
 
 
 def query_grads(both, u, v, cuts):
@@ -381,7 +396,7 @@
     pos = jnp.where((pos >= 0) & (pos < p_rows), pos, -1).reshape(1, -1)
     et, stats, qh, ql, ph, pl_ = all_scores(q_full, p_full, pos)
     both = [lax.psum(stats, "pa")]
-    u, v = unscaled(et, pos, [ph], [pl_])
+    u, v = all_unscaled(et, pos, ph, pl_)
     losses, gq = query_grads(both, u, v, (((0, q_rows),),))
     (gp,) = passage_grads(both, et, pos, qh, ql, ((0, p_rows),))
     q_part = lax.psum_scatter(gq, "pa", scatter_dimension=0, tiled=True)

time: 65.5 us -> 65.3 us (level)
  transfers between devices with their start and end apart: 22 -> 22, of which waited for: 9 -> 8; matrix products, arithmetic and copies ran while one was open for 4% -> 4% of each run, Pallas kernels for 10% -> 10%
where the time goes in v6:
time: 65.3 us; the launch traced here: 65 us
  starting transfers between devices  25.4 us (39%)
  waiting for transfers between devices  23.5 us (36%)
  Pallas kernels  10.4 us (16%)
  local copies, waits for them, and re-layouts  2.87 us (4%)
  other arithmetic  2.03 us (3%)
  between operations  0.77 us (1%)
    ppermute x22, starting transfers between devices, flip(): return lax.ppermute(x, AXES, [(i, i ^ mask) for i in range(n)])  25.4 us
    ppermute x22, waiting for transfers between devices, flip(): return lax.ppermute(x, AXES, [(i, i ^ mask) for i in range(n)])  23.5 us
    pallas_call x11, Pallas kernels, call(): pl.pallas_call(kernel, out_shape=[pltpu.VMEM(s, d) if kept else jax.Shape...  10.4 us
    unnamed x4, local copies, waits for them, and re-layouts  1.99 us
  transfers between devices with their start and end apart: 22, of which 8 were waited for; matrix products, arithmetic and copies ran while one was open for 4% of the time, Pallas kernels for 10%

profile of v6, /device:TPU:0, one launch (start us, length us, event | category | flops | bytes accessed | tf_op | source)
XLA Modules:
  0.0 65.0 jit_solution(2548762306701867313)
XLA Ops:
  0.6 4.1 %collective-permute-start.5 = (f32[64,1024]{1,0:T(8,128)}, f32[64,1024]{1,0:T(8,128)S(1)}, u32[]{:S(2)}, u32[]{:S(2)}) collective-permute-start(f32[64,1024]{1,0:T(8,128)} %passages.1), channel_id=1, source_target_pairs={{0,16},{1,17},{2,18},{3,19},{4,20},{5,21},{6,22},{7,23},{8,24},{9,... | collective-permute-start | bytes 786440 | tf_op jit(solution)/shard_map/ppermute | solution.py:233
  4.7 1.6 %collective-permute-start.8 = (f32[64,1024]{1,0:T(8,128)}, f32[64,1024]{1,0:T(8,128)S(1)}, u32[]{:S(2)}, u32[]{:S(2)}) collective-permute-start(f32[64,1024]{1,0:T(8,128)} %passages.1), channel_id=1, source_target_pairs={{0,8},{1,9},{2,10},{3,11},{4,12},{5,13},{6,14},{7,15},{8,0},{9,1},... | collective-permute-start | bytes 786440 | tf_op jit(solution)/shard_map/ppermute | solution.py:233
  6.3 1.5 %collective-permute-start = (f32[128,1024]{1,0:T(8,128)}, f32[128,1024]{1,0:T(8,128)S(1)}, u32[]{:S(2)}, u32[]{:S(2)}) collective-permute-start(f32[128,1024]{1,0:T(8,128)} %queries.1), channel_id=1, source_target_pairs={{0,1},{1,0},{2,3},{3,2},{4,5},{5,4},{6,7},{7,6},{8,9},{9,8},{10,11... | collective-permute-start | bytes 1572872 | tf_op jit(solution)/shard_map/ppermute | solution.py:233
  7.8 1.5 %collective-permute-start.3 = (f32[128,1024]{1,0:T(8,128)}, f32[128,1024]{1,0:T(8,128)S(1)}, u32[]{:S(2)}, u32[]{:S(2)}) collective-permute-start(f32[128,1024]{1,0:T(8,128)} %queries.1), channel_id=1, source_target_pairs={{0,2},{1,3},{2,0},{3,1},{4,6},{5,7},{6,4},{7,5},{8,10},{9,11},{10,... | collective-permute-start | bytes 1572872 | tf_op jit(solution)/shard_map/ppermute | solution.py:233
  9.3 0.8 %slice_bitcast_fusion.3 = (s32[1,128]{1,0:T(1,128)S(1)}, s32[1,128]{1,0:T(1,128)S(1)}, s32[1,128]{1,0:T(1,128)S(1)}, s32[1,128]{1,0:T(1,128)S(1)}) fusion(s32[512]{0:T(512)} %param.5), kind=kLoop, calls=%fused_computation.46 | loop fusion | bytes 4096 | tf_op jit(solution)/shard_map/slice | solution.py:241
  10.2 0.7 %bitcast_select_fusion.2 = s32[4,128]{1,0:T(4,128)S(1)} fusion(s32[512]{0:T(512)} %param.5, pred[]{:T(512)S(6)} %ne.67, s32[1,128]{1,0:T(1,128)S(1)} %get-tuple-element.116, s32[1,128]{1,0:T(1,128)S(1)} %get-tuple-element.117, s32[1,128]{1,0:T(1,128)S(1)} %get-tuple-element.118, s32[1,128]{1,0:T(1,128)S(1)} %get-tuple-element.115), kind=kLoop, calls=%fused_computation.33 | loop fusion | flops 2048 | bytes 6145 | tf_op jit(solution)/shard_map/jit(_where)/select_n | solution.py:241
  10.9 1.0 %copy-done = f32[128,1024]{1,0:T(8,128)S(1)} copy-done((f32[128,1024]{1,0:T(8,128)S(1)}, f32[128,1024]{1,0:T(8,128)}, u32[]{:S(2)}) %copy-start) | copy-done | bytes 524312
  11.9 0.9 %copy-done.1 = f32[64,1024]{1,0:T(8,128)S(1)} copy-done((f32[64,1024]{1,0:T(8,128)S(1)}, f32[64,1024]{1,0:T(8,128)}, u32[]{:S(2)}) %copy-start.1) | copy-done | bytes 262168
  13.1 0.7 %fusion.7 = s32[512]{0:T(512)S(1)} fusion(s32[512]{0:T(512)} %param.5, s32[2,128]{1,0:T(2,128)S(1)} %get-tuple-element.114, s32[2,128]{1,0:T(2,128)S(1)} %get-tuple-element.113, s32[]{:T(128)S(6)} %axis_index.25, s32[]{:T(128)S(6)} %axis_index.22, pred[]{:T(512)S(6)} %ne.67, pred[]{:T(512)S(6)} %ne.66, s32[1,128]{1,0:T(1,128)S(1)} %get-tuple-element.116, ...), kind=kLoop, calls=%fused_computation.23 | loop fusion | flops 38912 | bytes 8202 | tf_op jit(solution)/shard_map/jit(_where)/select_n | solution.py:254
  13.8 3.3 %collective-permute-done.8.refs_6_ = f32[64,1024]{1,0:T(8,128)S(1)} collective-permute-done((f32[64,1024]{1,0:T(8,128)}, f32[64,1024]{1,0:T(8,128)S(1)}, u32[]{:S(2)}, u32[]{:S(2)}) %collective-permute-start.8) | collective-permute-done | bytes 262176 | tf_op jit(solution)/shard_map/ppermute | solution.py:233
  17.7 1.5 %collective-permute-start.6 = (f32[64,1024]{1,0:T(8,128)S(1)}, f32[64,1024]{1,0:T(8,128)S(1)}, u32[]{:S(2)}, u32[]{:S(2)}) collective-permute-start(f32[64,1024]{1,0:T(8,128)S(1)} %collective-permute-done.5.refs_7_), channel_id=1, source_target_pairs={{0,8},{1,9},{2,10},{3,11},{4,12},{5,13},{6,14},{7,15},{8,0},{9,1},... | collective-permute-start | bytes 786440 | tf_op jit(solution)/shard_map/ppermute | solution.py:233
  19.7 1.6 %collective-permute-start.2 = (f32[64,1024]{1,0:T(8,128)S(1)}, f32[64,1024]{1,0:T(8,128)S(1)}, u32[]{:S(2)}, u32[]{:S(2)}) collective-permute-start(f32[64,1024]{1,0:T(8,128)S(1)} %slice.84), channel_id=1, source_target_pairs={{0,2},{1,3},{2,0},{3,1},{4,6},{5,7},{6,4},{7,5},{8,10},{9,11},{10,... | collective-permute-start | bytes 786440 | tf_op jit(solution)/shard_map/ppermute | solution.py:233
  21.3 1.6 %collective-permute-start.4 = (f32[64,1024]{1,0:T(8,128)S(1)}, f32[64,1024]{1,0:T(8,128)S(1)}, u32[]{:S(2)}, u32[]{:S(2)}) collective-permute-start(f32[64,1024]{1,0:T(8,128)S(1)} %slice.85), channel_id=1, source_target_pairs={{0,1},{1,0},{2,3},{3,2},{4,5},{5,4},{6,7},{7,6},{8,9},{9,8},{10,11... | collective-permute-start | bytes 786440 | tf_op jit(solution)/shard_map/ppermute | solution.py:233
  22.8 3.1 %collective-permute-done.6.z3 = f32[64,1024]{1,0:T(8,128)S(1)} collective-permute-done((f32[64,1024]{1,0:T(8,128)S(1)}, f32[64,1024]{1,0:T(8,128)S(1)}, u32[]{:S(2)}, u32[]{:S(2)}) %collective-permute-start.6) | collective-permute-done | bytes 262176 | tf_op jit(solution)/shard_map/ppermute | solution.py:233
  25.9 2.3 %shard_map.59 = (f32[384,384]{1,0:T(8,128)S(1)}, f32[8,384]{1,0:T(8,128)S(1)}, bf16[384,1024]{1,0:T(8,128)(2,1)S(1)}, bf16[384,1024]{1,0:T(8,128)(2,1)S(1)}, bf1...) custom-call(bf16[128,1024]{1,0:T(8,128)(2,1)S(1)} %get-tuple-element.57.refs_0_, ...), custom_call_target="tpu_custom_call" | custom-call | flops 1509949440 | bytes 8388608 | tf_op jit(solution)/shard_map/pallas_call | solution.py:19
  28.2 1.1 %collective-permute-done.4.db = f32[64,1024]{1,0:T(8,128)S(1)} collective-permute-done((f32[64,1024]{1,0:T(8,128)S(1)}, f32[64,1024]{1,0:T(8,128)S(1)}, u32[]{:S(2)}, u32[]{:S(2)}) %collective-permute-start.4) | collective-permute-done | bytes 262176 | tf_op jit(solution)/shard_map/ppermute | solution.py:233
  29.3 1.4 %shard_map.60 = (f32[128,384]{1,0:T(8,128)S(1)}, f32[512,128]{1,0:T(8,128)S(1)}, f32[8,512]{1,0:T(8,128)S(1)}, bf16[128,1024]{1,0:T(8,128)(2,1)S(1)}, bf16[128,1...) custom-call(f32[64,1024]{1,0:T(8,128)S(1)} %collective-permute-done.2.da, ...), custom_call_target="tpu_custom_call" | custom-call | flops 100663296 | bytes 8388608 | tf_op jit(solution)/shard_map/pallas_call | solution.py:19
  30.7 1.5 %collective-permute-start.13 = (f32[8,512]{1,0:T(8,128)S(1)}, f32[8,512]{1,0:T(8,128)S(1)}, u32[]{:S(2)}, u32[]{:S(2)}) collective-permute-start(f32[8,512]{1,0:T(8,128)S(1)} %get-tuple-element.69.refs_0_), channel_id=1, source_target_pairs={{0,3},{1,2},{2,1},{3,0},{4,7},{5,6},{6,5},{7,4},{8,11},{9,10},{10,... | collective-permute-start | bytes 49160 | tf_op jit(solution)/shard_map/ppermute | solution.py:233
  32.2 1.5 %collective-permute-start.12 = (f32[8,512]{1,0:T(8,128)S(1)}, f32[8,512]{1,0:T(8,128)S(1)}, u32[]{:S(2)}, u32[]{:S(2)}) collective-permute-start(f32[8,512]{1,0:T(8,128)S(1)} %get-tuple-element.69.refs_0_), channel_id=1, source_target_pairs={{0,2},{1,3},{2,0},{3,1},{4,6},{5,7},{6,4},{7,5},{8,10},{9,11},{10,... | collective-permute-start | bytes 49160 | tf_op jit(solution)/shard_map/ppermute | solution.py:233
  34.3 2.5 %shard_map.61 = (f32[512,512]{1,0:T(8,128)S(1)}, bf16[512,1024]{1,0:T(8,128)(2,1)S(1)}, bf16[512,1024]{1,0:T(8,128)(2,1)S(1)}, f32[512,1024]{1,0:T(8,128)S(1)}, f32[512,1024]{1,0:T(8,128)S(1)}) custom-call(f32[384,384]{1,0:T(8,128)S(1)} %get-tuple-element.70.et1, f32[128,384]{1,0:T(8,128)S(1)} %get-tuple-element.71.et_p, ...), custom_call_target="tpu_custom_call" | custom-call | flops 2147483648 | bytes 8388608 | tf_op jit(solution)/shard_map/pallas_call | solution.py:19
  36.8 0.6 collective-permute-done.11.refs_1_
  37.5 1.0 %shard_map.62 = f32[256,1024]{1,0:T(8,128)S(1)} custom-call(f32[8,512]{1,0:T(8,128)S(1)} %get-tuple-element.69.refs_0_, f32[8,512]{1,0:T(8,128)S(1)} %collective-permute-done.11.refs_1_, f32[8,512]{1,0:T(8,128)S(1)} %collective-permute-done.12.refs_2_, f32[8,512]{1,0:T(8,128)S(1)} %collective-permute-done.13.refs_3_, ...), custom_call_target="tpu_custom_call" | custom-call | flops 805306368 | bytes 8388608 | tf_op jit(solution)/shard_map/pallas_call | solution.py:19
  38.5 1.0 %shard_map.63 = (f32[192,1024]{1,0:T(8,128)S(1)}, f32[64,1024]{1,0:T(8,128)S(1)}) custom-call(f32[8,512]{1,0:T(8,128)S(1)} %get-tuple-element.69.refs_0_, f32[8,512]{1,0:T(8,128)S(1)} %collective-permute-done.11.refs_1_, f32[8,512]{1,0:T(8,128)S(1)} %collective-permute-done.12.refs_2_, f32[8,512]{1,0:T(8,128)S(1)} %collective-permute-done.13.refs_3_, ...), custom_call_target="tpu_custom_call" | custom-call | flops 805306368 | bytes 8388608 | tf_op jit(solution)/shard_map/pallas_call | solution.py:19
  40.1 0.9 %collective-permute-start.14 = (f32[96,1024]{1,0:T(8,128)S(1)}, f32[96,1024]{1,0:T(8,128)S(1)}, u32[]{:S(2)}, u32[]{:S(2)}) collective-permute-start(f32[96,1024]{1,0:T(8,128)S(1)} %get-tuple-element.93), channel_id=1, source_target_pairs={{0,1},{1,0},{2,3},{3,2},{4,5},{5,4},{6,7},{7,6},{8,9},{9,8},{10,11... | collective-permute-start | bytes 1179656 | tf_op jit(solution)/shard_map/ppermute | solution.py:233
  41.6 1.5 %collective-permute-start.17 = (f32[64,1024]{1,0:T(8,128)S(1)}, f32[64,1024]{1,0:T(8,128)S(1)}, u32[]{:S(2)}, u32[]{:S(2)}) collective-permute-start(f32[64,1024]{1,0:T(8,128)S(1)} %get-tuple-element.98), channel_id=1, source_target_pairs={{0,8},{1,9},{2,10},{3,11},{4,12},{5,13},{6,14},{7,15},{8,0},{9,1},... | collective-permute-start | bytes 786440 | tf_op jit(solution)/shard_map/ppermute | solution.py:233
  43.1 6.7 %collective-permute-done.17.b = f32[64,1024]{1,0:T(8,128)S(1)} collective-permute-done((f32[64,1024]{1,0:T(8,128)S(1)}, f32[64,1024]{1,0:T(8,128)S(1)}, u32[]{:S(2)}, u32[]{:S(2)}) %collective-permute-start.17) | collective-permute-done | bytes 262176 | tf_op jit(solution)/shard_map/ppermute | solution.py:233
  49.9 1.9 %collective-permute-start.21 = (f32[64,1024]{1,0:T(8,128)S(1)}, f32[64,1024]{1,0:T(8,128)S(1)}, u32[]{:S(2)}, u32[]{:S(2)}) collective-permute-start(f32[64,1024]{1,0:T(8,128)S(1)} %shard_map.66), channel_id=1, source_target_pairs={{0,16},{1,17},{2,18},{3,19},{4,20},{5,21},{6,22},{7,23},{8,24},{9,... | collective-permute-start | bytes 786440 | tf_op jit(solution)/shard_map/ppermute | solution.py:233
  51.7 1.4 %collective-permute-start.20 = (f32[64,1024]{1,0:T(8,128)S(1)}, f32[64,1024]{1,0:T(8,128)S(1)}, u32[]{:S(2)}, u32[]{:S(2)}) collective-permute-start(f32[64,1024]{1,0:T(8,128)S(1)} %get-tuple-element.104), channel_id=1, source_target_pairs={{0,8},{1,9},{2,10},{3,11},{4,12},{5,13},{6,14},{7,15},{8,0},{9,1},... | collective-permute-start | bytes 786440 | tf_op jit(solution)/shard_map/ppermute | solution.py:233
  53.2 1.2 %collective-permute-start.18 = (f32[96,1024]{1,0:T(8,128)S(1)}, f32[96,1024]{1,0:T(8,128)S(1)}, u32[]{:S(2)}, u32[]{:S(2)}) collective-permute-start(f32[96,1024]{1,0:T(8,128)S(1)} %get-tuple-element.101), channel_id=1, source_target_pairs={{0,1},{1,0},{2,3},{3,2},{4,5},{5,4},{6,7},{7,6},{8,9},{9,8},{10,11... | collective-permute-start | bytes 1179656 | tf_op jit(solution)/shard_map/ppermute | solution.py:233
  55.6 6.6 %collective-permute-done.20.r1 = f32[64,1024]{1,0:T(8,128)S(1)} collective-permute-done((f32[64,1024]{1,0:T(8,128)S(1)}, f32[64,1024]{1,0:T(8,128)S(1)}, u32[]{:S(2)}, u32[]{:S(2)}) %collective-permute-start.20) | collective-permute-done | bytes 262176 | tf_op jit(solution)/shard_map/ppermute | solution.py:233
  62.2 1.5 %collective-permute-done.21.r2 = f32[64,1024]{1,0:T(8,128)S(1)} collective-permute-done((f32[64,1024]{1,0:T(8,128)S(1)}, f32[64,1024]{1,0:T(8,128)S(1)}, u32[]{:S(2)}, u32[]{:S(2)}) %collective-permute-start.21) | collective-permute-done | bytes 262176 | tf_op jit(solution)/shard_map/ppermute | solution.py:233
  63.7 1.3 %shard_map.68 = (f32[128,1024]{1,0:T(8,128)}, f32[64,1024]{1,0:T(8,128)}) custom-call(f32[128,1024]{1,0:T(8,128)S(1)} %get-tuple-element.88.qn, f32[128,128]{1,0:T(8,128)S(1)} %get-tuple-element.89.qs, f32[64,1024]{1,0:T(8,128)S(1)} %get-tuple-element.90.pn, f32[64,128]{1,0:T(8,128)S(1)} %get-tuple-element.91.ps, f32[128,1024]{1,0:T(8,128)S(1)} %get-tuple-element.92.own, ...), custom_call_target="tpu_custom_call" | custom-call | flops 1572864 | bytes 8388608 | tf_op jit(solution)/shard_map/pallas_call | solution.py:19
  (37 shorter events, 4.2 us)
Async XLA Ops:
  0.6 17.0 %collective-permute-start.5 = (f32[64,1024]{1,0:T(8,128)}, f32[64,1024]{1,0:T(8,128)S(1)}, u32[]{:S(2)}, u32[]{:S(2)}) collective-permute-start(f32[64,1024]{1,0:T(8,128)} %passages.1), channel_id=1, source_target_pairs={{0,16},{1,17},{2,18},{3,19},{4,20},{5,21},{6,22},{7,23},{8,24},{9,... | collective-permute-start | bytes 786440 | tf_op jit(solution)/shard_map/ppermute | solution.py:233
  4.7 12.4 %collective-permute-start.8 = (f32[64,1024]{1,0:T(8,128)}, f32[64,1024]{1,0:T(8,128)S(1)}, u32[]{:S(2)}, u32[]{:S(2)}) collective-permute-start(f32[64,1024]{1,0:T(8,128)} %passages.1), channel_id=1, source_target_pairs={{0,8},{1,9},{2,10},{3,11},{4,12},{5,13},{6,14},{7,15},{8,0},{9,1},... | collective-permute-start | bytes 786440 | tf_op jit(solution)/shard_map/ppermute | solution.py:233
  6.3 13.3 %collective-permute-start = (f32[128,1024]{1,0:T(8,128)}, f32[128,1024]{1,0:T(8,128)S(1)}, u32[]{:S(2)}, u32[]{:S(2)}) collective-permute-start(f32[128,1024]{1,0:T(8,128)} %queries.1), channel_id=1, source_target_pairs={{0,1},{1,0},{2,3},{3,2},{4,5},{5,4},{6,7},{7,6},{8,9},{9,8},{10,11... | collective-permute-start | bytes 1572872 | tf_op jit(solution)/shard_map/ppermute | solution.py:233
  7.8 13.4 %collective-permute-start.3 = (f32[128,1024]{1,0:T(8,128)}, f32[128,1024]{1,0:T(8,128)S(1)}, u32[]{:S(2)}, u32[]{:S(2)}) collective-permute-start(f32[128,1024]{1,0:T(8,128)} %queries.1), channel_id=1, source_target_pairs={{0,2},{1,3},{2,0},{3,1},{4,6},{5,7},{6,4},{7,5},{8,10},{9,11},{10,... | collective-permute-start | bytes 1572872 | tf_op jit(solution)/shard_map/ppermute | solution.py:233
  10.9 1.0 %copy-start = (f32[128,1024]{1,0:T(8,128)S(1)}, f32[128,1024]{1,0:T(8,128)}, u32[]{:S(2)}) copy-start(f32[128,1024]{1,0:T(8,128)} %queries.1) | copy-start | bytes 1572868
  11.9 0.9 %copy-start.1 = (f32[64,1024]{1,0:T(8,128)S(1)}, f32[64,1024]{1,0:T(8,128)}, u32[]{:S(2)}) copy-start(f32[64,1024]{1,0:T(8,128)} %passages.1) | copy-start | bytes 786436
  17.2 2.0 %collective-permute-start.9 = (f32[64,1024]{1,0:T(8,128)S(1)}, f32[64,1024]{1,0:T(8,128)S(1)}, u32[]{:S(2)}, u32[]{:S(2)}) collective-permute-start(f32[64,1024]{1,0:T(8,128)S(1)} %collective-permute-done.8.refs_6_), channel_id=1, source_target_pairs={{0,4},{1,5},{2,6},{3,7},{4,0},{5,1},{6,2},{7,3},{8,12},{9,13},{10,... | collective-permute-start | bytes 786440 | tf_op jit(solution)/shard_map/ppermute | solution.py:233
  17.2 2.5 %collective-permute-start.1 = (f32[64,1024]{1,0:T(8,128)S(1)}, f32[64,1024]{1,0:T(8,128)S(1)}, u32[]{:S(2)}, u32[]{:S(2)}) collective-permute-start(f32[64,1024]{1,0:T(8,128)S(1)} %copy-done.1), channel_id=1, source_target_pairs={{0,4},{1,5},{2,6},{3,7},{4,0},{5,1},{6,2},{7,3},{8,12},{9,13},{10,... | collective-permute-start | bytes 786440 | tf_op jit(solution)/shard_map/ppermute | solution.py:233
  17.7 8.2 %collective-permute-start.6 = (f32[64,1024]{1,0:T(8,128)S(1)}, f32[64,1024]{1,0:T(8,128)S(1)}, u32[]{:S(2)}, u32[]{:S(2)}) collective-permute-start(f32[64,1024]{1,0:T(8,128)S(1)} %collective-permute-done.5.refs_7_), channel_id=1, source_target_pairs={{0,8},{1,9},{2,10},{3,11},{4,12},{5,13},{6,14},{7,15},{8,0},{9,1},... | collective-permute-start | bytes 786440 | tf_op jit(solution)/shard_map/ppermute | solution.py:233
  19.2 6.7 %collective-permute-start.10 = (f32[64,1024]{1,0:T(8,128)S(1)}, f32[64,1024]{1,0:T(8,128)S(1)}, u32[]{:S(2)}, u32[]{:S(2)}) collective-permute-start(f32[64,1024]{1,0:T(8,128)S(1)} %collective-permute-done.5.refs_7_), channel_id=1, source_target_pairs={{0,4},{1,5},{2,6},{3,7},{4,0},{5,1},{6,2},{7,3},{8,12},{9,13},{10,... | collective-permute-start | bytes 786440 | tf_op jit(solution)/shard_map/ppermute | solution.py:233
  19.7 8.6 %collective-permute-start.2 = (f32[64,1024]{1,0:T(8,128)S(1)}, f32[64,1024]{1,0:T(8,128)S(1)}, u32[]{:S(2)}, u32[]{:S(2)}) collective-permute-start(f32[64,1024]{1,0:T(8,128)S(1)} %slice.84), channel_id=1, source_target_pairs={{0,2},{1,3},{2,0},{3,1},{4,6},{5,7},{6,4},{7,5},{8,10},{9,11},{10,... | collective-permute-start | bytes 786440 | tf_op jit(solution)/shard_map/ppermute | solution.py:233
  21.3 8.1 %collective-permute-start.4 = (f32[64,1024]{1,0:T(8,128)S(1)}, f32[64,1024]{1,0:T(8,128)S(1)}, u32[]{:S(2)}, u32[]{:S(2)}) collective-permute-start(f32[64,1024]{1,0:T(8,128)S(1)} %slice.85), channel_id=1, source_target_pairs={{0,1},{1,0},{2,3},{3,2},{4,5},{5,4},{6,7},{7,6},{8,9},{9,8},{10,11... | collective-permute-start | bytes 786440 | tf_op jit(solution)/shard_map/ppermute | solution.py:233
  25.9 3.4 %collective-permute-start.7 = (f32[64,1024]{1,0:T(8,128)S(1)}, f32[64,1024]{1,0:T(8,128)S(1)}, u32[]{:S(2)}, u32[]{:S(2)}) collective-permute-start(f32[64,1024]{1,0:T(8,128)S(1)} %collective-permute-done.6.z3), channel_id=1, source_target_pairs={{0,4},{1,5},{2,6},{3,7},{4,0},{5,1},{6,2},{7,3},{8,12},{9,13},{10,... | collective-permute-start | bytes 786440 | tf_op jit(solution)/shard_map/ppermute | solution.py:233
  30.7 6.1 %collective-permute-start.13 = (f32[8,512]{1,0:T(8,128)S(1)}, f32[8,512]{1,0:T(8,128)S(1)}, u32[]{:S(2)}, u32[]{:S(2)}) collective-permute-start(f32[8,512]{1,0:T(8,128)S(1)} %get-tuple-element.69.refs_0_), channel_id=1, source_target_pairs={{0,3},{1,2},{2,1},{3,0},{4,7},{5,6},{6,5},{7,4},{8,11},{9,10},{10,... | collective-permute-start | bytes 49160 | tf_op jit(solution)/shard_map/ppermute | solution.py:233
  32.2 4.6 %collective-permute-start.12 = (f32[8,512]{1,0:T(8,128)S(1)}, f32[8,512]{1,0:T(8,128)S(1)}, u32[]{:S(2)}, u32[]{:S(2)}) collective-permute-start(f32[8,512]{1,0:T(8,128)S(1)} %get-tuple-element.69.refs_0_), channel_id=1, source_target_pairs={{0,2},{1,3},{2,0},{3,1},{4,6},{5,7},{6,4},{7,5},{8,10},{9,11},{10,... | collective-permute-start | bytes 49160 | tf_op jit(solution)/shard_map/ppermute | solution.py:233
  33.7 3.7 %collective-permute-start.11 = (f32[8,512]{1,0:T(8,128)S(1)}, f32[8,512]{1,0:T(8,128)S(1)}, u32[]{:S(2)}, u32[]{:S(2)}) collective-permute-start(f32[8,512]{1,0:T(8,128)S(1)} %get-tuple-element.69.refs_0_), channel_id=1, source_target_pairs={{0,1},{1,0},{2,3},{3,2},{4,5},{5,4},{6,7},{7,6},{8,9},{9,8},{10,11... | collective-permute-start | bytes 49160 | tf_op jit(solution)/shard_map/ppermute | solution.py:233
  38.5 3.1 %collective-permute-start.16 = (f32[256,1024]{1,0:T(8,128)S(1)}, f32[256,1024]{1,0:T(8,128)S(1)}, u32[]{:S(2)}, u32[]{:S(2)}) collective-permute-start(f32[256,1024]{1,0:T(8,128)S(1)} %shard_map.62), channel_id=1, source_target_pairs={{0,4},{1,5},{2,6},{3,7},{4,0},{5,1},{6,2},{7,3},{8,12},{9,13},{10,... | collective-permute-start | bytes 3145736 | tf_op jit(solution)/shard_map/ppermute | solution.py:233
  40.1 13.1 %collective-permute-start.14 = (f32[96,1024]{1,0:T(8,128)S(1)}, f32[96,1024]{1,0:T(8,128)S(1)}, u32[]{:S(2)}, u32[]{:S(2)}) collective-permute-start(f32[96,1024]{1,0:T(8,128)S(1)} %get-tuple-element.93), channel_id=1, source_target_pairs={{0,1},{1,0},{2,3},{3,2},{4,5},{5,4},{6,7},{7,6},{8,9},{9,8},{10,11... | collective-permute-start | bytes 1179656 | tf_op jit(solution)/shard_map/ppermute | solution.py:233
  41.0 12.2 %collective-permute-start.15 = (f32[96,1024]{1,0:T(8,128)S(1)}, f32[96,1024]{1,0:T(8,128)S(1)}, u32[]{:S(2)}, u32[]{:S(2)}) collective-permute-start(f32[96,1024]{1,0:T(8,128)S(1)} %get-tuple-element.94), channel_id=1, source_target_pairs={{0,2},{1,3},{2,0},{3,1},{4,6},{5,7},{6,4},{7,5},{8,10},{9,11},{10,... | collective-permute-start | bytes 1179656 | tf_op jit(solution)/shard_map/ppermute | solution.py:233
  41.6 8.2 %collective-permute-start.17 = (f32[64,1024]{1,0:T(8,128)S(1)}, f32[64,1024]{1,0:T(8,128)S(1)}, u32[]{:S(2)}, u32[]{:S(2)}) collective-permute-start(f32[64,1024]{1,0:T(8,128)S(1)} %get-tuple-element.98), channel_id=1, source_target_pairs={{0,8},{1,9},{2,10},{3,11},{4,12},{5,13},{6,14},{7,15},{8,0},{9,1},... | collective-permute-start | bytes 786440 | tf_op jit(solution)/shard_map/ppermute | solution.py:233
  49.9 13.9 %collective-permute-start.21 = (f32[64,1024]{1,0:T(8,128)S(1)}, f32[64,1024]{1,0:T(8,128)S(1)}, u32[]{:S(2)}, u32[]{:S(2)}) collective-permute-start(f32[64,1024]{1,0:T(8,128)S(1)} %shard_map.66), channel_id=1, source_target_pairs={{0,16},{1,17},{2,18},{3,19},{4,20},{5,21},{6,22},{7,23},{8,24},{9,... | collective-permute-start | bytes 786440 | tf_op jit(solution)/shard_map/ppermute | solution.py:233
  51.7 10.5 %collective-permute-start.20 = (f32[64,1024]{1,0:T(8,128)S(1)}, f32[64,1024]{1,0:T(8,128)S(1)}, u32[]{:S(2)}, u32[]{:S(2)}) collective-permute-start(f32[64,1024]{1,0:T(8,128)S(1)} %get-tuple-element.104), channel_id=1, source_target_pairs={{0,8},{1,9},{2,10},{3,11},{4,12},{5,13},{6,14},{7,15},{8,0},{9,1},... | collective-permute-start | bytes 786440 | tf_op jit(solution)/shard_map/ppermute | solution.py:233
  53.2 10.5 %collective-permute-start.18 = (f32[96,1024]{1,0:T(8,128)S(1)}, f32[96,1024]{1,0:T(8,128)S(1)}, u32[]{:S(2)}, u32[]{:S(2)}) collective-permute-start(f32[96,1024]{1,0:T(8,128)S(1)} %get-tuple-element.101), channel_id=1, source_target_pairs={{0,1},{1,0},{2,3},{3,2},{4,5},{5,4},{6,7},{7,6},{8,9},{9,8},{10,11... | collective-permute-start | bytes 1179656 | tf_op jit(solution)/shard_map/ppermute | solution.py:233
  54.5 9.3 %collective-permute-start.19 = (f32[96,1024]{1,0:T(8,128)S(1)}, f32[96,1024]{1,0:T(8,128)S(1)}, u32[]{:S(2)}, u32[]{:S(2)}) collective-permute-start(f32[96,1024]{1,0:T(8,128)S(1)} %get-tuple-element.102), channel_id=1, source_target_pairs={{0,2},{1,3},{2,0},{3,1},{4,6},{5,7},{6,4},{7,5},{8,10},{9,11},{10,... | collective-permute-start | bytes 1179656 | tf_op jit(solution)/shard_map/ppermute | solution.py:233
